TPU v7x, 32 devices: a whole 2x2x4 slice. The times are simulated.
32 devices in a mesh: section: 2 (over x), ctx: 4 (over z), fsdp: 4 (over y, core).
Axes of the slice: x: 2, y: 2, z: 4, core: 2. Of those that a mesh axis runs over, the one named last changes fastest.
Arguments:
- inputs: bfloat16 [4, 2, 1536, 576], P('fsdp', None, 'ctx'), may hold values from -6 to 6
- lengths: int32 [4, 2, 4], P('fsdp'), may hold values from 1 to 1344, 1536 in all within a row
- cotangent: bfloat16 [4, 2, 1536, 576], P('fsdp', None, 'ctx'), may hold values from -6 to 6
- w_query: bfloat16 [2, 576, 576], P('section', ('ctx', 'fsdp')), may hold values from -0.25 to 0.25
- w_key: bfloat16 [2, 576, 192], P('section', ('ctx', 'fsdp')), may hold values from -0.25 to 0.25
- w_value: bfloat16 [2, 576, 192], P('section', ('ctx', 'fsdp')), may hold values from -0.25 to 0.25
- w_out: bfloat16 [2, 576, 576], P('section', ('ctx', 'fsdp')), may hold values from -2.5 to 2.5
- w_gate: bfloat16 [2, 576, 1536], P('section', ('ctx', 'fsdp')), may hold values from -0.25 to 0.25
- w_up: bfloat16 [2, 576, 1536], P('section', ('ctx', 'fsdp')), may hold values from -0.25 to 0.25
- w_down: bfloat16 [2, 1536, 576], P('section', ('ctx', 'fsdp')), may hold values from -0.15625 to 0.15625
- g_attn: bfloat16 [2, 576], P('section', ('ctx', 'fsdp')), may hold values from 0.5 to 1.5
- g_mlp: bfloat16 [2, 576], P('section', ('ctx', 'fsdp')), may hold values from 0.5 to 1.5
Outputs:
- edges: float32 [2, 4, 2, 1536, 576], P('section', 'fsdp', None, 'ctx')
- grad_query: float32 [2, 576, 576], P('section', ('ctx', 'fsdp'))
- grad_key: float32 [2, 576, 192], P('section', ('ctx', 'fsdp'))
- grad_value: float32 [2, 576, 192], P('section', ('ctx', 'fsdp'))
- grad_out: float32 [2, 576, 576], P('section', ('ctx', 'fsdp'))
- grad_gate: float32 [2, 576, 1536], P('section', ('ctx', 'fsdp'))
- grad_up: float32 [2, 576, 1536], P('section', ('ctx', 'fsdp'))
- grad_down: float32 [2, 1536, 576], P('section', ('ctx', 'fsdp'))
- grad_attn_gain: float32 [2, 576], P('section', ('ctx', 'fsdp'))
- grad_mlp_gain: float32 [2, 576], P('section', ('ctx', 'fsdp'))
Inputs may be any that keep to these rules, and one draw needn't show every extreme that they name: Each row of 4 lengths sums to 1536; the largest in each row is exactly 1344.
All inputs are finite; a program needn't handle non-finite values.
Results may differ from a plain program's by a relative error of at most 0.035.
Values may be sent and summed in bfloat16 or wider, within the bound.
No kernel may reach another device: no remote copies, remote signals or barrier semaphores. Data moves between devices by JAX's collectives and lax.ppermute only.
A program may use at most 128 MiB of HBM per device.

v0:
```python
import jax
import jax.numpy as jnp
from jax import lax
from jax.sharding import PartitionSpec as P

D = 576
HQ = 9
KV = 3
HD = 64


EPSILON = 1e-05
THETA = 10000.0


def passed_along(value, axis, steps):
    count = lax.axis_size(axis)
    leading, last = (max(0, -steps), min(count, count - steps))
    return lax.ppermute(value, axis, [(source, source + steps) for source in range(leading, last)])


def doc_layout(lengths, positions):
    doc_ends = jnp.cumsum(lengths)
    passed = (positions[:, None] >= doc_ends[None, :]).astype(lengths.dtype)
    starts = jnp.sum(passed * lengths[None, :], axis=1)
    return (starts, positions - starts)


def rotate_half(values):
    middle = values.shape[-1] // 2
    return jnp.concatenate([-values[..., middle:], values[..., :middle]], axis=-1)


def rotate_back(values):
    middle = values.shape[-1] // 2
    return jnp.concatenate([values[..., middle:], -values[..., :middle]], axis=-1)


def angle_tables(offsets, head_width):
    middle = head_width // 2
    frequency = THETA ** (-jnp.arange(middle, dtype=jnp.float32) * 2.0 / head_width)
    angles = offsets.astype(jnp.float32)[:, None] * frequency[None, :]
    cosine = jnp.concatenate([jnp.cos(angles), jnp.cos(angles)], axis=-1)[:, None, :]
    sine_table = jnp.concatenate([jnp.sin(angles), jnp.sin(angles)], axis=-1)[:, None, :]
    return (cosine, sine_table)


def norm_back(d_normed, source, inverse, gain):
    scaled = source * inverse
    gain_grad = jnp.sum(d_normed * scaled, axis=0)
    d_scaled = d_normed * gain
    d_source = inverse * (d_scaled - scaled * jnp.mean(d_scaled * scaled, axis=-1, keepdims=True))
    return (d_source, gain_grad)


def layer_forward(layer_input, weights, lengths, offset_base):
    w_query, w_key, w_value, w_out, w_gate, w_up, w_down, g_attn, g_mlp = weights
    local_rows = layer_input.shape[0]
    group = HQ // KV
    scale = HD ** (-0.5)
    positions = offset_base + jnp.arange(local_rows, dtype=jnp.int32)
    last_query = positions[local_rows - 1]
    starts, offsets = doc_layout(lengths, positions)
    cosine, sine_table = angle_tables(offsets, HD)
    inverse = lax.rsqrt(jnp.mean(layer_input * layer_input, axis=-1, keepdims=True) + EPSILON)
    normed = (layer_input * inverse * g_attn.astype(jnp.float32)).astype(jnp.bfloat16)
    queries = jnp.dot(normed, w_query, preferred_element_type=jnp.float32).reshape(
        local_rows, HQ, HD
    )
    queries = (queries * cosine + rotate_half(queries) * sine_table).astype(jnp.bfloat16)
    keys_turned = jnp.dot(normed, w_key, preferred_element_type=jnp.float32).reshape(
        local_rows, KV, HD
    )
    keys_turned = (keys_turned * cosine + rotate_half(keys_turned) * sine_table).astype(
        jnp.bfloat16
    )
    values_local = jnp.dot(normed, w_value, preferred_element_type=jnp.float32).astype(jnp.bfloat16)
    pairs = jnp.concatenate([keys_turned.reshape(local_rows, KV * HD), values_local], axis=1)
    grouped = queries.reshape(local_rows, KV, group, HD)
    initial = (
        jnp.full((KV, group, local_rows), -1e30, jnp.float32),
        jnp.zeros((KV, group, local_rows), jnp.float32),
        jnp.zeros((KV, group, local_rows, HD), jnp.float32),
    )
    fold_carry = initial
    received = lax.all_gather(pairs, "ctx", axis=0, tiled=True)
    blocks = received.shape[0] // local_rows
    pieces = received.reshape(blocks, local_rows, 2, KV, HD)

    def visit_block_step(fold_state, scan_item):
        key_block, block_index = scan_item
        first_key = block_index * local_rows

        def visit_block_work(state):
            running, totals, weighted = state
            key_pos = first_key + jnp.arange(local_rows, dtype=jnp.int32)
            allowed = (key_pos[None, :] <= positions[:, None]) & (
                key_pos[None, :] >= starts[:, None]
            )
            scores = (
                jnp.einsum(
                    "qkgd,nkd->kgqn", grouped, key_block[:, 0], preferred_element_type=jnp.float32
                )
                * scale
            )
            scores = jnp.where(allowed, scores, -1e30)
            new_peak = jnp.maximum(running, jnp.max(scores, axis=-1))
            block_weights = jnp.where(allowed, jnp.exp(scores - new_peak[..., None]), 0.0)
            fading = jnp.exp(running - new_peak)
            totals = totals * fading + jnp.sum(block_weights, axis=-1)
            weighted = weighted * fading[..., None] + jnp.einsum(
                "kgqn,nkd->kgqd",
                block_weights.astype(jnp.bfloat16),
                key_block[:, 1],
                preferred_element_type=jnp.float32,
            )
            return (new_peak, totals, weighted)

        def visit_block_skip(state):
            return state

        return (
            lax.cond(first_key <= last_query, visit_block_work, visit_block_skip, fold_state),
            None,
        )

    fold_carry, _ = lax.scan(
        visit_block_step, fold_carry, (pieces, jnp.arange(blocks, dtype=jnp.int32))
    )
    running, totals, weighted = fold_carry
    attended = weighted / totals[..., None]
    log_total = running + jnp.log(totals)
    attended_low = (
        jnp.transpose(attended, (2, 0, 1, 3)).reshape(local_rows, HQ * HD).astype(jnp.bfloat16)
    )
    middle_state = layer_input + jnp.dot(attended_low, w_out, preferred_element_type=jnp.float32)
    inverse_mlp = lax.rsqrt(jnp.mean(middle_state * middle_state, axis=-1, keepdims=True) + EPSILON)
    normed_mlp = (middle_state * inverse_mlp * g_mlp.astype(jnp.float32)).astype(jnp.bfloat16)
    gate_value = jnp.dot(normed_mlp, w_gate, preferred_element_type=jnp.float32)
    up_value = jnp.dot(normed_mlp, w_up, preferred_element_type=jnp.float32)
    hidden = (jax.nn.silu(gate_value) * up_value).astype(jnp.bfloat16)
    result = middle_state + jnp.dot(hidden, w_down, preferred_element_type=jnp.float32)
    saved = (
        layer_input,
        inverse,
        normed,
        grouped,
        pairs,
        positions,
        starts,
        cosine,
        sine_table,
        attended,
        attended_low,
        log_total,
        middle_state,
        inverse_mlp,
        normed_mlp,
        gate_value,
        up_value,
        hidden,
    )
    return (result, saved)


def layer_backward(d_result, saved, weights):
    w_query, w_key, w_value, w_out, w_gate, w_up, w_down, g_attn, g_mlp = weights
    (
        layer_input,
        inverse,
        normed,
        grouped,
        pairs,
        positions,
        starts,
        cosine,
        sine_table,
        attended,
        attended_low,
        log_total,
        middle_state,
        inverse_mlp,
        normed_mlp,
        gate_value,
        up_value,
        hidden,
    ) = saved
    local_rows = layer_input.shape[0]
    group = HQ // KV
    scale = HD ** (-0.5)
    last_query = positions[local_rows - 1]
    mlp_grad = d_result.astype(jnp.bfloat16)
    down_grad = jnp.einsum("rf,rd->fd", hidden, mlp_grad, preferred_element_type=jnp.float32)
    d_hidden = jnp.einsum("rd,fd->rf", mlp_grad, w_down, preferred_element_type=jnp.float32)
    sigmoid = jax.nn.sigmoid(gate_value)
    d_gate = (d_hidden * up_value * sigmoid * (1.0 + gate_value * (1.0 - sigmoid))).astype(
        jnp.bfloat16
    )
    d_up = (d_hidden * gate_value * sigmoid).astype(jnp.bfloat16)
    gate_grad = jnp.einsum("rd,rf->df", normed_mlp, d_gate, preferred_element_type=jnp.float32)
    up_grad = jnp.einsum("rd,rf->df", normed_mlp, d_up, preferred_element_type=jnp.float32)
    d_normed_mlp = jnp.einsum(
        "rf,df->rd", d_gate, w_gate, preferred_element_type=jnp.float32
    ) + jnp.einsum("rf,df->rd", d_up, w_up, preferred_element_type=jnp.float32)
    d_mlp_in, mlp_gain_grad = norm_back(
        d_normed_mlp, middle_state, inverse_mlp, g_mlp.astype(jnp.float32)
    )
    d_middle = d_result + d_mlp_in
    attn_grad = d_middle.astype(jnp.bfloat16)
    out_grad = jnp.einsum("ra,rd->ad", attended_low, attn_grad, preferred_element_type=jnp.float32)
    d_attended = jnp.einsum(
        "rd,ad->ra", attn_grad, w_out, preferred_element_type=jnp.float32
    ).astype(jnp.bfloat16)
    d_heads = jnp.transpose(d_attended.reshape(local_rows, KV, group, HD), (1, 2, 0, 3))
    deltas = jnp.sum(d_heads.astype(jnp.float32) * attended, axis=-1)
    received = lax.all_gather(pairs, "ctx", axis=0, tiled=True)
    query_grad = jnp.zeros((KV, group, local_rows, HD), jnp.float32)
    blocks = received.shape[0] // local_rows
    pieces = received.reshape(blocks, local_rows, 2, KV, HD)

    def revisit_block_step(query_acc, scan_item):
        key_block, block_index = scan_item
        first_key = block_index * local_rows

        def revisit_block_work(query_state):
            key_pos = first_key + jnp.arange(local_rows, dtype=jnp.int32)
            allowed = (key_pos[None, :] <= positions[:, None]) & (
                key_pos[None, :] >= starts[:, None]
            )
            scores = (
                jnp.einsum(
                    "qkgd,nkd->kgqn", grouped, key_block[:, 0], preferred_element_type=jnp.float32
                )
                * scale
            )
            probabilities = jnp.where(allowed, jnp.exp(scores - log_total[..., None]), 0.0)
            value_grad = jnp.einsum(
                "kgqn,kgqd->nkd",
                probabilities.astype(jnp.bfloat16),
                d_heads,
                preferred_element_type=jnp.float32,
            )
            d_probs = jnp.einsum(
                "kgqd,nkd->kgqn", d_heads, key_block[:, 1], preferred_element_type=jnp.float32
            )
            d_scores = (probabilities * (d_probs - deltas[..., None])).astype(jnp.bfloat16)
            query_state = (
                query_state
                + jnp.einsum(
                    "kgqn,nkd->kgqd", d_scores, key_block[:, 0], preferred_element_type=jnp.float32
                )
                * scale
            )
            key_grad = (
                jnp.einsum("kgqn,qkgd->nkd", d_scores, grouped, preferred_element_type=jnp.float32)
                * scale
            )
            joined = jnp.concatenate(
                [key_grad.reshape(local_rows, KV * HD), value_grad.reshape(local_rows, KV * HD)],
                axis=1,
            )
            return (query_state, joined)

        def revisit_block_skip(query_state):
            return (query_state, jnp.zeros((local_rows, 2 * KV * HD), jnp.float32))

        return lax.cond(first_key <= last_query, revisit_block_work, revisit_block_skip, query_acc)

    query_grad, block_grads = lax.scan(
        revisit_block_step, query_grad, (pieces, jnp.arange(blocks, dtype=jnp.int32))
    )
    pair_grads = block_grads.reshape(received.shape[0], 2 * KV * HD)
    query_grad, pair_grads = (query_grad, pair_grads)
    own_pairs = lax.psum_scatter(
        pair_grads.astype(jnp.bfloat16), "ctx", scatter_dimension=0, tiled=True
    ).astype(jnp.float32)
    key_grads = own_pairs[:, : KV * HD].reshape(local_rows, KV, HD)
    key_grads = (
        (key_grads * cosine + rotate_back(key_grads * sine_table))
        .astype(jnp.bfloat16)
        .reshape(local_rows, KV * HD)
    )
    value_grads = own_pairs[:, KV * HD :].astype(jnp.bfloat16)
    query_turned = jnp.transpose(query_grad, (2, 0, 1, 3)).reshape(local_rows, HQ, HD)
    query_grads = (
        (query_turned * cosine + rotate_back(query_turned * sine_table))
        .astype(jnp.bfloat16)
        .reshape(local_rows, HQ * HD)
    )
    query_wgrad = jnp.einsum("rd,ra->da", normed, query_grads, preferred_element_type=jnp.float32)
    key_wgrad = jnp.einsum("rd,ra->da", normed, key_grads, preferred_element_type=jnp.float32)
    value_wgrad = jnp.einsum("rd,ra->da", normed, value_grads, preferred_element_type=jnp.float32)
    d_normed = jnp.einsum("ra,da->rd", query_grads, w_query, preferred_element_type=jnp.float32)
    d_normed = d_normed + jnp.einsum(
        "ra,da->rd", key_grads, w_key, preferred_element_type=jnp.float32
    )
    d_normed = d_normed + jnp.einsum(
        "ra,da->rd", value_grads, w_value, preferred_element_type=jnp.float32
    )
    d_attn_in, attn_gain_grad = norm_back(
        d_normed, layer_input, inverse, g_attn.astype(jnp.float32)
    )
    d_input = d_middle + d_attn_in
    return (
        d_input,
        (
            query_wgrad,
            key_wgrad,
            value_wgrad,
            out_grad,
            gate_grad,
            up_grad,
            down_grad,
            attn_gain_grad,
            mlp_gain_grad,
        ),
    )


def shards(
    inputs, lengths, cotangent, w_query, w_key, w_value, w_out, w_gate, w_up, w_down, g_attn, g_mlp
):
    micro = inputs.shape[1]
    local_rows = inputs.shape[2]
    leading = lax.axis_index("section") == 0
    offset_base = lax.axis_index("ctx") * local_rows
    gathered = (
        lax.all_gather(w_query, ("ctx", "fsdp"), axis=1, tiled=True),
        lax.all_gather(w_key, ("ctx", "fsdp"), axis=1, tiled=True),
        lax.all_gather(w_value, ("ctx", "fsdp"), axis=1, tiled=True),
        lax.all_gather(w_out, ("ctx", "fsdp"), axis=1, tiled=True),
        lax.all_gather(w_gate, ("ctx", "fsdp"), axis=1, tiled=True),
        lax.all_gather(w_up, ("ctx", "fsdp"), axis=1, tiled=True),
        lax.all_gather(w_down, ("ctx", "fsdp"), axis=1, tiled=True),
        lax.all_gather(g_attn, ("ctx", "fsdp"), axis=1, tiled=True),
        lax.all_gather(g_mlp, ("ctx", "fsdp"), axis=1, tiled=True),
    )
    weights = tuple((member[0] for member in gathered))
    silent = jnp.zeros((local_rows, D), jnp.bfloat16)
    incoming = silent
    kept_list = []
    results = []
    for moment in range(micro + 1):
        if moment < micro:
            own_input = inputs[0, moment]
        else:
            own_input = silent
        layer_input = jnp.where(leading, own_input, incoming).astype(jnp.float32)
        doc_lengths = jnp.where(
            leading, lengths[0, min(moment, micro - 1)], lengths[0, max(moment - 1, 0)]
        )
        result, saved = layer_forward(layer_input, weights, doc_lengths, offset_base)
        kept_list.append(saved)
        results.append(result)
        if moment < micro:
            incoming = passed_along(result.astype(jnp.bfloat16), "section", 1)
    regathered = (
        lax.all_gather(w_query, ("ctx", "fsdp"), axis=1, tiled=True),
        lax.all_gather(w_key, ("ctx", "fsdp"), axis=1, tiled=True),
        lax.all_gather(w_value, ("ctx", "fsdp"), axis=1, tiled=True),
        lax.all_gather(w_out, ("ctx", "fsdp"), axis=1, tiled=True),
        lax.all_gather(w_gate, ("ctx", "fsdp"), axis=1, tiled=True),
        lax.all_gather(w_up, ("ctx", "fsdp"), axis=1, tiled=True),
        lax.all_gather(w_down, ("ctx", "fsdp"), axis=1, tiled=True),
        lax.all_gather(g_attn, ("ctx", "fsdp"), axis=1, tiled=True),
        lax.all_gather(g_mlp, ("ctx", "fsdp"), axis=1, tiled=True),
    )
    weights = tuple((member[0] for member in regathered))
    arriving = jnp.zeros((local_rows, D), jnp.float32)
    input_grads = []
    shares = None
    for moment in range(micro + 1):
        if moment < micro:
            own_grad = cotangent[0, micro - 1 - moment].astype(jnp.float32)
        else:
            own_grad = jnp.zeros((local_rows, D), jnp.float32)
        d_result = jnp.where(leading, arriving, own_grad)
        d_input, layer_grads = layer_backward(d_result, kept_list[micro - moment], weights)
        input_grads.append(d_input)
        if moment < micro:
            arriving = passed_along(d_input.astype(jnp.bfloat16), "section", -1).astype(jnp.float32)
        tick_shares = (
            lax.psum_scatter(layer_grads[0], ("ctx", "fsdp"), scatter_dimension=0, tiled=True),
            lax.psum_scatter(layer_grads[1], ("ctx", "fsdp"), scatter_dimension=0, tiled=True),
            lax.psum_scatter(layer_grads[2], ("ctx", "fsdp"), scatter_dimension=0, tiled=True),
            lax.psum_scatter(layer_grads[3], ("ctx", "fsdp"), scatter_dimension=0, tiled=True),
            lax.psum_scatter(layer_grads[4], ("ctx", "fsdp"), scatter_dimension=0, tiled=True),
            lax.psum_scatter(layer_grads[5], ("ctx", "fsdp"), scatter_dimension=0, tiled=True),
            lax.psum_scatter(layer_grads[6], ("ctx", "fsdp"), scatter_dimension=0, tiled=True),
            lax.psum_scatter(layer_grads[7], ("ctx", "fsdp"), scatter_dimension=0, tiled=True),
            lax.psum_scatter(layer_grads[8], ("ctx", "fsdp"), scatter_dimension=0, tiled=True),
        )
        if shares is None:
            shares = tick_shares
        else:
            shares = tuple((earlier + later for earlier, later in zip(shares, tick_shares)))
    edge_rows = [
        jnp.where(leading, input_grads[micro - number], results[number + 1])
        for number in range(micro)
    ]
    edges = jnp.stack(edge_rows)[None, None]
    return (
        edges,
        shares[0][None],
        shares[1][None],
        shares[2][None],
        shares[3][None],
        shares[4][None],
        shares[5][None],
        shares[6][None],
        shares[7][None],
        shares[8][None],
    )


def solution(mesh):
    return jax.shard_map(
        shards,
        mesh=mesh,
        in_specs=(
            P("fsdp", None, "ctx", None),
            P("fsdp", None, None),
            P("fsdp", None, "ctx", None),
            P("section", ("ctx", "fsdp"), None),
            P("section", ("ctx", "fsdp"), None),
            P("section", ("ctx", "fsdp"), None),
            P("section", ("ctx", "fsdp"), None),
            P("section", ("ctx", "fsdp"), None),
            P("section", ("ctx", "fsdp"), None),
            P("section", ("ctx", "fsdp"), None),
            P("section", ("ctx", "fsdp")),
            P("section", ("ctx", "fsdp")),
        ),
        out_specs=(
            P("section", "fsdp", None, "ctx", None),
            P("section", ("ctx", "fsdp"), None),
            P("section", ("ctx", "fsdp"), None),
            P("section", ("ctx", "fsdp"), None),
            P("section", ("ctx", "fsdp"), None),
            P("section", ("ctx", "fsdp"), None),
            P("section", ("ctx", "fsdp"), None),
            P("section", ("ctx", "fsdp"), None),
            P("section", ("ctx", "fsdp")),
            P("section", ("ctx", "fsdp")),
        ),
        check_vma=False,
    )
```

profile of v0, /device:TPU:9, one launch (start us, length us, event | category | flops | bytes accessed | tf_op | source)
XLA Modules:
  0.0 1015.0 jit_solution(15168197724802254297)
XLA Ops:
  16.5 22.4 %all-reduce.17 = (bf16[576]{0:T(1024)(128)(2,1)S(1)}, bf16[576]{0:T(1024)(128)(2,1)S(1)}) all-reduce(bf16[576]{0:T(1024)(128)(2,1)S(1)} %dynamic-update-slice, bf16[576]{0:T(1024)(128)(2,1)S(1)} %dynamic-update-slice.1), channel_id=1, replica_groups=mesh['section'=2,'ctx'=4,'fsdp'=4] {'ctx','fsdp'}, use_global_device_ids=true, to_apply=%add | all-reduce | flops 1152 | bytes 4608
  39.6 27.8 %all_gather.49 = bf16[1,576,192]{2,0,1:T(2,128)(2,1)S(1)} all-gather(bf16[1,36,192]{2,0,1:T(2,128)(2,1)S(1)} %copy.187), channel_id=1, replica_groups=mesh['section'=2,'ctx'=4,'fsdp'=4] {'ctx','fsdp'}, dimensions={1}, use_global_device_ids=true | all-gather | bytes 235008 | tf_op jit(solution)/shard_map/all_gather | solution.py:329
  68.8 21.1 %all_gather.50 = bf16[1,576,192]{2,0,1:T(2,128)(2,1)S(1)} all-gather(bf16[1,36,192]{2,0,1:T(2,128)(2,1)S(1)} %copy.189), channel_id=1, replica_groups=mesh['section'=2,'ctx'=4,'fsdp'=4] {'ctx','fsdp'}, dimensions={1}, use_global_device_ids=true | all-gather | bytes 235008 | tf_op jit(solution)/shard_map/all_gather | solution.py:330
  95.2 32.4 %all_gather.52 = bf16[1,576,576]{2,0,1:T(2,128)(2,1)S(1)} all-gather(bf16[1,36,576]{2,0,1:T(2,128)(2,1)S(1)} %copy.191), channel_id=1, replica_groups=mesh['section'=2,'ctx'=4,'fsdp'=4] {'ctx','fsdp'}, dimensions={1}, use_global_device_ids=true | all-gather | bytes 705024 | tf_op jit(solution)/shard_map/all_gather | solution.py:328
  129.9 27.7 %all_gather.53 = bf16[1,576,576]{2,0,1:T(2,128)(2,1)S(1)} all-gather(bf16[1,36,576]{2,0,1:T(2,128)(2,1)S(1)} %copy.194), channel_id=1, replica_groups=mesh['section'=2,'ctx'=4,'fsdp'=4] {'ctx','fsdp'}, dimensions={1}, use_global_device_ids=true | all-gather | bytes 705024 | tf_op jit(solution)/shard_map/all_gather | solution.py:331
  162.2 16.0 %while.93 = (s32[]{:T(128)}, f32[3,3,384]{2,1,0:T(4,128)S(1)}, f32[3,3,384]{2,1,0:T(4,128)S(1)}, f32[3,3,384,64]{2,3,1,0:T(8,128)S(1)}, s32[4]{0:T(128)S(1)}, /*...) while((s32[]{:T(128)}, f32[3,3,384]{2,1,0:T(4,128)S(1)}, ...), condition=%wide.region_8.9_spmd.clone, body=%wide.region_3.8_spmd.clone.sunk | while | flops 357883392 | bytes 19853104 | solution.py:127
  185.6 46.6 %all-gather.11.cloned.1.call-done = bf16[1,576,1536]{2,0,1:T(2,128)(2,1)} async-done(((bf16[1,36,1536]{2,0,1:T(2,128)(2,1)}), bf16[1,576,1536]{2,0,1:T(2,128)(2,1)}) %all-gather.11.cloned.1.call-update) | async-done | bytes 1769488 | tf_op jit(solution)/shard_map/all_gather | solution.py:333
  240.6 32.1 %all-gather.13.cloned.1.call-done = bf16[1,1536,576]{2,1,0:T(8,128)(2,1)} async-done(((bf16[1,96,576]{2,1,0:T(8,128)(2,1)}), bf16[1,1536,576]{2,1,0:T(8,128)(2,1)}) %all-gather.13.cloned.1.call-update) | async-done | bytes 1769488 | tf_op jit(solution)/shard_map/all_gather | solution.py:334
  279.3 9.2 collective-permute-done
  291.8 30.1 %all-gather.15.cloned.1.call-done = bf16[1536,384]{0,1:T(8,128)(2,1)} async-done(((bf16[384,384]{0,1:T(8,128)(2,1)}), bf16[1536,384]{0,1:T(8,128)(2,1)}) %all-gather.15.cloned.1.call-update) | async-done | bytes 1179664 | tf_op jit(solution)/shard_map/all_gather | solution.py:86
  327.6 17.9 %while.94 = (s32[]{:T(128)}, f32[3,3,384]{2,1,0:T(4,128)S(1)}, f32[3,3,384]{2,1,0:T(4,128)S(1)}, f32[3,3,384,64]{2,3,1,0:T(8,128)}, s32[4]{0:T(128)S(1)}, /*inde...) while((s32[]{:T(128)}, f32[3,3,384]{2,1,0:T(4,128)S(1)}, ...), condition=%wide.region_18.19_spmd.clone, body=%wide.region_13.18_spmd.clone.sunk | while | flops 357883392 | bytes 26931048 | solution.py:127
  329.5 5.2 conditional.19
  358.0 8.5 collective-permute-done.1
  373.5 37.0 %all-gather.17.cloned.1.call-done = bf16[1536,384]{0,1:T(8,128)(2,1)} async-done(((bf16[384,384]{0,1:T(8,128)(2,1)}), bf16[1536,384]{0,1:T(8,128)(2,1)}) %all-gather.17.cloned.1.call-update) | async-done | bytes 1179664 | tf_op jit(solution)/shard_map/all_gather | solution.py:86
  416.4 17.8 %while.95 = (s32[]{:T(128)}, f32[3,3,384]{2,1,0:T(4,128)S(1)}, f32[3,3,384]{2,1,0:T(4,128)S(1)}, f32[3,3,384,64]{2,3,1,0:T(8,128)}, s32[4]{0:T(128)S(1)}, /*inde...) while((s32[]{:T(128)}, f32[3,3,384]{2,1,0:T(4,128)S(1)}, ...), condition=%wide.region_28.29_spmd.clone, body=%wide.region_23.28_spmd.clone.sunk | while | flops 357883392 | bytes 26931048 | solution.py:127
  450.8 30.5 %while.96 = (s32[]{:T(128)}, f32[3,3,384,64]{2,3,1,0:T(8,128)S(1)}, bf16[4,384,384]{2,1,0:T(8,128)(2,1)}, s32[4]{0:T(128)}, s32[]{:T(128)}, /*index=5*/s32[384]{...) while((s32[]{:T(128)}, f32[3,3,384,64]{2,3,1,0:T(8,128)S(1)}, ...), condition=%wide.region_35.36_spmd.clone, body=%wide.region_32.35_spmd.clone.sunk | while | flops 864240384 | bytes 32788284 | solution.py:269
  453.5 8.1 conditional.21
  465.1 8.1 conditional.21
  490.6 43.9 %reduce-scatter.17.cloned.1.call-done = bf16[384,384]{1,0:T(8,128)(2,1)} async-done(((bf16[1536,384]{1,0:T(8,128)(2,1)}), bf16[384,384]{1,0:T(8,128)(2,1)}) %reduce-scatter.17.cloned.1.call-update) | async-done | bytes 294928 | tf_op jit(solution)/shard_map/reduce_scatter | solution.py:274
  553.3 5.6 collective-permute-done.2
  568.9 30.0 %while.97 = (s32[]{:T(128)}, f32[3,3,384,64]{2,3,1,0:T(8,128)S(1)}, bf16[4,384,384]{2,1,0:T(8,128)(2,1)}, s32[4]{0:T(128)}, s32[]{:T(128)}, /*index=5*/s32[384]{...) while((s32[]{:T(128)}, f32[3,3,384,64]{2,3,1,0:T(8,128)S(1)}, ...), condition=%wide.region_43.44_spmd.clone, body=%wide.region_40.43_spmd.clone.sunk | while | flops 864240384 | bytes 32788284 | solution.py:269
  571.4 8.1 conditional.22
  582.9 8.1 conditional.22
  616.1 27.0 %reduce-scatter.19.cloned.1.call-done = bf16[384,384]{1,0:T(8,128)(2,1)} async-done(((bf16[1536,384]{1,0:T(8,128)(2,1)}), bf16[384,384]{1,0:T(8,128)(2,1)}) %reduce-scatter.19.cloned.1.call-update) | async-done | bytes 294928 | tf_op jit(solution)/shard_map/reduce_scatter | solution.py:274
  660.6 5.3 collective-permute-done.3
  674.8 24.8 %while.98 = (s32[]{:T(128)}, f32[3,3,384,64]{2,3,1,0:T(8,128)S(1)}, bf16[4,384,384]{2,1,0:T(8,128)(2,1)}, s32[4]{0:T(128)S(1)}, s32[]{:T(128)}, /*index=5*/s32[3...) while((s32[]{:T(128)}, f32[3,3,384,64]{2,3,1,0:T(8,128)S(1)}, ...), condition=%wide.region_51.52_spmd.clone, body=%wide.region_48.51_spmd.clone.sunk | while | flops 864240384 | bytes 32797500 | solution.py:269
  676.6 6.7 conditional.23
  686.1 6.7 conditional.23
  717.5 5.5 add_add_fusion.1
  731.5 9.3 reduce-scatter.21.cloned.1.call-done
  746.4 154.8 %fusion.326 = (f32[48,576]{1,0:T(8,128)}, f32[40,192]{1,0:T(8,128)}, f32[40,192]{1,0:T(8,128)}, f32[48,576]{1,0:T(8,128)}, f32[40,1536]{1,0:T(8,128)}, /*index=5*/f32[40,1536]{1,0:T(8,128)}) fusion(f32[576,576]{1,0:T(8,128)} %add_add_fusion.4, f32[576,192]{1,0:T(8,128)} %fusion.168, f32[576,192]{1,0:T(8,128)} %fusion.167, f32[576,576]{1,0:T(8,128)} %add_add_fusion.3, ...), kind=kCustom, calls=%all-reduce-scatter.6 | all-reduce-scatter fusion | flops 3096578 | bytes 11391488
  923.6 25.3 %all-reduce.16 = (f32[576]{0:T(1024)}, f32[576]{0:T(1024)}) all-reduce(f32[576]{0:T(1024)S(1)} %add_add_fusion.6, f32[576]{0:T(1024)S(1)} %add_add_fusion.5), channel_id=30, replica_groups=mesh['section'=2,'ctx'=4,'fsdp'=4] {'ctx','fsdp'}, use_global_device_ids=true, to_apply=%region_76.77.clone | all-reduce | flops 1152 | bytes 9216
  (928 shorter events, 415.4 us)
Async XLA Ops:
  7.2 152.1 %all-gather.7.cloned.1.call-start = ((), (), s32[]{:S(2)}) async-start(), calls=%async_computation.4 | async-start | bytes 1474560 | tf_op jit(solution)/shard_map/all_gather | solution.py:86
  11.4 147.7 %copy-start.95 = (f32[384,64]{0,1:T(8,128)}, f32[384,64]{0,1:T(8,128)S(1)}, u32[]{:S(2)}) copy-start(f32[384,64]{0,1:T(8,128)S(1)} %pad_maximum_fusion.8) | copy-start | bytes 294916
  92.0 91.1 %all-gather.9.cloned.1.call-start = ((), (), s32[]{:S(2)}) async-start(), calls=%async_computation.5 | async-start | bytes 3760128 | tf_op jit(solution)/shard_map/all_gather | solution.py:332
  93.0 139.2 %all-gather.11.cloned.1.call-start = ((), (), s32[]{:S(2)}) async-start(), calls=%async_computation.6 | async-start | bytes 3760128 | tf_op jit(solution)/shard_map/all_gather | solution.py:333
  93.9 178.7 %all-gather.13.cloned.1.call-start = ((), (), s32[]{:S(2)}) async-start(), calls=%async_computation.7 | async-start | bytes 2088960 | tf_op jit(solution)/shard_map/all_gather | solution.py:334
  94.5 227.4 %all-gather.15.cloned.1.call-start = ((), (), s32[]{:S(2)}) async-start(), calls=%async_computation.8 | async-start | bytes 1474560 | tf_op jit(solution)/shard_map/all_gather | solution.py:86
  276.0 12.5 %collective-permute-start = (bf16[384,576]{0,1:T(8,128)(2,1)S(1)}, bf16[384,576]{0,1:T(8,128)(2,1)S(1)}, u32[]{:S(2)}, u32[]{:S(2)}) collective-permute-start(bf16[384,576]{0,1:T(8,128)(2,1)S(1)} %fusion.164), channel_id=1, source_target_pairs={{0,16},{1,17},{2,18},{3,19},{4,20},{5,21},{6,22},{7,23},{8,24},{9,... | collective-permute-start | bytes 1327112 | tf_op jit(solution)/shard_map/ppermute | solution.py:19
  290.4 120.1 %all-gather.17.cloned.1.call-start = ((), (), s32[]{:S(2)}) async-start(), calls=%async_computation.9 | async-start | bytes 1474560 | tf_op jit(solution)/shard_map/all_gather | solution.py:86
  354.8 11.7 %collective-permute-start.1 = (bf16[384,576]{0,1:T(8,128)(2,1)S(1)}, bf16[384,576]{0,1:T(8,128)(2,1)S(1)}, u32[]{:S(2)}, u32[]{:S(2)}) collective-permute-start(bf16[384,576]{0,1:T(8,128)(2,1)S(1)} %get-tuple-element.1530), channel_id=1, source_target_pairs={{0,16},{1,17},{2,18},{3,19},{4,20},{5,21},{6,22},{7,23},{8,24},{9,... | collective-permute-start | bytes 1327112 | tf_op jit(solution)/shard_map/ppermute | solution.py:19
  366.4 179.1 %copy-start.9 = (bf16[384,576]{0,1:T(8,128)(2,1)}, bf16[384,576]{0,1:T(8,128)(2,1)S(1)}, u32[]{:S(2)}) copy-start(bf16[384,576]{0,1:T(8,128)(2,1)S(1)} %collective-permute-done.1) | copy-start | bytes 1327108
  368.2 166.3 %reduce-scatter.17.cloned.1.call-start = ((), (), s32[]{:S(2)}) async-start(), calls=%async_computation.10 | async-start | bytes 1474560 | tf_op jit(solution)/shard_map/reduce_scatter | solution.py:274
  481.3 161.8 %reduce-scatter.19.cloned.1.call-start = ((), (), s32[]{:S(2)}) async-start(), calls=%async_computation.11 | async-start | bytes 1474560 | tf_op jit(solution)/shard_map/reduce_scatter | solution.py:274
  545.9 13.0 %collective-permute-start.2 = (bf16[384,576]{0,1:T(8,128)(2,1)S(1)}, bf16[384,576]{0,1:T(8,128)(2,1)S(1)}, u32[]{:S(2)}, u32[]{:S(2)}) collective-permute-start(bf16[384,576]{0,1:T(8,128)(2,1)S(1)} %fusion.198), channel_id=1, source_target_pairs={{16,0},{17,1},{18,2},{19,3},{20,4},{21,5},{22,6},{23,7},{24,8},{25... | collective-permute-start | bytes 1327112 | tf_op jit(solution)/shard_map/ppermute | solution.py:19
  599.0 141.9 %reduce-scatter.21.cloned.1.call-start = ((), (), s32[]{:S(2)}) async-start(), calls=%async_computation.12 | async-start | bytes 1474560 | tf_op jit(solution)/shard_map/reduce_scatter | solution.py:274
  652.7 13.1 %collective-permute-start.3 = (bf16[384,576]{0,1:T(8,128)(2,1)S(1)}, bf16[384,576]{0,1:T(8,128)(2,1)S(1)}, u32[]{:S(2)}, u32[]{:S(2)}) collective-permute-start(bf16[384,576]{0,1:T(8,128)(2,1)S(1)} %fusion.306), channel_id=1, source_target_pairs={{16,0},{17,1},{18,2},{19,3},{20,4},{21,5},{22,6},{23,7},{24,8},{25... | collective-permute-start | bytes 1327112 | tf_op jit(solution)/shard_map/ppermute | solution.py:19
  699.6 308.0 %reduce-scatter.23.cloned.1.call-start = ((), (), s32[]{:S(2)}) async-start(), calls=%async_computation.13 | async-start | bytes 4177920 | tf_op jit(solution)/shard_map/reduce_scatter | solution.py:389
  902.8 58.6 %collective-permute-start.10 = (f32[40,192]{1,0:T(8,128)}, f32[40,192]{1,0:T(8,128)}, u32[]{:S(2)}, u32[]{:S(2)}) collective-permute-start(f32[40,192]{1,0:T(8,128)} %get-tuple-element.1440), channel_id=1, source_target_pairs={{0,1},{1,2},{2,3},{3,4},{4,5},{5,6},{6,7},{7,8},{8,9},{9,10},{10,1... | collective-permute-start | bytes 92168
  908.5 62.5 %collective-permute-start.8 = (f32[40,192]{1,0:T(8,128)}, f32[40,192]{1,0:T(8,128)}, u32[]{:S(2)}, u32[]{:S(2)}) collective-permute-start(f32[40,192]{1,0:T(8,128)} %get-tuple-element.1439), channel_id=1, source_target_pairs={{0,1},{1,2},{2,3},{3,4},{4,5},{5,6},{6,7},{7,8},{8,9},{9,10},{10,1... | collective-permute-start | bytes 92168
  910.4 48.4 %collective-permute-start.11 = (f32[20,192]{1,0:T(8,128)}, f32[20,192]{1,0:T(8,128)}, u32[]{:S(2)}, u32[]{:S(2)}) collective-permute-start(f32[20,192]{1,0:T(8,128)} %slice.267), channel_id=1, source_target_pairs={{0,2},{1,3},{2,4},{3,5},{4,6},{5,7},{6,8},{7,9},{8,10},{9,11},{10,... | collective-permute-start | bytes 46088
  913.3 54.5 %collective-permute-start.9 = (f32[20,192]{1,0:T(8,128)}, f32[20,192]{1,0:T(8,128)}, u32[]{:S(2)}, u32[]{:S(2)}) collective-permute-start(f32[20,192]{1,0:T(8,128)} %slice.266), channel_id=1, source_target_pairs={{0,2},{1,3},{2,4},{3,5},{4,6},{5,7},{6,8},{7,9},{8,10},{9,11},{10,... | collective-permute-start | bytes 46088
  955.0 46.5 %collective-permute-start.18 = (f32[40,1536]{1,0:T(8,128)S(1)}, f32[40,1536]{1,0:T(8,128)S(1)}, u32[]{:S(2)}, u32[]{:S(2)}) collective-permute-start(f32[40,1536]{1,0:T(8,128)S(1)} %copy-done.140), channel_id=1, source_target_pairs={{0,1},{1,2},{2,3},{3,4},{4,5},{5,6},{6,7},{7,8},{8,9},{9,10},{10,1... | collective-permute-start | bytes 737288
  958.9 22.4 %collective-permute-start.12 = (f32[48,576]{1,0:T(8,128)S(1)}, f32[48,576]{1,0:T(8,128)S(1)}, u32[]{:S(2)}, u32[]{:S(2)}) collective-permute-start(f32[48,576]{1,0:T(8,128)S(1)} %copy-done.161), channel_id=1, source_target_pairs={{0,1},{1,2},{2,3},{3,4},{4,5},{5,6},{6,7},{7,8},{8,9},{9,10},{10,1... | collective-permute-start | bytes 331784
  961.4 24.6 %collective-permute-start.13 = (f32[48,576]{1,0:T(8,128)S(1)}, f32[48,576]{1,0:T(8,128)S(1)}, u32[]{:S(2)}, u32[]{:S(2)}) collective-permute-start(f32[48,576]{1,0:T(8,128)S(1)} %copy-done.161), channel_id=1, source_target_pairs={{0,2},{1,3},{2,4},{3,5},{4,6},{5,7},{6,8},{7,9},{8,10},{9,11},{10,... | collective-permute-start | bytes 331784
  967.9 20.8 %collective-permute-start.14 = (f32[48,576]{1,0:T(8,128)S(1)}, f32[48,576]{1,0:T(8,128)S(1)}, u32[]{:S(2)}, u32[]{:S(2)}) collective-permute-start(f32[48,576]{1,0:T(8,128)S(1)} %copy-done.161), channel_id=1, source_target_pairs={{0,3},{1,4},{2,5},{3,6},{4,7},{5,8},{6,9},{7,10},{8,11},{9,12},{10... | collective-permute-start | bytes 331784
  971.1 6.8 collective-permute-start.15
  977.8 13.8 %collective-permute-start.7 = (f32[36,576]{1,0:T(8,128)S(1)}, f32[36,576]{1,0:T(8,128)S(1)}, u32[]{:S(2)}, u32[]{:S(2)}) collective-permute-start(f32[36,576]{1,0:T(8,128)S(1)} %slice.265), channel_id=1, source_target_pairs={{0,4},{1,5},{2,6},{3,7},{4,8},{5,9},{6,10},{7,11},{8,12},{9,13},{1... | collective-permute-start | bytes 248840
  981.3 13.2 %collective-permute-start.4 = (f32[48,576]{1,0:T(8,128)S(1)}, f32[48,576]{1,0:T(8,128)S(1)}, u32[]{:S(2)}, u32[]{:S(2)}) collective-permute-start(f32[48,576]{1,0:T(8,128)S(1)} %copy-done.160), channel_id=1, source_target_pairs={{0,1},{1,2},{2,3},{3,4},{4,5},{5,6},{6,7},{7,8},{8,9},{9,10},{10,1... | collective-permute-start | bytes 331784
  986.1 11.2 %collective-permute-start.5 = (f32[48,576]{1,0:T(8,128)S(1)}, f32[48,576]{1,0:T(8,128)S(1)}, u32[]{:S(2)}, u32[]{:S(2)}) collective-permute-start(f32[48,576]{1,0:T(8,128)S(1)} %copy-done.160), channel_id=1, source_target_pairs={{0,2},{1,3},{2,4},{3,5},{4,6},{5,7},{6,8},{7,9},{8,10},{9,11},{10,... | collective-permute-start | bytes 331784
  988.6 10.6 %collective-permute-start.6 = (f32[48,576]{1,0:T(8,128)S(1)}, f32[48,576]{1,0:T(8,128)S(1)}, u32[]{:S(2)}, u32[]{:S(2)}) collective-permute-start(f32[48,576]{1,0:T(8,128)S(1)} %copy-done.160), channel_id=1, source_target_pairs={{0,3},{1,4},{2,5},{3,6},{4,7},{5,8},{6,9},{7,10},{8,11},{9,12},{10... | collective-permute-start | bytes 331784
  991.6 9.8 collective-permute-start.19
  994.5 11.8 %collective-permute-start.16 = (f32[40,1536]{1,0:T(8,128)S(1)}, f32[40,1536]{1,0:T(8,128)S(1)}, u32[]{:S(2)}, u32[]{:S(2)}) collective-permute-start(f32[40,1536]{1,0:T(8,128)S(1)} %copy-done.139), channel_id=1, source_target_pairs={{0,1},{1,2},{2,3},{3,4},{4,5},{5,6},{6,7},{7,8},{8,9},{9,10},{10,1... | collective-permute-start | bytes 737288
  997.3 9.0 collective-permute-start.17
  (210 other events, 1646.6 us)
Sparse Core Ops, SparseCore 0:
  92.1 33.4 all-gather.6
  128.5 54.6 all-gather.8
  186.0 46.1 all-gather.10
  234.3 38.2 all-gather.12
  290.5 31.3 all-gather.14
  368.4 42.1 all-gather.16
  481.4 53.0 reduce-scatter.16
  599.1 43.9 reduce-scatter.18
  699.7 41.0 reduce-scatter.20
  745.2 97.3 reduce-scatter.22
where the time goes:
time: 1020 us; the launch traced here: 1010 us
  blocking collectives  311 us (30%)
  waiting for transfers between devices  261 us (26%)
  matrix products  160 us (16%)
  local copies, waits for them, and re-layouts  121 us (12%)
  starting transfers between devices  61.2 us (6%)
  other arithmetic  48 us (5%)
  loops' own time  32 us (3%)
  between operations  20.3 us (2%)
    unnamed x3, blocking collectives  202 us
    reduce_scatter x3, waiting for transfers between devices, layer_backward(): lax.psum_scatter(pair_grads.astype(jnp.bfloat16), 'ctx', scatter_dimensio...  80.2 us
    all_gather x3, waiting for transfers between devices, layer_forward(): received = lax.all_gather(pairs, 'ctx', axis=0, tiled=True)  67.1 us
    unnamed x16, starting transfers between devices  50 us
    all_gather x1, waiting for transfers between devices, shards(): lax.all_gather(w_up, ('ctx', 'fsdp'), axis=1, tiled=True)  46.6 us
    unnamed x431, local copies, waits for them, and re-layouts  44.7 us
    all_gather x1, blocking collectives, shards(): lax.all_gather(w_query, ('ctx', 'fsdp'), axis=1, tiled=True)  32.4 us
    all_gather x1, waiting for transfers between devices, shards(): lax.all_gather(w_down, ('ctx', 'fsdp'), axis=1, tiled=True)  32.1 us
  transfers between devices with their start and end apart: 30, of which 14 were waited for; matrix products, arithmetic and copies ran while one was open for 28% of the time, Pallas kernels for 0%

commit v1 on v0

v1 whole, which is shorter than its diff:
```python
import functools

import jax
import jax.numpy as jnp
from jax import lax
from jax.experimental import pallas as pl
from jax.experimental.pallas import tpu as pltpu
from jax.sharding import PartitionSpec as P

D = 576
HQ = 9
KV = 3
HD = 64
GROUP = HQ // KV
QW = HQ * HD
KW = KV * HD
TURNED = QW + KW
MIXED = 2 * QW + 2 * KW
HALF = MIXED // 2

EPSILON = 1e-05
THETA = 10000.0
BF = jnp.bfloat16
F32 = jnp.float32
I32 = jnp.int32
MIB = 1024 * 1024


def mm(left, right):
    return jnp.dot(left, right, preferred_element_type=F32)


def mm_nt(left, right):
    return lax.dot_general(left, right, (((1,), (1,)), ((), ())), preferred_element_type=F32)


def mm_tn(left, right):
    return lax.dot_general(left, right, (((0,), (0,)), ((), ())), preferred_element_type=F32)


def struct(shape, dtype):
    return jax.ShapeDtypeStruct(shape, dtype)


def flip(count, bit):
    return [(i, i ^ bit) for i in range(count)]


def ring(count, steps):
    return [(i, (i + steps) % count) for i in range(count)]


def swap_core(value):
    return lax.ppermute(value, "fsdp", flip(4, 1))


def swap_y(value):
    return lax.ppermute(value, "fsdp", flip(4, 2))


def swap_zpair(value):
    return lax.ppermute(value, "ctx", flip(4, 1))


def swap_x(value):
    return lax.ppermute(value, "section", flip(2, 1))


def spread_pairs(odd):
    pairs = []
    for z in range(4):
        for f in range(4):
            y, c = f // 2, f % 2
            half = 2 * z + odd
            member = min(half, 7 - half)
            pairs.append((z * 4 + f, (2 * c + member // 2) * 4 + 2 * y + member % 2))
    return pairs


def backwards(pairs):
    return [(target, source) for source, target in pairs]


def turn_tables(offsets):
    middle = HD // 2
    frequency = THETA ** (-jnp.arange(middle, dtype=F32) * 2.0 / HD)
    angles = offsets.astype(F32)[:, None] * frequency[None, :]
    cosine, sine = jnp.cos(angles), jnp.sin(angles)
    return jnp.concatenate([cosine] * 4, axis=1), jnp.concatenate([-sine, sine] * 2, axis=1)


def turn(values, cosine, sine):
    low = lax.broadcasted_iota(I32, (values.shape[0], 128), 1) % HD < HD // 2
    tiles = []
    for first in range(0, values.shape[1], 128):
        tile = values[:, first : first + 128]
        beside = jnp.where(low, pltpu.roll(tile, 128 - HD // 2, 1), pltpu.roll(tile, HD // 2, 1))
        tiles.append(tile * cosine + beside * sine)
    return jnp.concatenate(tiles, axis=1)


def norm(values, gain):
    inverse = lax.rsqrt(jnp.mean(values * values, axis=-1, keepdims=True) + EPSILON)
    scaled = values * inverse
    return inverse, scaled, (scaled * gain).astype(BF)


def norm_back(d_normed, scaled, inverse, gain):
    gain_grad = jnp.sum(d_normed * scaled, axis=0, keepdims=True)
    d_scaled = d_normed * gain
    d_source = inverse * (d_scaled - scaled * jnp.mean(d_scaled * scaled, axis=-1, keepdims=True))
    return d_source, gain_grad


def split_heads(piece_refs, key_scr, value_scr, parts):
    count = sum(ref.shape[0] for ref in piece_refs)
    index = 0
    for ref in piece_refs:
        rows = ref.shape[1] // parts
        for slot in range(ref.shape[0]):
            for part in range(parts):
                block = ref[slot, part * rows : (part + 1) * rows, :]
                at = pl.ds((part * count + index) * rows, rows)
                for group in range(KV):
                    key_scr[group, at, :] = block[:, group * HD : (group + 1) * HD]
                    value_scr[group, at, :] = block[:, KW + group * HD : KW + (group + 1) * HD]
            index += 1


def each_job(jobs, tile, visit):
    if tile is None:
        for first, rows, keys in jobs:
            visit(first, rows, keys)
        return
    _, rows, keys = jobs[0]

    @pl.loop(0, rows // tile)
    def _(step):
        visit(pl.multiple_of(step * tile, tile), tile, keys)


def store(slot, refs, at, value):
    for index, ref in enumerate(refs):

        @pl.when(slot == index)
        def _(ref=ref):
            ref[at] = value


def job_bias(first, rows, keys, position_ref, start_ref, key_position_ref):
    at = key_position_ref[:, :keys]
    allowed = (at <= position_ref[pl.ds(first, rows), :]) & (at >= start_ref[pl.ds(first, rows), :])
    return jnp.where(allowed, 0.0, -1e30)


def project_kernel(source_ref, mixed_ref, gain_ref, cosine_ref, sine_ref, query_ref, pairs_ref):
    _, _, normed = norm(source_ref[...].astype(F32), gain_ref[...])
    both = turn(mm(normed, mixed_ref[:, :TURNED]), cosine_ref[...], sine_ref[...]).astype(BF)
    edge = (2 * QW + KW) // 128 * 128
    values = mm(normed, mixed_ref[:, edge:])[:, 2 * QW + KW - edge :].astype(BF)
    query_ref[...] = both[:, :QW]
    pairs_ref[...] = jnp.concatenate([both[:, QW:], values], axis=1)


def attend_kernel(
    jobs, tile, parts, pieces,
    source_ref, query_ref, position_ref, start_ref, key_position_ref, mixed_ref, *refs,
):
    piece_refs, refs = refs[:pieces], refs[pieces:]
    attended_ref, log_ref, middle_ref = refs[:3]
    query_scr, key_scr, value_scr, out_scr, log_scr = refs[3:]
    split_heads(piece_refs, key_scr, value_scr, parts)
    for head in range(HQ):
        query_scr[head] = query_ref[:, head * HD : (head + 1) * HD] * jnp.asarray(HD**-0.5, BF)

    def visit(first, rows, keys):
        bias = job_bias(first, rows, keys, position_ref, start_ref, key_position_ref)
        at = pl.ds(first, rows)

        @pl.loop(0, KV)
        def _(group):
            key = key_scr[group, :keys, :]
            value = value_scr[group, :keys, :]
            for member in range(GROUP):
                head = group * GROUP + member
                scores = mm_nt(query_scr[head, at, :], key) + bias
                peak = jnp.max(scores, axis=1, keepdims=True)
                weights = jnp.exp(scores - peak)
                total = jnp.sum(weights, axis=1, keepdims=True)
                out_scr[head, at, :] = mm(weights.astype(BF), value) * (1.0 / total)
                log_scr[head, at, :] = peak + jnp.log(total)

    each_job(jobs, tile, visit)
    out = jnp.concatenate([out_scr[head] for head in range(HQ)], axis=1)
    attended_ref[...] = out
    log_ref[...] = jnp.concatenate([log_scr[head] for head in range(HQ)], axis=1)
    added = mm(out.astype(BF), mixed_ref[:, TURNED : TURNED + QW])
    middle_ref[...] = source_ref[...].astype(F32) + added


def mlp_kernel(middle_ref, gate_ref, up_ref, down_ref, gain_ref, result_ref, normed_scr, total_scr):
    middle = middle_ref[...]
    normed_scr[...] = norm(middle, gain_ref[...])[2]
    total_scr[...] = middle
    width = 384

    @pl.loop(0, gate_ref.shape[1] // width)
    def _(step):
        at = pl.ds(pl.multiple_of(step * width, width), width)
        gate = mm(normed_scr[...], gate_ref[:, at])
        up = mm(normed_scr[...], up_ref[:, at])
        hidden = (gate * jax.nn.sigmoid(gate) * up).astype(BF)
        total_scr[...] += mm(hidden, down_ref[at, :])

    result_ref[...] = total_scr[...].astype(BF)


def mlp_back_kernel(
    core_ref, d_result_ref, middle_ref, mixed_ref, gate_ref, up_ref, down_ref, gain_ref, *refs
):
    packed_refs, (gain_grad_ref, d_middle_ref, d_out_ref, normed_scr, total_scr) = refs[:2], refs[2:]
    core = core_ref[0]
    gain = gain_ref[...]
    inverse, scaled, normed = norm(middle_ref[...], gain)
    normed_scr[...] = normed
    total_scr[...] = jnp.zeros_like(total_scr)
    width = 384

    @pl.loop(0, gate_ref.shape[1] // width)
    def _(step):
        at = pl.ds(pl.multiple_of(step * width, width), width)
        low = d_result_ref[...]
        normed = normed_scr[...]
        gate = mm(normed, gate_ref[:, at])
        up = mm(normed, up_ref[:, at])
        d_hidden = mm_nt(low, down_ref[at, :])
        sigmoid = jax.nn.sigmoid(gate)
        silu = gate * sigmoid
        d_gate = (d_hidden * up * sigmoid * (1.0 + gate * (1.0 - sigmoid))).astype(BF)
        d_up = (d_hidden * silu).astype(BF)
        hidden = (silu * up).astype(BF)
        total_scr[...] += mm_nt(d_gate, gate_ref[:, at]) + mm_nt(d_up, up_ref[:, at])
        gate_grad = mm_tn(normed, d_gate)
        up_grad = mm_tn(normed, d_up)
        down_grad = mm_tn(hidden, low)
        slot = (step // 2) ^ core
        columns = pl.ds(pl.multiple_of((step % 2) * width, width), width)
        wide = [
            jnp.concatenate([grad[72 * k : 72 * k + 72] for grad in (gate_grad, up_grad)], axis=0)
            for k in range(8)
        ]
        wide = jnp.stack(wide).astype(BF)
        store(slot, packed_refs, (slice(None), slice(0, 144), columns), wide)
        down_grad = down_grad.reshape(2, 2, 96, D).astype(BF)
        down_grad = jnp.concatenate([down_grad, jnp.zeros((2, 2, 96, HALF - D), BF)], axis=3)
        for side in (0, 1):
            at = (pl.ds(2 * step, 2), slice(144, 240), slice(None))
            store(core ^ side, packed_refs, at, down_grad[:, side])

    d_mlp, gain_grad = norm_back(total_scr[...], scaled, inverse, gain)
    gain_grad_ref[...] = gain_grad
    d_middle = d_result_ref[...].astype(F32) + d_mlp
    d_middle_ref[...] = d_middle
    d_out_ref[...] = mm_nt(d_middle.astype(BF), mixed_ref[:, TURNED : TURNED + QW]).astype(BF)


def attend_back_kernel(
    jobs, tile, parts, pieces,
    d_out_ref, attended_ref, log_ref, query_ref, position_ref, start_ref, key_position_ref, *refs,
):
    piece_refs, refs = refs[:pieces], refs[pieces:]
    d_query_ref, d_pairs_ref = refs[:2]
    (
        query_scr, key_scr, value_scr, d_out_scr, log_scr, delta_scr, d_query_scr,
        d_key_scr, d_value_scr,
    ) = refs[2:]
    d_out = d_out_ref[...]
    split_heads(piece_refs, key_scr, value_scr, parts)
    for head in range(HQ):
        at = slice(head * HD, (head + 1) * HD)
        query_scr[head] = query_ref[:, at] * jnp.asarray(HD**-0.5, BF)
        d_out_scr[head] = d_out[:, at]
        log_scr[head] = log_ref[:, head : head + 1]
        delta_scr[head] = jnp.sum(d_out[:, at].astype(F32) * attended_ref[:, at], 1, keepdims=True)
    d_key_scr[...] = jnp.zeros_like(d_key_scr)
    d_value_scr[...] = jnp.zeros_like(d_value_scr)

    def visit(first, rows, keys):
        bias = job_bias(first, rows, keys, position_ref, start_ref, key_position_ref)
        at = pl.ds(first, rows)

        @pl.loop(0, KV)
        def _(group):
            key = key_scr[group, :keys, :]
            value = value_scr[group, :keys, :]
            for member in range(GROUP):
                head = group * GROUP + member
                query = query_scr[head, at, :]
                d_out = d_out_scr[head, at, :]
                chances = jnp.exp(mm_nt(query, key) + bias - log_scr[head, at, :])
                d_chances = mm_nt(d_out, value)
                d_scores = (chances * (d_chances - delta_scr[head, at, :])).astype(BF)
                d_query_scr[head, at, :] = mm(d_scores, key) * HD**-0.5
                d_value_scr[group, :, :keys] += mm_tn(d_out, chances.astype(BF))
                d_key_scr[group, :, :keys] += mm_tn(query, d_scores)

    each_job(jobs, tile, visit)
    d_query_ref[...] = jnp.concatenate([d_query_scr[head] for head in range(HQ)], axis=1)
    count, rows = d_pairs_ref.shape[0], d_pairs_ref.shape[1] // parts
    for first in range(0, count * parts, parts):
        at = slice(first * rows, (first + parts) * rows)
        grads = [scr[group, :, at].T for scr in (d_key_scr, d_value_scr) for group in range(KV)]
        grads = jnp.concatenate(grads, axis=1).astype(BF)
        for index in range(parts):
            part, piece = divmod(first + index, count)
            d_pairs_ref[piece, part * rows : (part + 1) * rows, :] = grads[
                index * rows : (index + 1) * rows
            ]


def input_kernel(
    adds, core_ref, source_ref, attended_ref, d_middle_ref, d_query_ref, mixed_ref, gain_ref,
    mlp_gain_grad_ref, cosine_ref, sine_ref, *refs,
):
    add_refs, d_source_ref, packed_refs = refs[:adds], refs[adds], refs[adds + 1 :]
    core = core_ref[0]
    gain = gain_ref[...]
    inverse, scaled, normed = norm(source_ref[...].astype(F32), gain)
    d_pairs = sum(ref[...].astype(F32) for ref in add_refs)
    d_both = jnp.concatenate([d_query_ref[...], d_pairs[:, :KW]], axis=1)
    d_both = turn(d_both, cosine_ref[...], -sine_ref[...]).astype(BF)
    d_values = d_pairs[:, KW:].astype(BF)
    d_middle = d_middle_ref[...]
    edge = (2 * QW + KW) // 128 * 128
    lead = 2 * QW + KW - edge
    d_tail = jnp.concatenate([jnp.zeros((d_values.shape[0], lead), BF), d_values], axis=1)
    d_normed = mm_nt(d_both, mixed_ref[:, :TURNED]) + mm_nt(d_tail, mixed_ref[:, edge:])
    d_attn, gain_grad = norm_back(d_normed, scaled, inverse, gain)
    d_source_ref[...] = (d_middle + d_attn).astype(BF)
    first = mm_tn(normed, d_both)
    second = jnp.concatenate(
        [
            mm_tn(attended_ref[...].astype(BF), d_middle.astype(BF)),
            mm_tn(normed, d_values),
        ],
        axis=1,
    )
    gains = (gain_grad, mlp_gain_grad_ref[...])
    for half, grad in enumerate((first, second)):
        blocks = []
        for block in range(8):
            at = 36 * (2 * block + half)
            tail = jnp.concatenate([g[:, at : at + 36] for g in gains] + [jnp.zeros((6, 36), F32)])
            tail = jnp.concatenate([tail, jnp.zeros((8, HALF - 36), F32)], axis=1)
            blocks.append(jnp.concatenate([grad[72 * block : 72 * block + 72], tail], axis=0))
        store(half ^ core, packed_refs, Ellipsis, jnp.stack(blocks).astype(BF))


def join_rows(parts, first):
    return jnp.concatenate([part.astype(F32)[first : first + 72] for part in parts]).astype(BF)


def assemble_kernel(mixed, index_ref, *refs):
    pieces, outs = refs[:16], refs[16:]
    x, z, y, core = (index_ref[i] for i in range(4))
    for place, steps in enumerate((0, 1, 3, 2)):
        row = (z + 4 - steps) % 4
        at = pl.ds(pl.multiple_of(row * 144, 144), 144)
        for cross in (0, 1):
            first = 8 * (place // 2) + 4 * cross
            here, there = (
                [pieces[first + 2 * dx + dy][place % 2] for dy in (0, 1)] for dx in (0, 1)
            )
            here, there = (
                [jnp.where(y == 0, *part), jnp.where(y == 0, *part[::-1])] for part in (here, there)
            )
            sides = [
                jnp.concatenate(
                    [jnp.where(x == 0, a, b), jnp.where(x == 0, b, a)], axis=1
                )
                for a, b in zip(here, there)
            ]
            side = core ^ cross
            columns = pl.ds(pl.multiple_of(side * HALF, HALF), HALF)
            if mixed:
                outs[0][at, columns] = join_rows(sides, 0)
                for beside, part in enumerate(sides):
                    outs[1][4 * row + 2 * beside + side] = part[64:80, :128].astype(F32)
            else:
                outs[0][at, columns] = join_rows(sides, 0)
                outs[1][at, columns] = join_rows(sides, 72)
                for beside, part in enumerate(sides):
                    rows = pl.ds(pl.multiple_of((4 * row + 2 * beside + side) * 96, 96), 96)
                    outs[2][rows, :] = part[144:240, :D]


class Fast:
    parts = 2
    tile = None

    def __init__(self):
        self.section = lax.axis_index("section")
        self.z = lax.axis_index("ctx")
        f = lax.axis_index("fsdp")
        self.y = f // 2
        self.core = f % 2


    def positions_of(self, dz, dc, rows):
        member = 2 * ((self.z % 2) ^ dz) + (self.core ^ dc)
        iota = jnp.arange(rows // 2, dtype=I32)
        return jnp.concatenate([half * (rows // 2) + iota for half in (member, 7 - member)])

    def lengths(self, lengths):
        mine = lax.dynamic_index_in_dim(lengths[0], self.section, 0, keepdims=False)
        other = swap_core(mine)
        return jnp.where(self.z // 2 == self.core, mine, other)

    def spread(self, block):
        half = block.shape[0] // 2
        even, odd = (
            lax.ppermute(block[k * half : (k + 1) * half], ("ctx", "fsdp"), spread_pairs(k))
            for k in (0, 1)
        )
        low = jnp.where(self.core == 0, even, odd)
        return jnp.concatenate([low, jnp.where(self.core == 0, odd, even)], axis=0)

    def unspread(self, block):
        half = block.shape[0] // 2
        low, high = block[:half], block[half:]
        parts = (jnp.where(self.core == 0, low, high), jnp.where(self.core == 0, high, low))
        return jnp.concatenate(
            [
                lax.ppermute(part, ("ctx", "fsdp"), backwards(spread_pairs(k)))
                for k, part in enumerate(parts)
            ],
            axis=0,
        )

    def key_positions(self, rows):
        full = jnp.stack([self.positions_of(dz, dc, rows) for dc in (0, 1) for dz in (0, 1)])
        return full.reshape(4, 2, rows // 2).swapaxes(0, 1).reshape(1, -1)

    def jobs(self, rows, keys):
        return ((0, rows // 2, keys // 2), (rows // 2, rows // 2, keys))

    def share_pairs(self, pairs):
        along = swap_zpair(pairs)
        return [part[None] for part in (pairs, along, swap_core(pairs), swap_core(along))]

    def reduce_pairs(self, grads):
        received = swap_core(grads[2:])
        along = grads[1].astype(F32) + received[1].astype(F32)
        return [grads[0], received[0], swap_zpair(along.astype(BF))]


    def gather(self, wide, down, gains):
        count, rows, width = wide.shape
        mine = lax.dynamic_slice_in_dim(wide, self.core * HALF, HALF, 2)
        other = swap_core(lax.dynamic_slice_in_dim(wide, (1 - self.core) * HALF, HALF, 2))
        joined = jnp.concatenate(
            [jnp.where(self.core == 0, mine, other), jnp.where(self.core == 0, other, mine)], axis=1
        )
        gains = jnp.pad(gains, ((0, 6), (0, HALF - rows)))
        mixed = jnp.concatenate([joined[0], gains], axis=0)
        deep = jnp.concatenate(
            [joined[1], joined[2], jnp.pad(down, ((0, 0), (0, HALF - D)))], axis=0
        )
        index = jnp.stack([self.section, self.z, self.y, self.core])
        packs = []
        for part in (mixed, deep):
            quarter = HALF // 2
            mine, other = (
                lax.dynamic_slice_in_dim(part, x * quarter, quarter, 1)
                for x in (self.section, 1 - self.section)
            )
            packs.append((mine, swap_x(other)))
        layers = []
        for layer in (0, 1):
            weights = []
            for name, (own, theirs) in zip(("mixed", "deep"), packs):
                start = jnp.where(self.section == layer, own, theirs)
                above = lax.ppermute(start, "ctx", ring(4, 1))
                below = lax.ppermute(start, "ctx", ring(4, 3))
                across = lax.ppermute(above, "ctx", ring(4, 1))
                pieces = []
                first = jnp.stack([start, above])
                first_y = swap_y(first)
                square = [first, first_y, swap_x(first), swap_x(first_y)]
                pieces += square + [swap_core(part) for part in square]
                second = jnp.stack([below, across])
                second_x = swap_x(second)
                square = [second, swap_y(second), second_x, swap_y(second_x)]
                pieces += square + [swap_core(part) for part in square]
                weights.append(self.assemble(name == "mixed", index, pieces))
            (mixed, gains), (gate, up, down) = weights
            gains = gains[:, 8:10, :rows].swapaxes(0, 1).reshape(2, 1, D)
            layers.append((mixed, gate, up, down, gains[0], gains[1]))
        return layers

    def assemble(self, mixed, index, pieces):
        if mixed:
            outs = (struct((D, MIXED), BF), struct((16, 16, 128), F32))
        else:
            rows = 16 * (pieces[0].shape[1] - 144)
            outs = (struct((D, MIXED), BF), struct((D, MIXED), BF), struct((rows, D), BF))
        return pl.pallas_call(
            functools.partial(assemble_kernel, mixed),
            out_shape=outs,
            in_specs=[pl.BlockSpec(memory_space=pltpu.SMEM)]
            + [pl.BlockSpec(memory_space=pltpu.VMEM)] * 16,
            compiler_params=pltpu.CompilerParams(vmem_limit_bytes=32 * MIB),
            name="assemble",
        )(index, *pieces)

    def lanes(self, value, x):
        half = value.shape[-1] // 2
        return lax.dynamic_slice_in_dim(value, x * half, half, value.ndim - 1)

    def row(self, value, y):
        return lax.dynamic_index_in_dim(value, y, 1, keepdims=False)

    def reduce_part(self, keep, send):
        held = keep.astype(F32) + swap_core(send).astype(F32)
        held = held.reshape((4, 2) + held.shape[1:])
        x, y = self.section, self.y
        first, second = held[:2], held[2:]
        first_sent = self.lanes(first, 1 - x).astype(BF)
        second_sent = self.row(second, 1 - y).astype(BF)
        first = self.lanes(first, x) + swap_x(first_sent).astype(F32)
        second = self.row(second, y) + swap_y(second_sent).astype(F32)
        first_sent = self.row(first, 1 - y).astype(BF)
        second_sent = self.lanes(second, 1 - x).astype(BF)
        first = self.row(first, y) + swap_y(first_sent).astype(F32)
        second = self.lanes(second, x) + swap_x(second_sent).astype(F32)
        held = jnp.concatenate([first, second])
        low = held.astype(BF)
        total = lax.dynamic_index_in_dim(held, self.z, 0, keepdims=False)
        for steps in (1, 2, 3):
            part = lax.dynamic_index_in_dim(low, (self.z + steps) % 4, 0, keepdims=False)
            total = total + lax.ppermute(part, "ctx", ring(4, steps)).astype(F32)
        return total

    def reduce(self, deep, mixed):
        return self.reduce_part(*mixed), self.reduce_part(*deep)

    def finish(self, first, second, rows):
        joined = []
        for a, b in zip(first, second):
            own = jnp.where(self.section == 0, a, b)
            other = swap_x(jnp.where(self.section == 0, b, a).astype(BF)).astype(F32)
            joined.append(
                jnp.concatenate(
                    [
                        jnp.where(self.section == 0, own, other),
                        jnp.where(self.section == 0, other, own),
                    ],
                    axis=1,
                )
            )
        mixed, deep = joined
        wide = jnp.stack([mixed[: 2 * rows], deep[: 2 * rows], deep[2 * rows : 4 * rows]])
        wide = wide.reshape(3, 2, rows, HALF)
        keep = lax.dynamic_index_in_dim(wide, self.core, 1, keepdims=False)
        sent = lax.dynamic_index_in_dim(wide, 1 - self.core, 1, keepdims=False)
        received = swap_core(sent.astype(BF)).astype(F32)
        left = jnp.where(self.core == 0, keep, received)
        right = jnp.where(self.core == 0, received, keep)
        gains = mixed[2 * rows : 2 * rows + 2, :rows]
        return jnp.concatenate([left, right], axis=2), deep[4 * rows :, :D], gains


class Plain:
    parts = 1
    tile = 16

    def __init__(self):
        self.section = lax.axis_index("section")
        self.ctx = lax.axis_index("ctx")
        self.core = jnp.zeros((), I32)

    def positions_of(self, dz, dc, rows):
        return self.ctx * rows + jnp.arange(rows, dtype=I32)

    def lengths(self, lengths):
        return lax.dynamic_index_in_dim(lengths[0], self.section, 0, keepdims=False)

    def spread(self, block):
        return block

    def unspread(self, block):
        return block

    def key_positions(self, rows):
        return jnp.arange(lax.axis_size("ctx") * rows, dtype=I32)[None]

    def jobs(self, rows, keys):
        return ((0, rows, keys),)

    def share_pairs(self, pairs):
        return [lax.all_gather(pairs, "ctx", axis=0)]

    def reduce_pairs(self, grads):
        return [lax.psum_scatter(grads, "ctx", scatter_dimension=0)]

    def gather(self, wide, down, gains):
        own = (wide, down, gains)
        theirs = tuple(swap_x(part) for part in own)
        layers = []
        for layer in (0, 1):
            w, d, g = (jnp.where(self.section == layer, a, b) for a, b in zip(own, theirs))
            w = lax.all_gather(w, ("ctx", "fsdp"), axis=1, tiled=True)
            d = lax.all_gather(d, ("ctx", "fsdp"), axis=0, tiled=True)
            g = lax.all_gather(g, ("ctx", "fsdp"), axis=1, tiled=True).astype(F32)
            layers.append((w[0], w[1], w[2], d, g[0][None], g[1][None]))
        return layers

    def reduce(self, deep, mixed):
        def columns(pair, first):
            return jnp.concatenate([part[:, first : first + 72] for part in pair], axis=2)

        wide = jnp.stack([columns(mixed, 0), columns(deep, 0), columns(deep, 72)])
        down = jnp.stack([part[:, 144:, :D] for part in deep], axis=1)
        gains = jnp.stack([part[:, 72:74, :36] for part in mixed], axis=1)
        gains = jnp.moveaxis(gains.reshape(16, 2, 36), 1, 0)
        axes = ("ctx", "fsdp")
        return tuple(
            lax.psum_scatter(part, axes, scatter_dimension=axis, tiled=True).astype(F32)
            for part, axis in (
                (wide.reshape(3, D, MIXED), 1),
                (down.reshape(-1, D), 0),
                (gains.reshape(2, D), 1),
            )
        )

    def finish(self, first, second, rows):
        return tuple(
            jnp.where(self.section == 0, a, b) + swap_x(jnp.where(self.section == 0, b, a))
            for a, b in zip(first, second)
        )


def vmem_call(kernel, out_shape, args, scratch=(), scalars=0, limit=56, flops=0, name=None):
    specs = [pl.BlockSpec(memory_space=pltpu.SMEM)] * scalars
    specs += [pl.BlockSpec(memory_space=pltpu.VMEM)] * (len(args) - scalars)
    return pl.pallas_call(
        kernel,
        out_shape=out_shape,
        in_specs=specs,
        scratch_shapes=list(scratch),
        compiler_params=pltpu.CompilerParams(vmem_limit_bytes=limit * MIB),
        cost_estimate=pl.CostEstimate(flops=flops, bytes_accessed=16 * MIB, transcendentals=0),
        name=name,
    )(*args)


def layer_forward(net, source, weights, place):
    mixed, gate, up, down, g_attn, g_mlp = weights
    positions, starts, cosine, sine, key_positions = place
    rows = source.shape[0]
    queries, pairs = vmem_call(
        project_kernel,
        (struct((rows, QW), BF), struct((rows, 2 * KW), BF)),
        (source, mixed, g_attn, cosine, sine),
        flops=2 * rows * D * MIXED,
        name="project",
    )
    pieces = net.share_pairs(pairs)
    keys = key_positions.shape[1]
    attended, log_total, middle = vmem_call(
        functools.partial(
            attend_kernel, net.jobs(rows, keys), net.tile, net.parts, len(pieces)
        ),
        (struct((rows, QW), F32), struct((rows, HQ), F32), struct((rows, D), F32)),
        (source, queries, positions, starts, key_positions, mixed, *pieces),
        [
            pltpu.VMEM((HQ, rows, HD), BF),
            pltpu.VMEM((KV, keys, HD), BF),
            pltpu.VMEM((KV, keys, HD), BF),
            pltpu.VMEM((HQ, rows, HD), F32),
            pltpu.VMEM((HQ, rows, 1), F32),
        ],
        flops=2 * rows * D * QW + 4 * rows * keys * QW,
        name="attend",
    )
    result = vmem_call(
        mlp_kernel,
        struct((rows, D), BF),
        (middle, gate, up, down, g_mlp),
        [pltpu.VMEM((rows, D), BF), pltpu.VMEM((rows, D), F32)],
        flops=6 * rows * D * gate.shape[1],
        name="mlp",
    )
    return result, (source, queries, pieces, attended, log_total, middle)


def layer_backward(net, d_result, kept, weights, place):
    mixed, gate, up, down, g_attn, g_mlp = weights
    source, queries, pieces, attended, log_total, middle = kept
    positions, starts, cosine, sine, key_positions = place
    rows, keys = source.shape[0], key_positions.shape[1]
    core = net.core.reshape(1)
    deep_shape = struct((8, 144 + down.shape[0] // 16, HALF), BF)
    keep, send, gain_grad, d_middle, d_attended = vmem_call(
        mlp_back_kernel,
        (
            deep_shape,
            deep_shape,
            struct((1, D), F32),
            struct((rows, D), F32),
            struct((rows, QW), BF),
        ),
        (core, d_result, middle, mixed, gate, up, down, g_mlp),
        [pltpu.VMEM((rows, D), BF), pltpu.VMEM((rows, D), F32)],
        scalars=1,
        flops=18 * rows * D * gate.shape[1],
        name="mlp_back",
    )
    d_queries, d_pairs = vmem_call(
        functools.partial(
            attend_back_kernel, net.jobs(rows, keys), net.tile, net.parts, len(pieces)
        ),
        (struct((rows, QW), F32), struct((keys // rows, rows, 2 * KW), BF)),
        (d_attended, attended, log_total, queries, positions, starts, key_positions, *pieces),
        [
            pltpu.VMEM((HQ, rows, HD), BF),
            pltpu.VMEM((KV, keys, HD), BF),
            pltpu.VMEM((KV, keys, HD), BF),
            pltpu.VMEM((HQ, rows, HD), BF),
            pltpu.VMEM((HQ, rows, 1), F32),
            pltpu.VMEM((HQ, rows, 1), F32),
            pltpu.VMEM((HQ, rows, HD), F32),
            pltpu.VMEM((KV, HD, keys), F32),
            pltpu.VMEM((KV, HD, keys), F32),
        ],
        flops=10 * rows * keys * QW,
        name="attend_back",
    )
    adds = net.reduce_pairs(d_pairs)
    mixed_shape = struct((8, 80, HALF), BF)
    d_source, mixed_keep, mixed_send = vmem_call(
        functools.partial(input_kernel, len(adds)),
        (struct((rows, D), BF), mixed_shape, mixed_shape),
        (
            core, source, attended, d_middle, d_queries, mixed, g_attn, gain_grad, cosine, sine,
            *adds,
        ),
        scalars=1,
        flops=6 * rows * D * MIXED,
        name="input",
    )
    return d_source, net.reduce((keep, send), (mixed_keep, mixed_send))


def shards(
    inputs, lengths, cotangent, w_query, w_key, w_value, w_out, w_gate, w_up, w_down, g_attn, g_mlp
):
    sizes = tuple(lax.axis_size(axis) for axis in ("section", "ctx", "fsdp"))
    net = Fast() if sizes == (2, 4, 4) else Plain()
    rows = inputs.shape[2]
    wide = jnp.stack(
        [jnp.concatenate([w_query[0], w_key[0], w_out[0], w_value[0]], axis=1), w_gate[0], w_up[0]]
    )
    layers = net.gather(wide, w_down[0], jnp.stack([g_attn[0], g_mlp[0]]))

    source = net.spread(lax.dynamic_index_in_dim(inputs[0], net.section, 0, keepdims=False))
    d_result = net.spread(lax.dynamic_index_in_dim(cotangent[0], net.section, 0, keepdims=False))
    own = net.lengths(lengths)
    positions = net.positions_of(0, 0, rows)
    passed = (positions[:, None] >= jnp.cumsum(own)[None, :]).astype(I32)
    starts = jnp.sum(passed * own[None, :], axis=1)
    cosine, sine = turn_tables(positions - starts)
    place = (positions[:, None], starts[:, None], cosine, sine, net.key_positions(rows))

    first, kept_first = layer_forward(net, source, layers[0], place)
    second, kept_second = layer_forward(net, first, layers[1], place)
    d_first, total_second = layer_backward(net, d_result, kept_second, layers[1], place)
    d_input, total_first = layer_backward(net, d_first, kept_first, layers[0], place)
    wide_grad, down_grad, gain_grads = net.finish(total_first, total_second, w_query.shape[1])
    second = net.unspread(second)
    d_input = net.unspread(d_input)
    kept = jnp.where(net.section == 0, d_input, second)
    crossed = swap_x(jnp.where(net.section == 0, second, d_input))
    edges = jnp.stack(
        [jnp.where(net.section == 0, kept, crossed), jnp.where(net.section == 0, crossed, kept)]
    ).astype(F32)
    mixed = wide_grad[0]
    return (
        edges[None, None],
        mixed[None, :, :QW],
        mixed[None, :, QW:TURNED],
        mixed[None, :, TURNED + QW :],
        mixed[None, :, TURNED : TURNED + QW],
        wide_grad[1][None],
        wide_grad[2][None],
        down_grad[None],
        gain_grads[0][None],
        gain_grads[1][None],
    )


def solution(mesh):
    rows = P("section", ("ctx", "fsdp"), None)
    gains = P("section", ("ctx", "fsdp"))
    blocks = P("fsdp", None, "ctx", None)
    return jax.shard_map(
        shards,
        mesh=mesh,
        in_specs=(blocks, P("fsdp", None, None), blocks) + (rows,) * 7 + (gains,) * 2,
        out_specs=(P("section", "fsdp", None, "ctx", None),) + (rows,) * 7 + (gains,) * 2,
        check_vma=False,
    )
```

time: 1020 us -> 515 us (0.50)
  blocking collectives: 311 us -> 0 us
  matrix products: 160 us -> 0 us
  Pallas kernels: 0 us -> 147 us
  waiting for transfers between devices: 261 us -> 148 us
  starting transfers between devices: 61.2 us -> 144 us
  local copies, waits for them, and re-layouts: 121 us -> 38.4 us
  loops' own time: 32 us -> 0 us
  other arithmetic: 48 us -> 23.9 us
  between operations: 20.3 us -> 2.52 us
    unnamed x3 -> x0, blocking collectives: 202 us -> none
    dot_general x105 -> x0, matrix products: 160 us -> none  [the longest x6 13.2 us: revisit_block_work(): jnp.einsum('kgqd,nkd->kgqn', d_heads, key_block[:, 1], preferred_element_...]
    pallas_call x0 -> x16, Pallas kernels: none -> 147 us  [the longest x12 140 us: vmem_call(): pl.pallas_call(kernel, out_shape=out_shape, in_specs=specs, scratch_shape...]
    all_gather x6 -> x0, waiting for transfers between devices: 146 us -> none  [the longest x3 67.1 us: layer_forward(): received = lax.all_gather(pairs, 'ctx', axis=0, tiled=True)]
    ppermute x4 -> x126, starting transfers between devices: 9.96 us -> 144 us  [the longest x45 45.9 us: swap_core(): return lax.ppermute(value, 'fsdp', flip(4, 1))]
    ppermute x4 -> x126, waiting for transfers between devices: 28.6 us -> 148 us  [the longest x25 62.4 us: swap_x(): return lax.ppermute(value, 'section', flip(2, 1))]
    all_gather x4 -> x0, blocking collectives: 109 us -> none  [the longest x1 32.4 us: shards(): lax.all_gather(w_query, ('ctx', 'fsdp'), axis=1, tiled=True)]
    reduce_scatter x4 -> x0, waiting for transfers between devices: 80.2 us -> none  [the longest x3 80.2 us: layer_backward(): lax.psum_scatter(pair_grads.astype(jnp.bfloat16), 'ctx', scatter_dimensio...]
  transfers between devices with their start and end apart: 30 -> 126, of which waited for: 14 -> 36; matrix products, arithmetic and copies ran while one was open for 28% -> 8% of each run, Pallas kernels for 0% -> 10%
where the time goes in v1:
time: 515 us; the launch traced here: 505 us
  waiting for transfers between devices  148 us (29%)
  Pallas kernels  147 us (29%)
  starting transfers between devices  144 us (28%)
  local copies, waits for them, and re-layouts  38.4 us (7%)
  other arithmetic  23.9 us (5%)
    pallas_call x12, Pallas kernels, vmem_call(): pl.pallas_call(kernel, out_shape=out_shape, in_specs=specs, scratch_shape...  140 us
    ppermute x25, waiting for transfers between devices, swap_x(): return lax.ppermute(value, 'section', flip(2, 1))  62.4 us
    ppermute x45, starting transfers between devices, swap_core(): return lax.ppermute(value, 'fsdp', flip(4, 1))  45.9 us
    ppermute x25, starting transfers between devices, swap_x(): return lax.ppermute(value, 'section', flip(2, 1))  21.8 us
    unnamed x89, local copies, waits for them, and re-layouts  21.6 us
    ppermute x12, starting transfers between devices, reduce_part(): total = total + lax.ppermute(part, 'ctx', ring(4, steps)).astype(F32)  20.2 us
    ppermute x12, waiting for transfers between devices, reduce_part(): total = total + lax.ppermute(part, 'ctx', ring(4, steps)).astype(F32)  18.1 us
    ppermute x20, waiting for transfers between devices, swap_y(): return lax.ppermute(value, 'fsdp', flip(4, 2))  17.5 us
  transfers between devices with their start and end apart: 126, of which 36 were waited for; matrix products, arithmetic and copies ran while one was open for 8% of the time, Pallas kernels for 10%

profile of v1, /device:TPU:9, one launch (start us, length us, event | category | flops | bytes accessed | tf_op | source)
XLA Modules:
  0.0 504.7 jit_solution(6527780868332471640)
XLA Ops:
  2.9 4.8 collective-permute-start
  65.2 4.8 collective-permute-start.63
  76.7 9.7 %collective-permute-done.63 = bf16[192,576]{1,0:T(8,128)(2,1)S(1)} collective-permute-done((bf16[192,576]{1,0:T(8,128)(2,1)S(1)}, bf16[192,576]{1,0:T(8,128)(2,1)S(1)}, u32[]{:S(2)}, u32[]{:S(2)}) %collective-permute-start.63) | collective-permute-done | bytes 221216 | tf_op jit(solution)/shard_map/ppermute | solution.py:422
  101.4 3.7 project.2
  122.7 5.5 %collective-permute-done.29.refs_3_ = bf16[2,240,384]{2,1,0:T(8,128)(2,1)} collective-permute-done((bf16[2,240,384]{2,1,0:T(8,128)(2,1)S(1)}, bf16[2,240,384]{2,1,0:T(8,128)(2,1)}, u32[]{:S(2)}, u32[]{:S(2)}) %collective-permute-start.29) | collective-permute-done | bytes 368672 | tf_op jit(solution)/shard_map/ppermute | solution.py:66
  140.5 14.5 %attend.2 = (f32[384,576]{1,0:T(8,128)}, f32[384,9]{1,0:T(8,128)}, f32[384,576]{1,0:T(8,128)}) custom-call(bf16[384,576]{1,0:T(8,128)(2,1)} %pad_maximum_fusion.5.source_ref, bf16[384,576]{1,0:T(8,128)(2,1)} %get-tuple-element.52.query_ref, s32[384,1]{1,0:T(8,128)} %broadcast_in_dim.63.position_ref, s32[384,1]{1,0:T(8,128)} %reduce_sum.13.start_ref, ...), custom_call_target="tpu_custom_call" | custom-call | flops 1613758464 | bytes 16777216 | tf_op jit(solution)/shard_map/attend/pallas_call | solution.py:646
  164.0 8.3 %mlp.2.source_ref = bf16[384,576]{1,0:T(8,128)(2,1)} custom-call(f32[384,576]{1,0:T(8,128)} %get-tuple-element.55.middle_ref, bf16[576,1536]{1,0:T(8,128)(2,1)} %copy-done.6, bf16[576,1536]{1,0:T(8,128)(2,1)} %copy-done.7, bf16[1536,576]{1,0:T(8,128)(2,1)} %copy-done.4, f32[1,576]{1,0:T(1,128)} %squeeze.168.gain_ref), custom_call_target="tpu_custom_call" | custom-call | flops 2038431744 | bytes 16777216 | tf_op jit(solution)/shard_map/mlp/pallas_call | solution.py:646
  172.3 3.8 project.3
  177.2 7.8 %collective-permute-done.60 = bf16[384,384]{1,0:T(8,128)(2,1)} collective-permute-done((bf16[384,384]{1,0:T(8,128)(2,1)}, bf16[384,384]{1,0:T(8,128)(2,1)}, u32[]{:S(2)}, u32[]{:S(2)}) %collective-permute-start.60) | collective-permute-done | bytes 294944 | tf_op jit(solution)/shard_map/ppermute | solution.py:62
  193.7 14.8 %attend.3 = (f32[384,576]{1,0:T(8,128)}, f32[384,9]{1,0:T(8,128)}, f32[384,576]{1,0:T(8,128)}) custom-call(bf16[384,576]{1,0:T(8,128)(2,1)} %mlp.2.source_ref, bf16[384,576]{1,0:T(8,128)(2,1)} %get-tuple-element.61.query_ref, s32[384,1]{1,0:T(8,128)} %broadcast_in_dim.63.position_ref, s32[384,1]{1,0:T(8,128)} %reduce_sum.13.start_ref, ...), custom_call_target="tpu_custom_call" | custom-call | flops 1613758464 | bytes 16777216 | tf_op jit(solution)/shard_map/attend/pallas_call | solution.py:646
  208.5 17.9 %mlp_back.2 = (bf16[8,240,768]{2,1,0:T(8,128)(2,1)}, bf16[8,240,768]{2,1,0:T(8,128)(2,1)}, f32[1,576]{1,0:T(1,128)}, f32[384,576]{1,0:T(8,128)}, bf16[384,576]{1,0:T(8,128)(2,1)}) custom-call(s32[1]{0:T(128)} %bitcast.core_ref, bf16[384,576]{1,0:T(8,128)(2,1)} %pad_maximum_fusion.6.d_result_ref, f32[384,576]{1,0:T(8,128)} %get-tuple-element.64.middle_ref, ...), custom_call_target="tpu_custom_call" | custom-call | flops 6115295232 | bytes 16777216 | tf_op jit(solution)/shard_map/mlp_back/pallas_call | solution.py:646
  226.4 18.5 %attend_back.2 = (f32[384,576]{1,0:T(8,128)}, bf16[4,384,384]{2,1,0:T(8,128)(2,1)}) custom-call(bf16[384,576]{1,0:T(8,128)(2,1)} %get-tuple-element.69.d_out_ref, f32[384,576]{1,0:T(8,128)} %get-tuple-element.63.attended_ref, f32[384,9]{1,0:T(8,128)} %get-tuple-element.70.log_ref, bf16[384,576]{1,0:T(8,128)(2,1)} %get-tuple-element.61.query_ref, ...), custom_call_target="tpu_custom_call" | custom-call | flops 3397386240 | bytes 16777216 | tf_op jit(solution)/shard_map/attend_back/pallas_call | solution.py:646
  249.2 8.4 %mlp.3 = bf16[384,576]{1,0:T(8,128)(2,1)} custom-call(f32[384,576]{1,0:T(8,128)} %get-tuple-element.64.middle_ref, bf16[576,1536]{1,0:T(8,128)(2,1)} %copy-done.8, bf16[576,1536]{1,0:T(8,128)(2,1)} %copy-done.9, bf16[1536,576]{1,0:T(8,128)(2,1)} %copy-done.5, f32[1,576]{1,0:T(1,128)} %squeeze.170.gain_ref), custom_call_target="tpu_custom_call" | custom-call | flops 2038431744 | bytes 16777216 | tf_op jit(solution)/shard_map/mlp/pallas_call | solution.py:646
  259.1 7.1 %input.2 = (bf16[384,576]{1,0:T(8,128)(2,1)}, bf16[8,80,768]{2,1,0:T(8,128)(2,1)}, bf16[8,80,768]{2,1,0:T(8,128)(2,1)}) custom-call(s32[1]{0:T(128)} %bitcast.core_ref, bf16[384,576]{1,0:T(8,128)(2,1)} %mlp.2.source_ref, f32[384,576]{1,0:T(8,128)} %get-tuple-element.63.attended_ref, f32[384,576]{1,0:T(8,128)} %get-tuple-element.68.d_middle_ref, ...), custom_call_target="tpu_custom_call" | custom-call | flops 2038431744 | bytes 16777216 | tf_op jit(solution)/shard_map/input/pallas_call | solution.py:646
  266.1 17.9 %mlp_back.3 = (bf16[8,240,768]{2,1,0:T(8,128)(2,1)}, bf16[8,240,768]{2,1,0:T(8,128)(2,1)}, f32[1,576]{1,0:T(1,128)}, f32[384,576]{1,0:T(8,128)}, bf16[384,576]{1,0:T(8,128)(2,1)}) custom-call(s32[1]{0:T(128)} %bitcast.core_ref, bf16[384,576]{1,0:T(8,128)(2,1)} %get-tuple-element.74.d_result_ref, f32[384,576]{1,0:T(8,128)} %get-tuple-element.55.middle_ref, ...), custom_call_target="tpu_custom_call" | custom-call | flops 6115295232 | bytes 16777216 | tf_op jit(solution)/shard_map/mlp_back/pallas_call | solution.py:646
  284.0 18.4 %attend_back.3 = (f32[384,576]{1,0:T(8,128)}, bf16[4,384,384]{2,1,0:T(8,128)(2,1)}) custom-call(bf16[384,576]{1,0:T(8,128)(2,1)} %get-tuple-element.76.d_out_ref, f32[384,576]{1,0:T(8,128)} %get-tuple-element.54.attended_ref, f32[384,9]{1,0:T(8,128)} %get-tuple-element.77.log_ref, bf16[384,576]{1,0:T(8,128)(2,1)} %get-tuple-element.52.query_ref, ...), custom_call_target="tpu_custom_call" | custom-call | flops 3397386240 | bytes 16777216 | tf_op jit(solution)/shard_map/attend_back/pallas_call | solution.py:646
  309.7 5.7 %collective-permute-done.88 = bf16[192,576]{1,0:T(8,128)(2,1)S(1)} collective-permute-done((bf16[192,576]{1,0:T(8,128)(2,1)S(1)}, bf16[192,576]{1,0:T(8,128)(2,1)S(1)}, u32[]{:S(2)}, u32[]{:S(2)}) %collective-permute-start.88) | collective-permute-done | bytes 221216 | tf_op jit(solution)/shard_map/ppermute | solution.py:434
  318.5 3.7 collective-permute-start.85
  324.4 4.7 collective-permute-done.85.refs_2_
  329.8 7.2 %input.3 = (bf16[384,576]{1,0:T(8,128)(2,1)}, bf16[8,80,768]{2,1,0:T(8,128)(2,1)}, bf16[8,80,768]{2,1,0:T(8,128)(2,1)}) custom-call(s32[1]{0:T(128)} %bitcast.core_ref, bf16[384,576]{1,0:T(8,128)(2,1)} %pad_maximum_fusion.5.source_ref, f32[384,576]{1,0:T(8,128)} %get-tuple-element.54.attended_ref, f32[384,576]{1,0:T(8,128)} %get-tuple-element.75.d_middle_ref, ...), custom_call_target="tpu_custom_call" | custom-call | flops 2038431744 | bytes 16777216 | tf_op jit(solution)/shard_map/input/pallas_call | solution.py:646
  343.6 6.5 %collective-permute-done.86 = bf16[192,576]{1,0:T(8,128)(2,1)S(1)} collective-permute-done((bf16[192,576]{1,0:T(8,128)(2,1)S(1)}, bf16[192,576]{1,0:T(8,128)(2,1)S(1)}, u32[]{:S(2)}, u32[]{:S(2)}) %collective-permute-start.86) | collective-permute-done | bytes 221216 | tf_op jit(solution)/shard_map/ppermute | solution.py:434
  351.7 3.8 collective-permute-done.102
  357.6 13.8 %collective-permute-done.103 = bf16[2,80,384]{2,1,0:T(8,128)(2,1)S(1)} collective-permute-done((bf16[2,80,384]{2,1,0:T(8,128)(2,1)S(1)}, bf16[2,80,384]{2,1,0:T(8,128)(2,1)S(1)}, u32[]{:S(2)}, u32[]{:S(2)}) %collective-permute-start.103) | collective-permute-done | bytes 122912 | tf_op jit(solution)/shard_map/ppermute | solution.py:66
  389.7 4.2 collective-permute-done.95
  395.4 10.2 %collective-permute-done.93 = bf16[2,80,384]{2,1,0:T(8,128)(2,1)S(1)} collective-permute-done((bf16[2,80,384]{2,1,0:T(8,128)(2,1)S(1)}, bf16[2,80,384]{2,1,0:T(8,128)(2,1)S(1)}, u32[]{:S(2)}, u32[]{:S(2)}) %collective-permute-start.93) | collective-permute-done | bytes 122912 | tf_op jit(solution)/shard_map/ppermute | solution.py:58
  407.5 10.6 %collective-permute-done.117 = bf16[2,2,240,384]{3,2,0,1:T(8,128)(2,1)S(1)} collective-permute-done((bf16[2,2,240,384]{3,2,0,1:T(8,128)(2,1)S(1)}, bf16[2,2,240,384]{3,2,0,1:T(8,128)(2,1)S(1)}, u32[]{:S(2)}, u32[]{:S(2)}) %collective-permute-start.117) | collective-permute-done | bytes 737312 | tf_op jit(solution)/shard_map/ppermute | solution.py:66
  426.1 6.3 %collective-permute-start.104 = (bf16[80,384]{1,0:T(8,128)(2,1)S(1)}, bf16[80,384]{1,0:T(8,128)(2,1)S(1)}, u32[]{:S(2)}, u32[]{:S(2)}) collective-permute-start(bf16[80,384]{1,0:T(8,128)(2,1)S(1)} %copy-done.24), channel_id=1, source_target_pairs={{0,4},{4,8},{8,12},{12,0},{1,5},{5,9},{9,13},{13,1},{2,6},{6,10},{... | collective-permute-start | bytes 184328 | tf_op jit(solution)/shard_map/ppermute | solution.py:541
  435.5 9.2 %collective-permute-done.109 = bf16[2,2,240,384]{3,2,0,1:T(8,128)(2,1)S(1)} collective-permute-done((bf16[2,2,240,384]{3,2,0,1:T(8,128)(2,1)S(1)}, bf16[2,2,240,384]{3,2,0,1:T(8,128)(2,1)S(1)}, u32[]{:S(2)}, u32[]{:S(2)}) %collective-permute-start.109) | collective-permute-done | bytes 737312 | tf_op jit(solution)/shard_map/ppermute | solution.py:66
  445.0 7.5 %collective-permute-done.112 = bf16[2,240,384]{2,1,0:T(8,128)(2,1)S(1)} collective-permute-done((bf16[2,240,384]{2,1,0:T(8,128)(2,1)S(1)}, bf16[2,240,384]{2,1,0:T(8,128)(2,1)S(1)}, u32[]{:S(2)}, u32[]{:S(2)}) %collective-permute-start.112) | collective-permute-done | bytes 368672 | tf_op jit(solution)/shard_map/ppermute | solution.py:66
  465.7 10.4 %collective-permute-done.121 = bf16[240,384]{1,0:T(8,128)(2,1)S(1)} collective-permute-done((bf16[240,384]{1,0:T(8,128)(2,1)S(1)}, bf16[240,384]{1,0:T(8,128)(2,1)S(1)}, u32[]{:S(2)}, u32[]{:S(2)}) %collective-permute-start.121) | collective-permute-done | bytes 184352 | tf_op jit(solution)/shard_map/ppermute | solution.py:541
  476.1 4.3 collective-permute-done.115
  488.8 9.4 %collective-permute-start.125 = (bf16[3,36,768]{2,1,0:T(8,128)(2,1)S(1)}, bf16[3,36,768]{2,1,0:T(8,128)(2,1)S(1)}, u32[]{:S(2)}, u32[]{:S(2)}) collective-permute-start(bf16[3,36,768]{2,1,0:T(8,128)(2,1)S(1)} %fusion.28), channel_id=1, source_target_pairs={{0,1},{1,0},{2,3},{3,2},{4,5},{5,4},{6,7},{7,6},{8,9},{9,8},{10,11... | collective-permute-start | bytes 497672 | tf_op jit(solution)/shard_map/ppermute | solution.py:54
  (464 shorter events, 218.7 us)
Async XLA Ops:
  2.9 19.5 %collective-permute-start = (bf16[192,576]{1,0:T(8,128)(2,1)}, bf16[192,576]{1,0:T(8,128)(2,1)S(1)}, u32[]{:S(2)}, u32[]{:S(2)}) collective-permute-start(bf16[192,576]{1,0:T(8,128)(2,1)} %bitcast.1), channel_id=1, source_target_pairs={{0,0},{1,8},{2,2},{3,10},{4,4},{5,12},{6,6},{7,14},{8,5},{9,13},{1... | collective-permute-start | bytes 663560 | tf_op jit(solution)/shard_map/ppermute | solution.py:422
  15.5 16.5 %collective-permute-start.25 = (bf16[240,384]{1,0:T(8,128)(2,1)S(1)}, bf16[240,384]{1,0:T(8,128)(2,1)S(1)}, u32[]{:S(2)}, u32[]{:S(2)}) collective-permute-start(bf16[240,384]{1,0:T(8,128)(2,1)S(1)} %constant_dynamic-slice_fusion.11), channel_id=1, source_target_pairs={{0,16},{16,0},{1,17},{17,1},{2,18},{18,2},{3,19},{19,3},{4,20},{20... | collective-permute-start | bytes 552968 | tf_op jit(solution)/shard_map/ppermute | solution.py:66
  65.2 21.2 %collective-permute-start.63 = (bf16[192,576]{1,0:T(8,128)(2,1)S(1)}, bf16[192,576]{1,0:T(8,128)(2,1)S(1)}, u32[]{:S(2)}, u32[]{:S(2)}) collective-permute-start(bf16[192,576]{1,0:T(8,128)(2,1)S(1)} %bitcast.217), channel_id=1, source_target_pairs={{0,0},{1,8},{2,2},{3,10},{4,4},{5,12},{6,6},{7,14},{8,5},{9,13},{1... | collective-permute-start | bytes 663560 | tf_op jit(solution)/shard_map/ppermute | solution.py:422
  70.1 19.0 %collective-permute-start.64 = (bf16[192,576]{1,0:T(8,128)(2,1)S(1)}, bf16[192,576]{1,0:T(8,128)(2,1)S(1)}, u32[]{:S(2)}, u32[]{:S(2)}) collective-permute-start(bf16[192,576]{1,0:T(8,128)(2,1)S(1)} %bitcast.216), channel_id=1, source_target_pairs={{0,1},{1,9},{2,3},{3,11},{4,5},{5,13},{6,7},{7,15},{8,4},{9,12},{1... | collective-permute-start | bytes 663560 | tf_op jit(solution)/shard_map/ppermute | solution.py:422
  71.9 17.2 %collective-permute-start.34 = (bf16[240,384]{1,0:T(8,128)(2,1)S(1)}, bf16[240,384]{1,0:T(8,128)(2,1)}, u32[]{:S(2)}, u32[]{:S(2)}) collective-permute-start(bf16[240,384]{1,0:T(8,128)(2,1)S(1)} %get-tuple-element.170), channel_id=1, source_target_pairs={{0,12},{4,0},{8,4},{12,8},{1,13},{5,1},{9,5},{13,9},{2,14},{6,2},{... | collective-permute-start | bytes 552968 | tf_op jit(solution)/shard_map/ppermute | solution.py:484
  71.9 17.2 %collective-permute-start.73 = (bf16[240,384]{1,0:T(8,128)(2,1)S(1)}, bf16[240,384]{1,0:T(8,128)(2,1)S(1)}, u32[]{:S(2)}, u32[]{:S(2)}) collective-permute-start(bf16[240,384]{1,0:T(8,128)(2,1)S(1)} %get-tuple-element.169), channel_id=1, source_target_pairs={{0,12},{4,0},{8,4},{12,8},{1,13},{5,1},{9,5},{13,9},{2,14},{6,2},{... | collective-permute-start | bytes 552968 | tf_op jit(solution)/shard_map/ppermute | solution.py:484
  73.2 26.7 %collective-permute-start.27 = (bf16[2,240,384]{2,1,0:T(8,128)(2,1)S(1)}, bf16[2,240,384]{2,1,0:T(8,128)(2,1)S(1)}, u32[]{:S(2)}, u32[]{:S(2)}) collective-permute-start(bf16[2,240,384]{2,1,0:T(8,128)(2,1)S(1)} %pad_maximum_fusion.8.refs_0_), channel_id=1, source_target_pairs={{0,2},{1,3},{2,0},{3,1},{4,6},{5,7},{6,4},{7,5},{8,10},{9,11},{10,... | collective-permute-start | bytes 1105928 | tf_op jit(solution)/shard_map/ppermute | solution.py:58
  86.4 18.7 %collective-permute-start.28 = (bf16[2,240,384]{2,1,0:T(8,128)(2,1)S(1)}, bf16[2,240,384]{2,1,0:T(8,128)(2,1)S(1)}, u32[]{:S(2)}, u32[]{:S(2)}) collective-permute-start(bf16[2,240,384]{2,1,0:T(8,128)(2,1)S(1)} %pad_maximum_fusion.8.refs_0_), channel_id=1, source_target_pairs={{0,16},{16,0},{1,17},{17,1},{2,18},{18,2},{3,19},{19,3},{4,20},{20... | collective-permute-start | bytes 1105928 | tf_op jit(solution)/shard_map/ppermute | solution.py:66
  89.1 19.0 %collective-permute-start.30 = (bf16[2,240,384]{2,1,0:T(8,128)(2,1)S(1)}, bf16[2,240,384]{2,1,0:T(8,128)(2,1)S(1)}, u32[]{:S(2)}, u32[]{:S(2)}) collective-permute-start(bf16[2,240,384]{2,1,0:T(8,128)(2,1)S(1)} %pad_maximum_fusion.8.refs_0_), channel_id=1, source_target_pairs={{0,1},{1,0},{2,3},{3,2},{4,5},{5,4},{6,7},{7,6},{8,9},{9,8},{10,11... | collective-permute-start | bytes 1105928 | tf_op jit(solution)/shard_map/ppermute | solution.py:54
  99.9 18.8 %collective-permute-start.36 = (bf16[2,240,384]{2,1,0:T(8,128)(2,1)S(1)}, bf16[2,240,384]{2,1,0:T(8,128)(2,1)}, u32[]{:S(2)}, u32[]{:S(2)}) collective-permute-start(bf16[2,240,384]{2,1,0:T(8,128)(2,1)S(1)} %pad_maximum_fusion.9.refs_8_), channel_id=1, source_target_pairs={{0,2},{1,3},{2,0},{3,1},{4,6},{5,7},{6,4},{7,5},{8,10},{9,11},{10,... | collective-permute-start | bytes 1105928 | tf_op jit(solution)/shard_map/ppermute | solution.py:58
  134.1 27.4 %collective-permute-start.69 = (bf16[2,240,384]{2,1,0:T(8,128)(2,1)S(1)}, bf16[2,240,384]{2,1,0:T(8,128)(2,1)}, u32[]{:S(2)}, u32[]{:S(2)}) collective-permute-start(bf16[2,240,384]{2,1,0:T(8,128)(2,1)S(1)} %pad_maximum_fusion.10.refs_0_), channel_id=1, source_target_pairs={{0,1},{1,0},{2,3},{3,2},{4,5},{5,4},{6,7},{7,6},{8,9},{9,8},{10,11... | collective-permute-start | bytes 1105928 | tf_op jit(solution)/shard_map/ppermute | solution.py:54
  134.2 27.6 %collective-permute-start.75 = (bf16[2,240,384]{2,1,0:T(8,128)(2,1)S(1)}, bf16[2,240,384]{2,1,0:T(8,128)(2,1)}, u32[]{:S(2)}, u32[]{:S(2)}) collective-permute-start(bf16[2,240,384]{2,1,0:T(8,128)(2,1)S(1)} %pad_maximum_fusion.11.refs_8_), channel_id=1, source_target_pairs={{0,2},{1,3},{2,0},{3,1},{4,6},{5,7},{6,4},{7,5},{8,10},{9,11},{10,... | collective-permute-start | bytes 1105928 | tf_op jit(solution)/shard_map/ppermute | solution.py:58
  134.3 27.7 %collective-permute-start.76 = (bf16[2,240,384]{2,1,0:T(8,128)(2,1)S(1)}, bf16[2,240,384]{2,1,0:T(8,128)(2,1)}, u32[]{:S(2)}, u32[]{:S(2)}) collective-permute-start(bf16[2,240,384]{2,1,0:T(8,128)(2,1)S(1)} %pad_maximum_fusion.11.refs_8_), channel_id=1, source_target_pairs={{0,16},{16,0},{1,17},{17,1},{2,18},{18,2},{3,19},{19,3},{4,20},{20... | collective-permute-start | bytes 1105928 | tf_op jit(solution)/shard_map/ppermute | solution.py:66
  135.6 27.8 %collective-permute-start.78 = (bf16[2,240,384]{2,1,0:T(8,128)(2,1)S(1)}, bf16[2,240,384]{2,1,0:T(8,128)(2,1)}, u32[]{:S(2)}, u32[]{:S(2)}) collective-permute-start(bf16[2,240,384]{2,1,0:T(8,128)(2,1)S(1)} %pad_maximum_fusion.11.refs_8_), channel_id=1, source_target_pairs={{0,1},{1,0},{2,3},{3,2},{4,5},{5,4},{6,7},{7,6},{8,9},{9,8},{10,11... | collective-permute-start | bytes 1105928 | tf_op jit(solution)/shard_map/ppermute | solution.py:54
  140.3 35.8 %collective-permute-start.68 = (bf16[2,240,384]{2,1,0:T(8,128)(2,1)S(1)}, bf16[2,240,384]{2,1,0:T(8,128)(2,1)}, u32[]{:S(2)}, u32[]{:S(2)}) collective-permute-start(bf16[2,240,384]{2,1,0:T(8,128)(2,1)S(1)} %collective-permute-done.66.refs_1_), channel_id=1, source_target_pairs={{0,16},{16,0},{1,17},{17,1},{2,18},{18,2},{3,19},{19,3},{4,20},{20... | collective-permute-start | bytes 1105928 | tf_op jit(solution)/shard_map/ppermute | solution.py:66
  176.9 16.8 %collective-permute-start.61 = (bf16[384,384]{1,0:T(8,128)(2,1)}, bf16[384,384]{1,0:T(8,128)(2,1)}, u32[]{:S(2)}, u32[]{:S(2)}) collective-permute-start(bf16[384,384]{1,0:T(8,128)(2,1)} %get-tuple-element.62), channel_id=1, source_target_pairs={{0,1},{1,0},{2,3},{3,2},{4,5},{5,4},{6,7},{7,6},{8,9},{9,8},{10,11... | collective-permute-start | bytes 884744 | tf_op jit(solution)/shard_map/ppermute | solution.py:54
  307.0 76.5 %collective-permute-start.116 = (bf16[8,240,768]{2,1,0:T(8,128)(2,1)}, bf16[8,240,768]{2,1,0:T(8,128)(2,1)}, u32[]{:S(2)}, u32[]{:S(2)}) collective-permute-start(bf16[8,240,768]{2,1,0:T(8,128)(2,1)} %get-tuple-element.89), channel_id=1, source_target_pairs={{0,1},{1,0},{2,3},{3,2},{4,5},{5,4},{6,7},{7,6},{8,9},{9,8},{10,11... | collective-permute-start | bytes 8847368 | tf_op jit(solution)/shard_map/ppermute | solution.py:54
  318.3 22.5 %collective-permute-start.99 = (bf16[8,80,768]{2,1,0:T(8,128)(2,1)}, bf16[8,80,768]{2,1,0:T(8,128)(2,1)S(1)}, u32[]{:S(2)}, u32[]{:S(2)}) collective-permute-start(bf16[8,80,768]{2,1,0:T(8,128)(2,1)} %get-tuple-element.85), channel_id=1, source_target_pairs={{0,1},{1,0},{2,3},{3,2},{4,5},{5,4},{6,7},{7,6},{8,9},{9,8},{10,11... | collective-permute-start | bytes 2949128 | tf_op jit(solution)/shard_map/ppermute | solution.py:54
  322.9 96.4 %collective-permute-start.108 = (bf16[8,240,768]{2,1,0:T(8,128)(2,1)}, bf16[8,240,768]{2,1,0:T(8,128)(2,1)}, u32[]{:S(2)}, u32[]{:S(2)}) collective-permute-start(bf16[8,240,768]{2,1,0:T(8,128)(2,1)} %get-tuple-element.87), channel_id=1, source_target_pairs={{0,1},{1,0},{2,3},{3,2},{4,5},{5,4},{6,7},{7,6},{8,9},{9,8},{10,11... | collective-permute-start | bytes 8847368 | tf_op jit(solution)/shard_map/ppermute | solution.py:54
  340.8 40.6 %collective-permute-start.91 = (bf16[8,80,768]{2,1,0:T(8,128)(2,1)}, bf16[8,80,768]{2,1,0:T(8,128)(2,1)}, u32[]{:S(2)}, u32[]{:S(2)}) collective-permute-start(bf16[8,80,768]{2,1,0:T(8,128)(2,1)} %get-tuple-element.83), channel_id=1, source_target_pairs={{0,1},{1,0},{2,3},{3,2},{4,5},{5,4},{6,7},{7,6},{8,9},{9,8},{10,11... | collective-permute-start | bytes 2949128 | tf_op jit(solution)/shard_map/ppermute | solution.py:54
  355.5 20.4 %collective-permute-start.90 = (bf16[384,576]{1,0:T(8,128)(2,1)S(1)}, bf16[384,576]{1,0:T(8,128)(2,1)S(1)}, u32[]{:S(2)}, u32[]{:S(2)}) collective-permute-start(bf16[384,576]{1,0:T(8,128)(2,1)S(1)} %broadcast_select_fusion), channel_id=1, source_target_pairs={{0,16},{16,0},{1,17},{17,1},{2,18},{18,2},{3,19},{19,3},{4,20},{20... | collective-permute-start | bytes 1327112 | tf_op jit(solution)/shard_map/ppermute | solution.py:66
  375.9 77.1 %collective-permute-start.106 = (bf16[80,384]{1,0:T(8,128)(2,1)}, bf16[80,384]{1,0:T(8,128)(2,1)S(1)}, u32[]{:S(2)}, u32[]{:S(2)}) collective-permute-start(bf16[80,384]{1,0:T(8,128)(2,1)} %get-tuple-element.191), channel_id=1, source_target_pairs={{0,12},{4,0},{8,4},{12,8},{1,13},{5,1},{9,5},{13,9},{2,14},{6,2},{... | collective-permute-start | bytes 184328 | tf_op jit(solution)/shard_map/ppermute | solution.py:541
  375.9 80.6 %collective-permute-start.105 = (bf16[80,384]{1,0:T(8,128)(2,1)}, bf16[80,384]{1,0:T(8,128)(2,1)}, u32[]{:S(2)}, u32[]{:S(2)}) collective-permute-start(bf16[80,384]{1,0:T(8,128)(2,1)} %get-tuple-element.192), channel_id=1, source_target_pairs={{0,8},{4,12},{8,0},{12,4},{1,9},{5,13},{9,1},{13,5},{2,10},{6,14},... | collective-permute-start | bytes 184328 | tf_op jit(solution)/shard_map/ppermute | solution.py:541
  388.1 18.9 %collective-permute-start.119 = (bf16[2,240,768]{2,1,0:T(8,128)(2,1)S(1)}, bf16[2,240,768]{2,1,0:T(8,128)(2,1)S(1)}, u32[]{:S(2)}, u32[]{:S(2)}) collective-permute-start(bf16[2,240,768]{2,1,0:T(8,128)(2,1)S(1)} %fusion.3), channel_id=1, source_target_pairs={{0,2},{1,3},{2,0},{3,1},{4,6},{5,7},{6,4},{7,5},{8,10},{9,11},{10,... | collective-permute-start | bytes 2211848 | tf_op jit(solution)/shard_map/ppermute | solution.py:58
  407.3 18.8 %collective-permute-start.120 = (bf16[2,240,384]{2,1,0:T(8,128)(2,1)S(1)}, bf16[2,240,384]{2,1,0:T(8,128)(2,1)S(1)}, u32[]{:S(2)}, u32[]{:S(2)}) collective-permute-start(bf16[2,240,384]{2,1,0:T(8,128)(2,1)S(1)} %dynamic-slice_convert_fusion.2), channel_id=1, source_target_pairs={{0,16},{16,0},{1,17},{17,1},{2,18},{18,2},{3,19},{19,3},{4,20},{20... | collective-permute-start | bytes 1105928 | tf_op jit(solution)/shard_map/ppermute | solution.py:66
  426.1 30.8 %collective-permute-start.104 = (bf16[80,384]{1,0:T(8,128)(2,1)S(1)}, bf16[80,384]{1,0:T(8,128)(2,1)S(1)}, u32[]{:S(2)}, u32[]{:S(2)}) collective-permute-start(bf16[80,384]{1,0:T(8,128)(2,1)S(1)} %copy-done.24), channel_id=1, source_target_pairs={{0,4},{4,8},{8,12},{12,0},{1,5},{5,9},{9,13},{13,1},{2,6},{6,10},{... | collective-permute-start | bytes 184328 | tf_op jit(solution)/shard_map/ppermute | solution.py:541
  434.1 18.5 %collective-permute-start.112 = (bf16[2,240,384]{2,1,0:T(8,128)(2,1)S(1)}, bf16[2,240,384]{2,1,0:T(8,128)(2,1)S(1)}, u32[]{:S(2)}, u32[]{:S(2)}) collective-permute-start(bf16[2,240,384]{2,1,0:T(8,128)(2,1)S(1)} %dynamic-slice_convert_fusion.4), channel_id=1, source_target_pairs={{0,16},{16,0},{1,17},{17,1},{2,18},{18,2},{3,19},{19,3},{4,20},{20... | collective-permute-start | bytes 1105928 | tf_op jit(solution)/shard_map/ppermute | solution.py:66
  459.0 17.2 %collective-permute-start.121 = (bf16[240,384]{1,0:T(8,128)(2,1)S(1)}, bf16[240,384]{1,0:T(8,128)(2,1)S(1)}, u32[]{:S(2)}, u32[]{:S(2)}) collective-permute-start(bf16[240,384]{1,0:T(8,128)(2,1)S(1)} %get-tuple-element.163), channel_id=1, source_target_pairs={{0,4},{4,8},{8,12},{12,0},{1,5},{5,9},{9,13},{13,1},{2,6},{6,10},{... | collective-permute-start | bytes 552968 | tf_op jit(solution)/shard_map/ppermute | solution.py:541
  459.8 20.6 %collective-permute-start.115 = (bf16[240,384]{1,0:T(8,128)(2,1)S(1)}, bf16[240,384]{1,0:T(8,128)(2,1)S(1)}, u32[]{:S(2)}, u32[]{:S(2)}) collective-permute-start(bf16[240,384]{1,0:T(8,128)(2,1)S(1)} %get-tuple-element.167), channel_id=1, source_target_pairs={{0,12},{4,0},{8,4},{12,8},{1,13},{5,1},{9,5},{13,9},{2,14},{6,2},{... | collective-permute-start | bytes 552968 | tf_op jit(solution)/shard_map/ppermute | solution.py:541
  460.4 20.0 %collective-permute-start.114 = (bf16[240,384]{1,0:T(8,128)(2,1)S(1)}, bf16[240,384]{1,0:T(8,128)(2,1)S(1)}, u32[]{:S(2)}, u32[]{:S(2)}) collective-permute-start(bf16[240,384]{1,0:T(8,128)(2,1)S(1)} %get-tuple-element.168), channel_id=1, source_target_pairs={{0,8},{4,12},{8,0},{12,4},{1,9},{5,13},{9,1},{13,5},{2,10},{6,14},... | collective-permute-start | bytes 552968 | tf_op jit(solution)/shard_map/ppermute | solution.py:541
  461.3 22.2 %collective-permute-start.113 = (bf16[240,384]{1,0:T(8,128)(2,1)S(1)}, bf16[240,384]{1,0:T(8,128)(2,1)S(1)}, u32[]{:S(2)}, u32[]{:S(2)}) collective-permute-start(bf16[240,384]{1,0:T(8,128)(2,1)S(1)} %get-tuple-element.166), channel_id=1, source_target_pairs={{0,4},{4,8},{8,12},{12,0},{1,5},{5,9},{9,13},{13,1},{2,6},{6,10},{... | collective-permute-start | bytes 552968 | tf_op jit(solution)/shard_map/ppermute | solution.py:541
  464.6 20.3 %collective-permute-start.107 = (bf16[80,384]{1,0:T(8,128)(2,1)S(1)}, bf16[80,384]{1,0:T(8,128)(2,1)S(1)}, u32[]{:S(2)}, u32[]{:S(2)}) collective-permute-start(bf16[80,384]{1,0:T(8,128)(2,1)S(1)} %get-tuple-element.134), channel_id=1, source_target_pairs={{0,16},{16,0},{1,17},{17,1},{2,18},{18,2},{3,19},{19,3},{4,20},{20... | collective-permute-start | bytes 184328 | tf_op jit(solution)/shard_map/ppermute | solution.py:66
  (130 other events, 993.1 us)

commit v2 on v1

--- a/solution.py
+++ b/solution.py
@@ -64,6 +64,14 @@
 
 def swap_x(value):
     return lax.ppermute(value, "section", flip(2, 1))
+
+
+def swap_corner(value):
+    return lax.ppermute(value, ("section", "fsdp"), flip(8, 6))
+
+
+def tie(value, *others):
+    return lax.optimization_barrier((value, others))[0]
 
 
 def spread_pairs(odd):
@@ -269,11 +277,11 @@
     d_out_ref, attended_ref, log_ref, query_ref, position_ref, start_ref, key_position_ref, *refs,
 ):
     piece_refs, refs = refs[:pieces], refs[pieces:]
-    d_query_ref, d_pairs_ref = refs[:2]
+    d_query_ref, d_pairs_refs = refs[0], refs[1:-9]
     (
         query_scr, key_scr, value_scr, d_out_scr, log_scr, delta_scr, d_query_scr,
         d_key_scr, d_value_scr,
-    ) = refs[2:]
+    ) = refs[-9:]
     d_out = d_out_ref[...]
     split_heads(piece_refs, key_scr, value_scr, parts)
     for head in range(HQ):
@@ -306,14 +314,15 @@
 
     each_job(jobs, tile, visit)
     d_query_ref[...] = jnp.concatenate([d_query_scr[head] for head in range(HQ)], axis=1)
-    count, rows = d_pairs_ref.shape[0], d_pairs_ref.shape[1] // parts
+    near, whole = d_pairs_refs[0].shape[:2]
+    count, rows = near * len(d_pairs_refs), whole // parts
     for first in range(0, count * parts, parts):
         at = slice(first * rows, (first + parts) * rows)
         grads = [scr[group, :, at].T for scr in (d_key_scr, d_value_scr) for group in range(KV)]
         grads = jnp.concatenate(grads, axis=1).astype(BF)
         for index in range(parts):
             part, piece = divmod(first + index, count)
-            d_pairs_ref[piece, part * rows : (part + 1) * rows, :] = grads[
+            d_pairs_refs[piece // near][piece % near, part * rows : (part + 1) * rows, :] = grads[
                 index * rows : (index + 1) * rows
             ]
 
@@ -356,47 +365,72 @@
         store(half ^ core, packed_refs, Ellipsis, jnp.stack(blocks).astype(BF))
 
 
-def join_rows(parts, first):
-    return jnp.concatenate([part.astype(F32)[first : first + 72] for part in parts]).astype(BF)
-
-
 def assemble_kernel(mixed, index_ref, *refs):
-    pieces, outs = refs[:16], refs[16:]
+    pieces, outs = refs[:8], refs[8:]
     x, z, y, core = (index_ref[i] for i in range(4))
+
+    def ordered(parts):
+        rows = [
+            [jnp.where(y == 0, a, b), jnp.where(y == 0, b, a)] for a, b in parts
+        ]
+        return [
+            part
+            for a, b in zip(*rows)
+            for part in (jnp.where(core == 0, a, b), jnp.where(core == 0, b, a))
+        ]
+
+    gains = jnp.zeros((8, D), F32)
+    owner = lax.broadcasted_iota(I32, (8, D), 1) // 144
     for place, steps in enumerate((0, 1, 3, 2)):
         row = (z + 4 - steps) % 4
         at = pl.ds(pl.multiple_of(row * 144, 144), 144)
-        for cross in (0, 1):
-            first = 8 * (place // 2) + 4 * cross
-            here, there = (
-                [pieces[first + 2 * dx + dy][place % 2] for dy in (0, 1)] for dx in (0, 1)
+        for dx in (0, 1):
+            columns = pl.ds(pl.multiple_of((x ^ dx) * HALF, HALF), HALF)
+            parts = ordered(
+                [
+                    [pieces[4 * cross + 2 * dx + dy][place].astype(F32) for dy in (0, 1)]
+                    for cross in (0, 1)
+                ]
             )
-            here, there = (
-                [jnp.where(y == 0, *part), jnp.where(y == 0, *part[::-1])] for part in (here, there)
-            )
-            sides = [
-                jnp.concatenate(
-                    [jnp.where(x == 0, a, b), jnp.where(x == 0, b, a)], axis=1
-                )
-                for a, b in zip(here, there)
-            ]
-            side = core ^ cross
-            columns = pl.ds(pl.multiple_of(side * HALF, HALF), HALF)
+            outs[0][at, columns] = jnp.concatenate([part[:36] for part in parts]).astype(BF)
             if mixed:
-                outs[0][at, columns] = join_rows(sides, 0)
-                for beside, part in enumerate(sides):
-                    outs[1][4 * row + 2 * beside + side] = part[64:80, :128].astype(F32)
+                block = jnp.concatenate([part[32:40, :36] for part in parts], axis=1)
+                here = (owner == row) & (x == dx)
+                gains = jnp.where(here, jnp.concatenate([block] * 4, axis=1), gains)
             else:
-                outs[0][at, columns] = join_rows(sides, 0)
-                outs[1][at, columns] = join_rows(sides, 72)
-                for beside, part in enumerate(sides):
-                    rows = pl.ds(pl.multiple_of((4 * row + 2 * beside + side) * 96, 96), 96)
-                    outs[2][rows, :] = part[144:240, :D]
+                outs[1][at, columns] = jnp.concatenate([part[36:72] for part in parts]).astype(BF)
+                for index, part in enumerate(parts):
+                    first = (4 * row + index) * 96 + (x ^ dx) * 48
+                    rows = pl.ds(pl.multiple_of(first, 16), 48)
+                    outs[2][rows, :] = part[72:120, :D].astype(BF)
+    if mixed:
+        outs[1][...] = gains[4:5]
+        outs[2][...] = gains[5:6]
+
+
+def split_square_kernel(index_ref, keep_ref, received_ref, *out_refs):
+    x, y = index_ref[0], index_ref[1]
+    half = keep_ref.shape[2] // 2
+    for index, ref in enumerate(out_refs):
+        dx, dy = divmod(index, 2)
+        lanes = pl.ds(pl.multiple_of((x ^ dx) * half, half), half)
+        for z in range(4):
+            block = 2 * z + (y ^ dy)
+            held = keep_ref[block, :, lanes].astype(F32) + received_ref[block, :, lanes].astype(F32)
+            ref[z] = held.astype(ref.dtype)
+
+
+def split_column_kernel(index_ref, *refs):
+    parts, out_refs = refs[:4], refs[4:]
+    for steps, ref in enumerate(out_refs):
+        row = (index_ref[2] + steps) % 4
+        ref[...] = sum(part[row].astype(F32) for part in parts).astype(ref.dtype)
 
 
 class Fast:
     parts = 2
     tile = None
+    limit = staticmethod(lambda mib: mib)
 
     def __init__(self):
         self.section = lax.axis_index("section")
@@ -449,69 +483,52 @@
         return [part[None] for part in (pairs, along, swap_core(pairs), swap_core(along))]
 
     def reduce_pairs(self, grads):
-        received = swap_core(grads[2:])
-        along = grads[1].astype(F32) + received[1].astype(F32)
-        return [grads[0], received[0], swap_zpair(along.astype(BF))]
-
-
-    def gather(self, wide, down, gains):
-        count, rows, width = wide.shape
-        mine = lax.dynamic_slice_in_dim(wide, self.core * HALF, HALF, 2)
-        other = swap_core(lax.dynamic_slice_in_dim(wide, (1 - self.core) * HALF, HALF, 2))
-        joined = jnp.concatenate(
-            [jnp.where(self.core == 0, mine, other), jnp.where(self.core == 0, other, mine)], axis=1
-        )
-        gains = jnp.pad(gains, ((0, 6), (0, HALF - rows)))
-        mixed = jnp.concatenate([joined[0], gains], axis=0)
-        deep = jnp.concatenate(
-            [joined[1], joined[2], jnp.pad(down, ((0, 0), (0, HALF - D)))], axis=0
-        )
-        index = jnp.stack([self.section, self.z, self.y, self.core])
-        packs = []
-        for part in (mixed, deep):
-            quarter = HALF // 2
-            mine, other = (
-                lax.dynamic_slice_in_dim(part, x * quarter, quarter, 1)
-                for x in (self.section, 1 - self.section)
-            )
-            packs.append((mine, swap_x(other)))
-        layers = []
-        for layer in (0, 1):
-            weights = []
-            for name, (own, theirs) in zip(("mixed", "deep"), packs):
-                start = jnp.where(self.section == layer, own, theirs)
-                above = lax.ppermute(start, "ctx", ring(4, 1))
-                below = lax.ppermute(start, "ctx", ring(4, 3))
-                across = lax.ppermute(above, "ctx", ring(4, 1))
-                pieces = []
-                first = jnp.stack([start, above])
-                first_y = swap_y(first)
-                square = [first, first_y, swap_x(first), swap_x(first_y)]
-                pieces += square + [swap_core(part) for part in square]
-                second = jnp.stack([below, across])
-                second_x = swap_x(second)
-                square = [second, swap_y(second), second_x, swap_y(second_x)]
-                pieces += square + [swap_core(part) for part in square]
-                weights.append(self.assemble(name == "mixed", index, pieces))
-            (mixed, gains), (gate, up, down) = weights
-            gains = gains[:, 8:10, :rows].swapaxes(0, 1).reshape(2, 1, D)
-            layers.append((mixed, gate, up, down, gains[0], gains[1]))
-        return layers
-
-    def assemble(self, mixed, index, pieces):
+        near, far = grads
+        received = swap_core(far)
+        along = near[1].astype(F32) + received[1].astype(F32)
+        return [near[0], received[0], swap_zpair(along.astype(BF))]
+
+
+    def pack(self, wide, down, gains):
+        rows = wide.shape[1]
+        gains = jnp.pad(gains, ((0, 2), (0, MIXED - rows)))
+        mixed = jnp.concatenate([wide[0], gains], axis=0)
+        half = down.shape[0] // 2
+        down = jnp.pad(jnp.stack([down[:half], down[half:]], axis=1), ((0, 0), (0, 0), (0, HALF - D)))
+        deep = jnp.concatenate([wide[1], wide[2], down.reshape(half, MIXED)], axis=0)
+        return [
+            (self.lanes(part, self.section), swap_x(self.lanes(part, 1 - self.section)))
+            for part in (mixed, deep)
+        ]
+
+    def column(self, pack, layer, *after):
+        start = tie(jnp.where(self.section == layer, *pack), *after)
+        above = lax.ppermute(start, "ctx", ring(4, 1))
+        below = lax.ppermute(start, "ctx", ring(4, 3))
+        return start, above, below, lax.ppermute(start, "ctx", ring(4, 2))
+
+    def square(self, column, *after):
+        column = jnp.stack(tie(column, *after))
+        return column, swap_y(column), swap_x(column), swap_corner(column)
+
+    def assemble(self, square, rows, *after):
+        square = tie(square, *after)
+        pieces = square + tuple(swap_core(part) for part in square)
+        mixed = square[0].shape[1] < 2 * rows
         if mixed:
-            outs = (struct((D, MIXED), BF), struct((16, 16, 128), F32))
+            outs = (struct((D, MIXED), BF), struct((1, D), F32), struct((1, D), F32))
         else:
-            rows = 16 * (pieces[0].shape[1] - 144)
-            outs = (struct((D, MIXED), BF), struct((D, MIXED), BF), struct((rows, D), BF))
-        return pl.pallas_call(
+            depth = 32 * (square[0].shape[1] - 2 * rows)
+            outs = (struct((D, MIXED), BF), struct((D, MIXED), BF), struct((depth, D), BF))
+        weights = pl.pallas_call(
             functools.partial(assemble_kernel, mixed),
             out_shape=outs,
             in_specs=[pl.BlockSpec(memory_space=pltpu.SMEM)]
-            + [pl.BlockSpec(memory_space=pltpu.VMEM)] * 16,
-            compiler_params=pltpu.CompilerParams(vmem_limit_bytes=32 * MIB),
+            + [pl.BlockSpec(memory_space=pltpu.VMEM)] * 8,
+            compiler_params=pltpu.CompilerParams(vmem_limit_bytes=24 * MIB),
             name="assemble",
-        )(index, *pieces)
+        )(jnp.stack([self.section, self.z, self.y, self.core]), *pieces)
+        return weights
 
     def lanes(self, value, x):
         half = value.shape[-1] // 2
@@ -520,29 +537,45 @@
     def row(self, value, y):
         return lax.dynamic_index_in_dim(value, y, 1, keepdims=False)
 
-    def reduce_part(self, keep, send):
-        held = keep.astype(F32) + swap_core(send).astype(F32)
-        held = held.reshape((4, 2) + held.shape[1:])
-        x, y = self.section, self.y
-        first, second = held[:2], held[2:]
-        first_sent = self.lanes(first, 1 - x).astype(BF)
-        second_sent = self.row(second, 1 - y).astype(BF)
-        first = self.lanes(first, x) + swap_x(first_sent).astype(F32)
-        second = self.row(second, y) + swap_y(second_sent).astype(F32)
-        first_sent = self.row(first, 1 - y).astype(BF)
-        second_sent = self.lanes(second, 1 - x).astype(BF)
-        first = self.row(first, y) + swap_y(first_sent).astype(F32)
-        second = self.lanes(second, x) + swap_x(second_sent).astype(F32)
-        held = jnp.concatenate([first, second])
-        low = held.astype(BF)
-        total = lax.dynamic_index_in_dim(held, self.z, 0, keepdims=False)
-        for steps in (1, 2, 3):
-            part = lax.dynamic_index_in_dim(low, (self.z + steps) % 4, 0, keepdims=False)
-            total = total + lax.ppermute(part, "ctx", ring(4, steps)).astype(F32)
-        return total
-
-    def reduce(self, deep, mixed):
-        return self.reduce_part(*mixed), self.reduce_part(*deep)
+    def reduce_core(self, keep, send):
+        return keep, swap_core(send)
+
+    def index(self):
+        return jnp.stack([self.section, self.y, self.z])
+
+    def split_square(self, keep, received):
+        shape = (4,) + keep.shape[1:2] + (keep.shape[2] // 2,)
+        return vmem_call(
+            split_square_kernel,
+            [struct(shape, F32)] + [struct(shape, BF)] * 3,
+            (self.index(), keep, received),
+            scalars=1,
+            limit=20,
+            name="split_square",
+        )
+
+    def move_square(self, parts):
+        swaps = (swap_y, swap_x, swap_corner)
+        return [parts[0]] + [swap(part) for swap, part in zip(swaps, parts[1:])]
+
+    def split_column(self, parts):
+        shape = parts[0].shape[1:]
+        return vmem_call(
+            split_column_kernel,
+            [struct(shape, F32)] + [struct(shape, BF)] * 3,
+            (self.index(), *parts),
+            scalars=1,
+            limit=16,
+            name="split_column",
+        )
+
+    def move_column(self, parts):
+        return [parts[0]] + [
+            lax.ppermute(part, "ctx", ring(4, steps)) for steps, part in zip((1, 2, 3), parts[1:])
+        ]
+
+    def total(self, parts):
+        return sum(part.astype(F32) for part in parts)
 
     def finish(self, first, second, rows):
         joined = []
@@ -573,6 +606,7 @@
 class Plain:
     parts = 1
     tile = 16
+    limit = staticmethod(lambda mib: 60)
 
     def __init__(self):
         self.section = lax.axis_index("section")
@@ -601,21 +635,49 @@
         return [lax.all_gather(pairs, "ctx", axis=0)]
 
     def reduce_pairs(self, grads):
-        return [lax.psum_scatter(grads, "ctx", scatter_dimension=0)]
-
-    def gather(self, wide, down, gains):
-        own = (wide, down, gains)
-        theirs = tuple(swap_x(part) for part in own)
-        layers = []
-        for layer in (0, 1):
-            w, d, g = (jnp.where(self.section == layer, a, b) for a, b in zip(own, theirs))
-            w = lax.all_gather(w, ("ctx", "fsdp"), axis=1, tiled=True)
-            d = lax.all_gather(d, ("ctx", "fsdp"), axis=0, tiled=True)
-            g = lax.all_gather(g, ("ctx", "fsdp"), axis=1, tiled=True).astype(F32)
-            layers.append((w[0], w[1], w[2], d, g[0][None], g[1][None]))
-        return layers
-
-    def reduce(self, deep, mixed):
+        return [lax.psum_scatter(grads[0], "ctx", scatter_dimension=0)]
+
+    def pack(self, wide, down, gains):
+        packs = []
+        for own in ((wide[0], gains), (wide[1], wide[2], down)):
+            packs.append((own, tuple(swap_x(part) for part in own)))
+        return packs
+
+    def column(self, pack, layer, *after):
+        return [jnp.where(self.section == layer, a, b) for a, b in zip(*pack)]
+
+    def square(self, column, *after):
+        return column
+
+    def assemble(self, square, rows, *after):
+        axes = ("ctx", "fsdp")
+        weights = [
+            lax.all_gather(part, axes, axis=int(part.shape[0] == 2), tiled=True) for part in square
+        ]
+        if len(weights) == 2:
+            gains = weights[1].astype(F32)
+            return weights[0], gains[:1], gains[1:]
+        return weights
+
+    def reduce_core(self, keep, send):
+        return keep, send
+
+    def split_square(self, keep, send):
+        return [keep, send]
+
+    def move_square(self, parts):
+        return parts
+
+    def split_column(self, parts):
+        return parts
+
+    def move_column(self, parts):
+        return parts
+
+    def total(self, parts):
+        return parts
+
+    def reduce(self, mixed, deep):
         def columns(pair, first):
             return jnp.concatenate([part[:, first : first + 72] for part in pair], axis=2)
 
@@ -634,13 +696,14 @@
         )
 
     def finish(self, first, second, rows):
+        first, second = self.reduce(*first), self.reduce(*second)
         return tuple(
             jnp.where(self.section == 0, a, b) + swap_x(jnp.where(self.section == 0, b, a))
             for a, b in zip(first, second)
         )
 
 
-def vmem_call(kernel, out_shape, args, scratch=(), scalars=0, limit=56, flops=0, name=None):
+def vmem_call(kernel, out_shape, args, scratch=(), scalars=0, limit=16, name=None):
     specs = [pl.BlockSpec(memory_space=pltpu.SMEM)] * scalars
     specs += [pl.BlockSpec(memory_space=pltpu.VMEM)] * (len(args) - scalars)
     return pl.pallas_call(
@@ -649,28 +712,27 @@
         in_specs=specs,
         scratch_shapes=list(scratch),
         compiler_params=pltpu.CompilerParams(vmem_limit_bytes=limit * MIB),
-        cost_estimate=pl.CostEstimate(flops=flops, bytes_accessed=16 * MIB, transcendentals=0),
         name=name,
     )(*args)
 
 
-def layer_forward(net, source, weights, place):
-    mixed, gate, up, down, g_attn, g_mlp = weights
-    positions, starts, cosine, sine, key_positions = place
+def project(net, source, mixed, g_attn, place):
     rows = source.shape[0]
     queries, pairs = vmem_call(
         project_kernel,
         (struct((rows, QW), BF), struct((rows, 2 * KW), BF)),
-        (source, mixed, g_attn, cosine, sine),
-        flops=2 * rows * D * MIXED,
+        (source, mixed, g_attn, place[2], place[3]),
+        limit=12,
         name="project",
     )
-    pieces = net.share_pairs(pairs)
-    keys = key_positions.shape[1]
-    attended, log_total, middle = vmem_call(
-        functools.partial(
-            attend_kernel, net.jobs(rows, keys), net.tile, net.parts, len(pieces)
-        ),
+    return queries, net.share_pairs(pairs)
+
+
+def attend_forward(net, source, queries, pieces, mixed, place):
+    positions, starts, _, _, key_positions = place
+    rows, keys = source.shape[0], key_positions.shape[1]
+    return vmem_call(
+        functools.partial(attend_kernel, net.jobs(rows, keys), net.tile, net.parts, len(pieces)),
         (struct((rows, QW), F32), struct((rows, HQ), F32), struct((rows, D), F32)),
         (source, queries, positions, starts, key_positions, mixed, *pieces),
         [
@@ -680,28 +742,27 @@
             pltpu.VMEM((HQ, rows, HD), F32),
             pltpu.VMEM((HQ, rows, 1), F32),
         ],
-        flops=2 * rows * D * QW + 4 * rows * keys * QW,
+        limit=net.limit(28),
         name="attend",
     )
-    result = vmem_call(
+
+
+def mlp_forward(middle, gate, up, down, g_mlp):
+    rows = middle.shape[0]
+    return vmem_call(
         mlp_kernel,
         struct((rows, D), BF),
         (middle, gate, up, down, g_mlp),
         [pltpu.VMEM((rows, D), BF), pltpu.VMEM((rows, D), F32)],
-        flops=6 * rows * D * gate.shape[1],
+        limit=16,
         name="mlp",
     )
-    return result, (source, queries, pieces, attended, log_total, middle)
-
-
-def layer_backward(net, d_result, kept, weights, place):
-    mixed, gate, up, down, g_attn, g_mlp = weights
-    source, queries, pieces, attended, log_total, middle = kept
-    positions, starts, cosine, sine, key_positions = place
-    rows, keys = source.shape[0], key_positions.shape[1]
-    core = net.core.reshape(1)
+
+
+def mlp_backward(net, d_result, middle, mixed, gate, up, down, g_mlp):
+    rows = middle.shape[0]
     deep_shape = struct((8, 144 + down.shape[0] // 16, HALF), BF)
-    keep, send, gain_grad, d_middle, d_attended = vmem_call(
+    return vmem_call(
         mlp_back_kernel,
         (
             deep_shape,
@@ -710,17 +771,23 @@
             struct((rows, D), F32),
             struct((rows, QW), BF),
         ),
-        (core, d_result, middle, mixed, gate, up, down, g_mlp),
+        (net.core.reshape(1), d_result, middle, mixed, gate, up, down, g_mlp),
         [pltpu.VMEM((rows, D), BF), pltpu.VMEM((rows, D), F32)],
         scalars=1,
-        flops=18 * rows * D * gate.shape[1],
+        limit=28,
         name="mlp_back",
     )
-    d_queries, d_pairs = vmem_call(
+
+
+def attend_backward(net, d_attended, attended, log_total, queries, pieces, place):
+    positions, starts, _, _, key_positions = place
+    rows, keys = positions.shape[0], key_positions.shape[1]
+    return vmem_call(
         functools.partial(
             attend_back_kernel, net.jobs(rows, keys), net.tile, net.parts, len(pieces)
         ),
-        (struct((rows, QW), F32), struct((keys // rows, rows, 2 * KW), BF)),
+        [struct((rows, QW), F32)]
+        + [struct((keys // rows // net.parts, rows, 2 * KW), BF)] * net.parts,
         (d_attended, attended, log_total, queries, positions, starts, key_positions, *pieces),
         [
             pltpu.VMEM((HQ, rows, HD), BF),
@@ -733,23 +800,27 @@
             pltpu.VMEM((KV, HD, keys), F32),
             pltpu.VMEM((KV, HD, keys), F32),
         ],
-        flops=10 * rows * keys * QW,
+        limit=net.limit(32),
         name="attend_back",
     )
-    adds = net.reduce_pairs(d_pairs)
+
+
+def input_backward(
+    net, source, attended, d_middle, d_queries, adds, gain_grad, mixed, g_attn, place
+):
+    rows = source.shape[0]
     mixed_shape = struct((8, 80, HALF), BF)
-    d_source, mixed_keep, mixed_send = vmem_call(
+    return vmem_call(
         functools.partial(input_kernel, len(adds)),
         (struct((rows, D), BF), mixed_shape, mixed_shape),
         (
-            core, source, attended, d_middle, d_queries, mixed, g_attn, gain_grad, cosine, sine,
-            *adds,
+            net.core.reshape(1), source, attended, d_middle, d_queries, mixed, g_attn, gain_grad,
+            place[2], place[3], *adds,
         ),
         scalars=1,
-        flops=6 * rows * D * MIXED,
+        limit=20,
         name="input",
     )
-    return d_source, net.reduce((keep, send), (mixed_keep, mixed_send))
 
 
 def shards(
@@ -761,23 +832,89 @@
     wide = jnp.stack(
         [jnp.concatenate([w_query[0], w_key[0], w_out[0], w_value[0]], axis=1), w_gate[0], w_up[0]]
     )
-    layers = net.gather(wide, w_down[0], jnp.stack([g_attn[0], g_mlp[0]]))
-
-    source = net.spread(lax.dynamic_index_in_dim(inputs[0], net.section, 0, keepdims=False))
-    d_result = net.spread(lax.dynamic_index_in_dim(cotangent[0], net.section, 0, keepdims=False))
     own = net.lengths(lengths)
     positions = net.positions_of(0, 0, rows)
     passed = (positions[:, None] >= jnp.cumsum(own)[None, :]).astype(I32)
     starts = jnp.sum(passed * own[None, :], axis=1)
     cosine, sine = turn_tables(positions - starts)
     place = (positions[:, None], starts[:, None], cosine, sine, net.key_positions(rows))
-
-    first, kept_first = layer_forward(net, source, layers[0], place)
-    second, kept_second = layer_forward(net, first, layers[1], place)
-    d_first, total_second = layer_backward(net, d_result, kept_second, layers[1], place)
-    d_input, total_first = layer_backward(net, d_first, kept_first, layers[0], place)
-    wide_grad, down_grad, gain_grads = net.finish(total_first, total_second, w_query.shape[1])
-    second = net.unspread(second)
+    shard = w_query.shape[1]
+
+    mixed_pack, deep_pack = net.pack(wide, w_down[0], jnp.stack([g_attn[0], g_mlp[0]]))
+    mixed_column = net.column(mixed_pack, 0)
+    deep_column = net.column(deep_pack, 0, mixed_column)
+    source = lax.dynamic_index_in_dim(inputs[0], net.section, 0, keepdims=False)
+    source = net.spread(tie(source, mixed_column))
+    d_result = lax.dynamic_index_in_dim(cotangent[0], net.section, 0, keepdims=False)
+    mixed_square = net.square(mixed_column)
+    deep_square = net.square(deep_column, mixed_square)
+    mixed_0, g_attn_0, g_mlp_0 = net.assemble(mixed_square, shard)
+
+    queries_0, pieces_0 = project(net, source, mixed_0, g_attn_0, place)
+    mixed_column = net.column(mixed_pack, 1, deep_column, queries_0)
+    deep_column = net.column(deep_pack, 1, deep_column, queries_0)
+    attended_0, log_0, middle_0 = attend_forward(net, source, queries_0, pieces_0, mixed_0, place)
+    mixed_column, deep_column, deep_square = tie((mixed_column, deep_column, deep_square), middle_0)
+    mixed_square = net.square(mixed_column, deep_square)
+    deep_0 = net.assemble(deep_square, shard, mixed_column, deep_column)
+    first = mlp_forward(middle_0, *deep_0, g_mlp_0)
+    deep_square = net.square(deep_column, mixed_square, first)
+    mixed_1, g_attn_1, g_mlp_1 = net.assemble(mixed_square, shard, first)
+
+    queries_1, pieces_1 = project(net, first, mixed_1, g_attn_1, place)
+    d_result = net.spread(tie(d_result, pieces_1))
+    attended_1, log_1, middle_1 = attend_forward(net, first, queries_1, pieces_1, mixed_1, place)
+    deep_1 = net.assemble(deep_square, shard, middle_1)
+
+    deep_keep, deep_send, gain_grad, d_middle, d_attended = mlp_backward(
+        net, d_result, middle_1, mixed_1, *deep_1, g_mlp_1
+    )
+    deep_sum_1 = net.reduce_core(deep_keep, deep_send)
+    d_queries, *d_pairs = attend_backward(
+        net, d_attended, attended_1, log_1, queries_1, pieces_1, place
+    )
+    deep_sum_1 = net.split_square(*tie(deep_sum_1, d_pairs))
+    second = mlp_forward(tie(middle_1, deep_sum_1), *deep_1, g_mlp_1)
+    adds = tie(net.reduce_pairs(d_pairs), deep_sum_1, second)
+    d_first, mixed_keep, mixed_send = input_backward(
+        net, first, attended_1, d_middle, d_queries, adds, gain_grad, mixed_1, g_attn_1, place
+    )
+    deep_sum_1 = net.move_square(deep_sum_1)
+    mixed_sum_1 = net.reduce_core(mixed_keep, mixed_send)
+
+    deep_keep, deep_send, gain_grad, d_middle, d_attended = mlp_backward(
+        net, d_first, middle_0, mixed_0, *deep_0, g_mlp_0
+    )
+    deep_sum_0 = net.reduce_core(deep_keep, deep_send)
+    mixed_sum_1 = net.split_square(*tie(mixed_sum_1, d_attended))
+    deep_sum_1 = net.split_column(tie(deep_sum_1, d_attended))
+    d_attended = tie(d_attended, mixed_sum_1, deep_sum_1)
+    mixed_sum_1 = net.move_square(mixed_sum_1)
+    deep_sum_1 = net.move_column(deep_sum_1)
+    d_queries, *d_pairs = attend_backward(
+        net, d_attended, attended_0, log_0, queries_0, pieces_0, place
+    )
+    deep_sum_0 = net.split_square(*tie(deep_sum_0, d_pairs))
+    mixed_sum_1 = net.split_column(tie(mixed_sum_1, d_pairs))
+    deep_sum_1 = net.total(tie(deep_sum_1, d_pairs))
+    second = net.unspread(tie(second, d_pairs))
+    adds = tie(net.reduce_pairs(d_pairs), deep_sum_0, mixed_sum_1, deep_sum_1)
+    d_input, mixed_keep, mixed_send = input_backward(
+        net, source, attended_0, d_middle, d_queries, adds, gain_grad, mixed_0, g_attn_0, place
+    )
+    deep_sum_0 = net.move_square(deep_sum_0)
+    mixed_sum_1 = net.move_column(mixed_sum_1)
+
+    mixed_sum_0 = net.reduce_core(mixed_keep, mixed_send)
+    mixed_sum_1 = net.total(tie(mixed_sum_1, d_input))
+    deep_sum_0 = tie(deep_sum_0, d_input)
+    mixed_sum_0 = net.move_square(tie(net.split_square(*mixed_sum_0), deep_sum_0))
+    deep_sum_0 = net.move_column(net.split_column(deep_sum_0))
+    deep_sum_0 = net.total(tie(deep_sum_0, mixed_sum_0))
+    mixed_sum_0 = net.total(net.move_column(net.split_column(mixed_sum_0)))
+    wide_grad, down_grad, gain_grads = net.finish(
+        (mixed_sum_0, deep_sum_0), (mixed_sum_1, deep_sum_1), shard
+    )
     d_input = net.unspread(d_input)
     kept = jnp.where(net.section == 0, d_input, second)
     crossed = swap_x(jnp.where(net.section == 0, second, d_input))

time: 515 us -> 416 us (0.81)
  the two profiles are of different devices: /device:TPU:9 before, /device:TPU:0 now
where the time goes in v2:
time: 416 us; the launch traced here: 409 us
  waiting for transfers between devices  145 us (35%)
  Pallas kernels  121 us (29%)
  starting transfers between devices  93.3 us (22%)
  local copies, waits for them, and re-layouts  32.7 us (8%)
  other arithmetic  15.2 us (4%)
    pallas_call x20, Pallas kernels, vmem_call(): pl.pallas_call(kernel, out_shape=out_shape, in_specs=specs, scratch_shape...  110 us
    ppermute x8, waiting for transfers between devices, swap_corner(): return lax.ppermute(value, ('section', 'fsdp'), flip(8, 6))  49.9 us
    ppermute x8, waiting for transfers between devices, swap_y(): return lax.ppermute(value, 'fsdp', flip(4, 2))  23.6 us
    unnamed x155, local copies, waits for them, and re-layouts  23 us
    ppermute x13, starting transfers between devices, swap_x(): return lax.ppermute(value, 'section', flip(2, 1))  18.6 us
    ppermute x12, starting transfers between devices, move_column(): lax.ppermute(part, 'ctx', ring(4, steps))  17.3 us
    ppermute x4, waiting for transfers between devices, spread(): lax.ppermute(block[k * half:(k + 1) * half], ('ctx', 'fsdp'), spread_pair...  16.2 us
    ppermute x4, waiting for transfers between devices, column(): return (start, above, below, lax.ppermute(start, 'ctx', ring(4, 2)))  11.9 us
  transfers between devices with their start and end apart: 93, of which 42 were waited for; matrix products, arithmetic and copies ran while one was open for 6% of the time, Pallas kernels for 20%

profile of v2, /device:TPU:0, one launch (start us, length us, event | category | flops | bytes accessed | tf_op | source)
XLA Modules:
  0.0 409.3 jit_solution(687068344715645957)
XLA Ops:
  18.2 3.2 collective-permute-done.3
  36.2 5.6 %collective-permute-done.5 = bf16[192,576]{1,0:T(8,128)(2,1)S(1)} collective-permute-done((bf16[192,576]{1,0:T(8,128)(2,1)S(1)}, bf16[192,576]{1,0:T(8,128)(2,1)S(1)}, u32[]{:S(2)}, u32[]{:S(2)}) %collective-permute-start.5) | collective-permute-done | bytes 221216 | tf_op jit(solution)/shard_map/ppermute | solution.py:456
  41.8 3.8 collective-permute-done.18
  46.2 8.7 %collective-permute-done.20 = bf16[120,768]{1,0:T(8,128)(2,1)S(1)} collective-permute-done((bf16[120,768]{1,0:T(8,128)(2,1)S(1)}, bf16[120,768]{1,0:T(8,128)(2,1)S(1)}, u32[]{:S(2)}, u32[]{:S(2)}) %collective-permute-start.20) | collective-permute-done | bytes 184352 | tf_op jit(solution)/shard_map/ppermute | solution.py:508
  58.7 3.8 collective-permute-start.22
  71.5 6.1 %collective-permute-done.24 = bf16[120,768]{1,0:T(8,128)(2,1)S(1)} collective-permute-done((bf16[120,768]{1,0:T(8,128)(2,1)}, bf16[120,768]{1,0:T(8,128)(2,1)S(1)}, u32[]{:S(2)}, u32[]{:S(2)}) %collective-permute-start.24) | collective-permute-done | bytes 184352 | tf_op jit(solution)/shard_map/ppermute | solution.py:506
  87.3 12.2 %attend.2 = (f32[384,576]{1,0:T(8,128)S(1)}, f32[384,9]{1,0:T(8,128)S(1)}, f32[384,576]{1,0:T(8,128)S(1)}) custom-call(bf16[384,576]{1,0:T(8,128)(2,1)S(1)} %pad_maximum_fusion.2.source_ref, bf16[384,576]{1,0:T(8,128)(2,1)S(1)} %copy-done.28, s32[384,1]{1,0:T(8,128)S(1)} %broadcast_in_dim.63.position_ref, s32[384,1]{1,0:T(8,128)S(1)} %reduce_sum.13.start_ref, ...), custom_call_target="tpu_custom_call" | custom-call | tf_op jit(solution)/shard_map/attend/pallas_call | solution.py:709
  107.2 3.5 assemble.5
  110.8 4.7 %mlp.2.source_ref = bf16[384,576]{1,0:T(8,128)(2,1)S(1)} custom-call(f32[384,576]{1,0:T(8,128)S(1)} %get-tuple-element.192.middle_ref, bf16[576,1536]{1,0:T(8,128)(2,1)S(1)} %get-tuple-element.216.gate_ref, bf16[576,1536]{1,0:T(8,128)(2,1)S(1)} %get-tuple-element.217.up_ref, bf16[1536,576]{1,0:T(8,128)(2,1)S(1)} %get-tuple-element.218.down_ref, ...), custom_call_target="tpu_custom_call" | custom-call | tf_op jit(solution)/shard_map/mlp/pallas_call | solution.py:709
  131.1 3.3 collective-permute-done.41
  142.6 12.4 %attend.3 = (f32[384,576]{1,0:T(8,128)S(1)}, f32[384,9]{1,0:T(8,128)S(1)}, f32[384,576]{1,0:T(8,128)S(1)}) custom-call(bf16[384,576]{1,0:T(8,128)(2,1)S(1)} %copy-done.5, bf16[384,576]{1,0:T(8,128)(2,1)S(1)} %copy-done.31, s32[384,1]{1,0:T(8,128)S(1)} %copy-done.12, s32[384,1]{1,0:T(8,128)S(1)} %copy-done.15, s32[1,1536]{1,0:T(1,128)S(1)} %reshape.149.key_position_ref, ...), custom_call_target="tpu_custom_call" | custom-call | tf_op jit(solution)/shard_map/attend/pallas_call | solution.py:709
  155.0 8.2 %collective-permute-done.48.refs_3_ = bf16[4,120,768]{2,1,0:T(8,128)(2,1)} collective-permute-done((bf16[4,120,768]{2,1,0:T(8,128)(2,1)}, bf16[4,120,768]{2,1,0:T(8,128)(2,1)}, u32[]{:S(2)}, u32[]{:S(2)}) %collective-permute-start.48) | collective-permute-done | bytes 737312 | tf_op jit(solution)/shard_map/ppermute | solution.py:70
  164.2 10.6 %collective-permute-done.45 = bf16[192,576]{1,0:T(8,128)(2,1)S(1)} collective-permute-done((bf16[192,576]{1,0:T(8,128)(2,1)S(1)}, bf16[192,576]{1,0:T(8,128)(2,1)S(1)}, u32[]{:S(2)}, u32[]{:S(2)}) %collective-permute-start.45) | collective-permute-done | bytes 221216 | tf_op jit(solution)/shard_map/ppermute | solution.py:456
  175.0 3.7 assemble.7
  178.8 12.3 %mlp_back.2 = (bf16[8,240,768]{2,1,0:T(8,128)(2,1)S(1)}, bf16[8,240,768]{2,1,0:T(8,128)(2,1)S(1)}, f32[1,576]{1,0:T(1,128)S(1)}, f32[384,576]{1,0:T(8,128)S(1)}, bf16[384,576]{1,0:T(8,128)(2,1)S(1)}) custom-call(s32[1]{0:T(128)} %bitcast.core_ref, bf16[384,576]{1,0:T(8,128)(2,1)S(1)} %pad_maximum_fusion.3.d_result_ref, ...), custom_call_target="tpu_custom_call" | custom-call | tf_op jit(solution)/shard_map/mlp_back/pallas_call | solution.py:709
  191.2 16.2 %attend_back.2 = (f32[384,576]{1,0:T(8,128)S(1)}, bf16[2,384,384]{2,1,0:T(8,128)(2,1)S(1)}, bf16[2,384,384]{2,1,0:T(8,128)(2,1)S(1)}) custom-call(bf16[384,576]{1,0:T(8,128)(2,1)S(1)} %get-tuple-element.248.d_out_ref, f32[384,576]{1,0:T(8,128)S(1)} %get-tuple-element.232.attended_ref, f32[384,9]{1,0:T(8,128)S(1)} %get-tuple-element.249.log_ref, ...), custom_call_target="tpu_custom_call" | custom-call | tf_op jit(solution)/shard_map/attend_back/pallas_call | solution.py:709
  211.2 4.9 %mlp.3 = bf16[384,576]{1,0:T(8,128)(2,1)S(1)} custom-call(f32[384,576]{1,0:T(8,128)S(1)} %get-tuple-element.262.middle_ref, bf16[576,1536]{1,0:T(8,128)(2,1)S(1)} %get-tuple-element.243.gate_ref, bf16[576,1536]{1,0:T(8,128)(2,1)S(1)} %get-tuple-element.244.up_ref, bf16[1536,576]{1,0:T(8,128)(2,1)S(1)} %get-tuple-element.245.down_ref, f32[1,576]{1,0:T(1,128)S(1)} %copy-done.52), custom_call_target="tpu_custom_call" | custom-call | tf_op jit(solution)/shard_map/mlp/pallas_call | solution.py:709
  216.0 3.0 collective-permute-done.54.refs_2_
  219.1 3.0 input.2
  222.1 12.2 %mlp_back.3 = (bf16[8,240,768]{2,1,0:T(8,128)(2,1)S(1)}, bf16[8,240,768]{2,1,0:T(8,128)(2,1)S(1)}, f32[1,576]{1,0:T(1,128)S(1)}, f32[384,576]{1,0:T(8,128)S(1)}, bf16[384,576]{1,0:T(8,128)(2,1)S(1)}) custom-call(s32[1]{0:T(128)} %bitcast.core_ref, bf16[384,576]{1,0:T(8,128)(2,1)S(1)} %get-tuple-element.266.d_result_ref, f32[384,576]{1,0:T(8,128)S(1)} %copy-done.26, ...), custom_call_target="tpu_custom_call" | custom-call | tf_op jit(solution)/shard_map/mlp_back/pallas_call | solution.py:709
  238.3 15.0 %collective-permute-done.57.refs_1_ = bf16[4,240,384]{2,1,0:T(8,128)(2,1)S(1)} collective-permute-done((bf16[4,240,384]{2,1,0:T(8,128)(2,1)S(1)}, bf16[4,240,384]{2,1,0:T(8,128)(2,1)S(1)}, u32[]{:S(2)}, u32[]{:S(2)}) %collective-permute-start.57) | collective-permute-done | bytes 737312 | tf_op jit(solution)/shard_map/ppermute | solution.py:58
  254.7 15.6 %collective-permute-done.59.refs_3_ = bf16[4,240,384]{2,1,0:T(8,128)(2,1)S(1)} collective-permute-done((bf16[4,240,384]{2,1,0:T(8,128)(2,1)S(1)}, bf16[4,240,384]{2,1,0:T(8,128)(2,1)S(1)}, u32[]{:S(2)}, u32[]{:S(2)}) %collective-permute-start.59) | collective-permute-done | bytes 737312 | tf_op jit(solution)/shard_map/ppermute | solution.py:70
  276.0 16.3 %attend_back.3 = (f32[384,576]{1,0:T(8,128)S(1)}, bf16[2,384,384]{2,1,0:T(8,128)(2,1)S(1)}, bf16[2,384,384]{2,1,0:T(8,128)(2,1)S(1)}) custom-call(bf16[384,576]{1,0:T(8,128)(2,1)S(1)} %get-tuple-element.285.d_out_ref, f32[384,576]{1,0:T(8,128)S(1)} %copy-done.24, f32[384,9]{1,0:T(8,128)S(1)} %copy-done.46, bf16[384,576]{1,0:T(8,128)(2,1)S(1)} %copy-done.29, ...), custom_call_target="tpu_custom_call" | custom-call | tf_op jit(solution)/shard_map/attend_back/pallas_call | solution.py:709
  297.5 3.1 collective-permute-done.63.refs_1_
  301.7 3.1 collective-permute-start.72
  309.7 3.0 input.3
  319.3 3.8 collective-permute-start.70
  323.2 3.7 collective-permute-done.70
  329.3 5.0 %collective-permute-done.75.refs_1_ = bf16[4,240,384]{2,1,0:T(8,128)(2,1)S(1)} collective-permute-done((bf16[4,240,384]{2,1,0:T(8,128)(2,1)S(1)}, bf16[4,240,384]{2,1,0:T(8,128)(2,1)S(1)}, u32[]{:S(2)}, u32[]{:S(2)}) %collective-permute-start.75) | collective-permute-done | bytes 737312 | tf_op jit(solution)/shard_map/ppermute | solution.py:58
  335.7 16.8 %collective-permute-done.77.refs_3_ = bf16[4,240,384]{2,1,0:T(8,128)(2,1)S(1)} collective-permute-done((bf16[4,240,384]{2,1,0:T(8,128)(2,1)S(1)}, bf16[4,240,384]{2,1,0:T(8,128)(2,1)S(1)}, u32[]{:S(2)}, u32[]{:S(2)}) %collective-permute-start.77) | collective-permute-done | bytes 737312 | tf_op jit(solution)/shard_map/ppermute | solution.py:70
  379.0 3.6 collective-permute-done.80.refs_3_
  398.6 3.9 collective-permute-done.91
  (416 shorter events, 173.0 us)
Async XLA Ops:
  9.0 16.7 %collective-permute-start.17 = (bf16[120,768]{1,0:T(8,128)(2,1)}, bf16[120,768]{1,0:T(8,128)(2,1)}, u32[]{:S(2)}, u32[]{:S(2)}) collective-permute-start(bf16[120,768]{1,0:T(8,128)(2,1)} %constant_dynamic-slice_fusion.1), channel_id=1, source_target_pairs={{0,16},{16,0},{1,17},{17,1},{2,18},{18,2},{3,19},{19,3},{4,20},{20... | collective-permute-start | bytes 552968 | tf_op jit(solution)/shard_map/ppermute | solution.py:66
  29.5 16.1 %collective-permute-start.18 = (bf16[120,768]{1,0:T(8,128)(2,1)S(1)}, bf16[120,768]{1,0:T(8,128)(2,1)S(1)}, u32[]{:S(2)}, u32[]{:S(2)}) collective-permute-start(bf16[120,768]{1,0:T(8,128)(2,1)S(1)} %get-tuple-element.196), channel_id=1, source_target_pairs={{0,4},{4,8},{8,12},{12,0},{1,5},{5,9},{9,13},{13,1},{2,6},{6,10},{... | collective-permute-start | bytes 552968 | tf_op jit(solution)/shard_map/ppermute | solution.py:506
  35.8 19.2 %collective-permute-start.20 = (bf16[120,768]{1,0:T(8,128)(2,1)S(1)}, bf16[120,768]{1,0:T(8,128)(2,1)S(1)}, u32[]{:S(2)}, u32[]{:S(2)}) collective-permute-start(bf16[120,768]{1,0:T(8,128)(2,1)S(1)} %get-tuple-element.196), channel_id=1, source_target_pairs={{0,8},{4,12},{8,0},{12,4},{1,9},{5,13},{9,1},{13,5},{2,10},{6,14},... | collective-permute-start | bytes 552968 | tf_op jit(solution)/shard_map/ppermute | solution.py:508
  35.8 19.2 %collective-permute-start.9 = (bf16[4,40,768]{2,1,0:T(8,128)(2,1)S(1)}, bf16[4,40,768]{2,1,0:T(8,128)(2,1)S(1)}, u32[]{:S(2)}, u32[]{:S(2)}) collective-permute-start(bf16[4,40,768]{2,1,0:T(8,128)(2,1)S(1)} %pad_maximum_fusion.7.refs_0_), channel_id=1, source_target_pairs={{0,1},{1,0},{2,3},{3,2},{4,5},{5,4},{6,7},{7,6},{8,9},{9,8},{10,11... | collective-permute-start | bytes 737288 | tf_op jit(solution)/shard_map/ppermute | solution.py:54
  65.4 35.8 %collective-permute-start.27 = (bf16[4,120,768]{2,1,0:T(8,128)(2,1)S(1)}, bf16[4,120,768]{2,1,0:T(8,128)(2,1)}, u32[]{:S(2)}, u32[]{:S(2)}) collective-permute-start(bf16[4,120,768]{2,1,0:T(8,128)(2,1)S(1)} %pad_maximum_fusion.refs_0_), channel_id=1, source_target_pairs={{0,2},{1,3},{2,0},{3,1},{4,6},{5,7},{6,4},{7,5},{8,10},{9,11},{10,... | collective-permute-start | bytes 2211848 | tf_op jit(solution)/shard_map/ppermute | solution.py:58
  66.9 34.3 %collective-permute-start.28 = (bf16[4,120,768]{2,1,0:T(8,128)(2,1)S(1)}, bf16[4,120,768]{2,1,0:T(8,128)(2,1)}, u32[]{:S(2)}, u32[]{:S(2)}) collective-permute-start(bf16[4,120,768]{2,1,0:T(8,128)(2,1)S(1)} %pad_maximum_fusion.refs_0_), channel_id=1, source_target_pairs={{0,16},{16,0},{1,17},{17,1},{2,18},{18,2},{3,19},{19,3},{4,20},{20... | collective-permute-start | bytes 2211848 | tf_op jit(solution)/shard_map/ppermute | solution.py:66
  69.0 32.2 %collective-permute-start.29 = (bf16[4,120,768]{2,1,0:T(8,128)(2,1)S(1)}, bf16[4,120,768]{2,1,0:T(8,128)(2,1)}, u32[]{:S(2)}, u32[]{:S(2)}) collective-permute-start(bf16[4,120,768]{2,1,0:T(8,128)(2,1)S(1)} %pad_maximum_fusion.refs_0_), channel_id=1, source_target_pairs={{0,18},{1,19},{2,16},{3,17},{16,2},{17,3},{18,0},{19,1},{4,22},{5,... | collective-permute-start | bytes 2211848 | tf_op jit(solution)/shard_map/ppermute | solution.py:70
  80.1 21.1 %collective-permute-start.25 = (bf16[120,768]{1,0:T(8,128)(2,1)}, bf16[120,768]{1,0:T(8,128)(2,1)}, u32[]{:S(2)}, u32[]{:S(2)}) collective-permute-start(bf16[120,768]{1,0:T(8,128)(2,1)} %get-tuple-element.235), channel_id=1, source_target_pairs={{0,12},{4,0},{8,4},{12,8},{1,13},{5,1},{9,5},{13,9},{2,14},{6,2},{... | collective-permute-start | bytes 552968 | tf_op jit(solution)/shard_map/ppermute | solution.py:507
  82.5 18.7 %collective-permute-start.26 = (bf16[120,768]{1,0:T(8,128)(2,1)}, bf16[120,768]{1,0:T(8,128)(2,1)}, u32[]{:S(2)}, u32[]{:S(2)}) collective-permute-start(bf16[120,768]{1,0:T(8,128)(2,1)} %get-tuple-element.235), channel_id=1, source_target_pairs={{0,8},{4,12},{8,0},{12,4},{1,9},{5,13},{9,1},{13,5},{2,10},{6,14},... | collective-permute-start | bytes 552968 | tf_op jit(solution)/shard_map/ppermute | solution.py:508
  127.6 27.4 %collective-permute-start.46 = (bf16[4,120,768]{2,1,0:T(8,128)(2,1)}, bf16[4,120,768]{2,1,0:T(8,128)(2,1)}, u32[]{:S(2)}, u32[]{:S(2)}) collective-permute-start(bf16[4,120,768]{2,1,0:T(8,128)(2,1)} %pad_maximum_fusion.1.refs_0_), channel_id=1, source_target_pairs={{0,2},{1,3},{2,0},{3,1},{4,6},{5,7},{6,4},{7,5},{8,10},{9,11},{10,... | collective-permute-start | bytes 2211848 | tf_op jit(solution)/shard_map/ppermute | solution.py:58
  128.1 26.9 %collective-permute-start.47 = (bf16[4,120,768]{2,1,0:T(8,128)(2,1)}, bf16[4,120,768]{2,1,0:T(8,128)(2,1)}, u32[]{:S(2)}, u32[]{:S(2)}) collective-permute-start(bf16[4,120,768]{2,1,0:T(8,128)(2,1)} %pad_maximum_fusion.1.refs_0_), channel_id=1, source_target_pairs={{0,16},{16,0},{1,17},{17,1},{2,18},{18,2},{3,19},{19,3},{4,20},{20... | collective-permute-start | bytes 2211848 | tf_op jit(solution)/shard_map/ppermute | solution.py:66
  129.6 33.6 %collective-permute-start.48 = (bf16[4,120,768]{2,1,0:T(8,128)(2,1)}, bf16[4,120,768]{2,1,0:T(8,128)(2,1)}, u32[]{:S(2)}, u32[]{:S(2)}) collective-permute-start(bf16[4,120,768]{2,1,0:T(8,128)(2,1)} %pad_maximum_fusion.1.refs_0_), channel_id=1, source_target_pairs={{0,18},{1,19},{2,16},{3,17},{16,2},{17,3},{18,0},{19,1},{4,22},{5,... | collective-permute-start | bytes 2211848 | tf_op jit(solution)/shard_map/ppermute | solution.py:70
  137.5 26.7 %collective-permute-start.44 = (bf16[192,576]{1,0:T(8,128)(2,1)S(1)}, bf16[192,576]{1,0:T(8,128)(2,1)S(1)}, u32[]{:S(2)}, u32[]{:S(2)}) collective-permute-start(bf16[192,576]{1,0:T(8,128)(2,1)S(1)} %get-tuple-element.410), channel_id=1, source_target_pairs={{0,0},{1,8},{2,2},{3,10},{4,4},{5,12},{6,6},{7,14},{8,5},{9,13},{1... | collective-permute-start | bytes 663560 | tf_op jit(solution)/shard_map/ppermute | solution.py:456
  191.1 18.7 %collective-permute-start.55 = (bf16[8,240,768]{2,1,0:T(8,128)(2,1)S(1)}, bf16[8,240,768]{2,1,0:T(8,128)(2,1)S(1)}, u32[]{:S(2)}, u32[]{:S(2)}) collective-permute-start(bf16[8,240,768]{2,1,0:T(8,128)(2,1)S(1)} %get-tuple-element.255), channel_id=1, source_target_pairs={{0,1},{1,0},{2,3},{3,2},{4,5},{5,4},{6,7},{7,6},{8,9},{9,8},{10,11... | collective-permute-start | bytes 8847368 | tf_op jit(solution)/shard_map/ppermute | solution.py:54
  234.3 74.1 %collective-permute-start.62 = (bf16[8,240,768]{2,1,0:T(8,128)(2,1)S(1)}, bf16[8,240,768]{2,1,0:T(8,128)(2,1)S(1)}, u32[]{:S(2)}, u32[]{:S(2)}) collective-permute-start(bf16[8,240,768]{2,1,0:T(8,128)(2,1)S(1)} %get-tuple-element.292), channel_id=1, source_target_pairs={{0,1},{1,0},{2,3},{3,2},{4,5},{5,4},{6,7},{7,6},{8,9},{9,8},{10,11... | collective-permute-start | bytes 8847368 | tf_op jit(solution)/shard_map/ppermute | solution.py:54
  234.4 40.8 %collective-permute-start.56 = (bf16[8,80,768]{2,1,0:T(8,128)(2,1)S(1)}, bf16[8,80,768]{2,1,0:T(8,128)(2,1)S(1)}, u32[]{:S(2)}, u32[]{:S(2)}) collective-permute-start(bf16[8,80,768]{2,1,0:T(8,128)(2,1)S(1)} %get-tuple-element.270), channel_id=1, source_target_pairs={{0,1},{1,0},{2,3},{3,2},{4,5},{5,4},{6,7},{7,6},{8,9},{9,8},{10,11... | collective-permute-start | bytes 2949128 | tf_op jit(solution)/shard_map/ppermute | solution.py:54
  234.8 18.5 %collective-permute-start.57 = (bf16[4,240,384]{2,1,0:T(8,128)(2,1)S(1)}, bf16[4,240,384]{2,1,0:T(8,128)(2,1)S(1)}, u32[]{:S(2)}, u32[]{:S(2)}) collective-permute-start(bf16[4,240,384]{2,1,0:T(8,128)(2,1)S(1)} %get-tuple-element.259), channel_id=1, source_target_pairs={{0,2},{1,3},{2,0},{3,1},{4,6},{5,7},{6,4},{7,5},{8,10},{9,11},{10,... | collective-permute-start | bytes 2211848 | tf_op jit(solution)/shard_map/ppermute | solution.py:58
  235.4 19.4 %collective-permute-start.58 = (bf16[4,240,384]{2,1,0:T(8,128)(2,1)S(1)}, bf16[4,240,384]{2,1,0:T(8,128)(2,1)S(1)}, u32[]{:S(2)}, u32[]{:S(2)}) collective-permute-start(bf16[4,240,384]{2,1,0:T(8,128)(2,1)S(1)} %get-tuple-element.260), channel_id=1, source_target_pairs={{0,16},{16,0},{1,17},{17,1},{2,18},{18,2},{3,19},{19,3},{4,20},{20... | collective-permute-start | bytes 2211848 | tf_op jit(solution)/shard_map/ppermute | solution.py:66
  236.9 33.4 %collective-permute-start.59 = (bf16[4,240,384]{2,1,0:T(8,128)(2,1)S(1)}, bf16[4,240,384]{2,1,0:T(8,128)(2,1)S(1)}, u32[]{:S(2)}, u32[]{:S(2)}) collective-permute-start(bf16[4,240,384]{2,1,0:T(8,128)(2,1)S(1)} %get-tuple-element.261), channel_id=1, source_target_pairs={{0,18},{1,19},{2,16},{3,17},{16,2},{17,3},{18,0},{19,1},{4,22},{5,... | collective-permute-start | bytes 2211848 | tf_op jit(solution)/shard_map/ppermute | solution.py:70
  271.3 21.1 %collective-permute-start.66 = (bf16[240,384]{1,0:T(8,128)(2,1)S(1)}, bf16[240,384]{1,0:T(8,128)(2,1)S(1)}, u32[]{:S(2)}, u32[]{:S(2)}) collective-permute-start(bf16[240,384]{1,0:T(8,128)(2,1)S(1)} %get-tuple-element.282), channel_id=1, source_target_pairs={{0,4},{4,8},{8,12},{12,0},{1,5},{5,9},{9,13},{13,1},{2,6},{6,10},{... | collective-permute-start | bytes 552968 | tf_op jit(solution)/shard_map/ppermute | solution.py:574
  271.6 21.3 %collective-permute-start.67 = (bf16[240,384]{1,0:T(8,128)(2,1)S(1)}, bf16[240,384]{1,0:T(8,128)(2,1)S(1)}, u32[]{:S(2)}, u32[]{:S(2)}) collective-permute-start(bf16[240,384]{1,0:T(8,128)(2,1)S(1)} %get-tuple-element.283), channel_id=1, source_target_pairs={{0,8},{4,12},{8,0},{12,4},{1,9},{5,13},{9,1},{13,5},{2,10},{6,14},... | collective-permute-start | bytes 552968 | tf_op jit(solution)/shard_map/ppermute | solution.py:574
  273.3 21.1 %collective-permute-start.68 = (bf16[240,384]{1,0:T(8,128)(2,1)S(1)}, bf16[240,384]{1,0:T(8,128)(2,1)S(1)}, u32[]{:S(2)}, u32[]{:S(2)}) collective-permute-start(bf16[240,384]{1,0:T(8,128)(2,1)S(1)} %get-tuple-element.284), channel_id=1, source_target_pairs={{0,12},{4,0},{8,4},{12,8},{1,13},{5,1},{9,5},{13,9},{2,14},{6,2},{... | collective-permute-start | bytes 552968 | tf_op jit(solution)/shard_map/ppermute | solution.py:574
  301.7 16.1 %collective-permute-start.72 = (bf16[192,576]{1,0:T(8,128)(2,1)S(1)}, bf16[192,576]{1,0:T(8,128)(2,1)S(1)}, u32[]{:S(2)}, u32[]{:S(2)}) collective-permute-start(bf16[192,576]{1,0:T(8,128)(2,1)S(1)} %get-tuple-element.406), channel_id=1, source_target_pairs={{1,0},{9,1},{3,2},{11,3},{5,4},{13,5},{7,6},{15,7},{4,8},{12,9},{6... | collective-permute-start | bytes 663560 | tf_op jit(solution)/shard_map/ppermute | solution.py:468
  313.5 39.9 %collective-permute-start.74 = (bf16[8,80,768]{2,1,0:T(8,128)(2,1)S(1)}, bf16[8,80,768]{2,1,0:T(8,128)(2,1)S(1)}, u32[]{:S(2)}, u32[]{:S(2)}) collective-permute-start(bf16[8,80,768]{2,1,0:T(8,128)(2,1)S(1)} %get-tuple-element.317), channel_id=1, source_target_pairs={{0,1},{1,0},{2,3},{3,2},{4,5},{5,4},{6,7},{7,6},{8,9},{9,8},{10,11... | collective-permute-start | bytes 2949128 | tf_op jit(solution)/shard_map/ppermute | solution.py:54
  315.8 18.5 %collective-permute-start.75 = (bf16[4,240,384]{2,1,0:T(8,128)(2,1)S(1)}, bf16[4,240,384]{2,1,0:T(8,128)(2,1)S(1)}, u32[]{:S(2)}, u32[]{:S(2)}) collective-permute-start(bf16[4,240,384]{2,1,0:T(8,128)(2,1)S(1)} %get-tuple-element.296), channel_id=1, source_target_pairs={{0,2},{1,3},{2,0},{3,1},{4,6},{5,7},{6,4},{7,5},{8,10},{9,11},{10,... | collective-permute-start | bytes 2211848 | tf_op jit(solution)/shard_map/ppermute | solution.py:58
  316.3 19.4 %collective-permute-start.76 = (bf16[4,240,384]{2,1,0:T(8,128)(2,1)S(1)}, bf16[4,240,384]{2,1,0:T(8,128)(2,1)S(1)}, u32[]{:S(2)}, u32[]{:S(2)}) collective-permute-start(bf16[4,240,384]{2,1,0:T(8,128)(2,1)S(1)} %get-tuple-element.297), channel_id=1, source_target_pairs={{0,16},{16,0},{1,17},{17,1},{2,18},{18,2},{3,19},{19,3},{4,20},{20... | collective-permute-start | bytes 2211848 | tf_op jit(solution)/shard_map/ppermute | solution.py:66
  317.8 34.6 %collective-permute-start.77 = (bf16[4,240,384]{2,1,0:T(8,128)(2,1)S(1)}, bf16[4,240,384]{2,1,0:T(8,128)(2,1)S(1)}, u32[]{:S(2)}, u32[]{:S(2)}) collective-permute-start(bf16[4,240,384]{2,1,0:T(8,128)(2,1)S(1)} %get-tuple-element.298), channel_id=1, source_target_pairs={{0,18},{1,19},{2,16},{3,17},{16,2},{17,3},{18,0},{19,1},{4,22},{5,... | collective-permute-start | bytes 2211848 | tf_op jit(solution)/shard_map/ppermute | solution.py:70
  327.8 44.9 %collective-permute-start.73 = (bf16[384,576]{1,0:T(8,128)(2,1)}, bf16[384,576]{1,0:T(8,128)(2,1)}, u32[]{:S(2)}, u32[]{:S(2)}) collective-permute-start(bf16[384,576]{1,0:T(8,128)(2,1)} %broadcast_select_fusion), channel_id=1, source_target_pairs={{0,16},{16,0},{1,17},{17,1},{2,18},{18,2},{3,19},{19,3},{4,20},{20... | collective-permute-start | bytes 1327112 | tf_op jit(solution)/shard_map/ppermute | solution.py:66
  356.9 17.4 %collective-permute-start.78 = (bf16[4,80,384]{2,1,0:T(8,128)(2,1)}, bf16[4,80,384]{2,1,0:T(8,128)(2,1)S(1)}, u32[]{:S(2)}, u32[]{:S(2)}) collective-permute-start(bf16[4,80,384]{2,1,0:T(8,128)(2,1)} %get-tuple-element.327), channel_id=1, source_target_pairs={{0,2},{1,3},{2,0},{3,1},{4,6},{5,7},{6,4},{7,5},{8,10},{9,11},{10,... | collective-permute-start | bytes 737288 | tf_op jit(solution)/shard_map/ppermute | solution.py:58
  368.5 18.5 %collective-permute-start.88 = (bf16[240,384]{1,0:T(8,128)(2,1)S(1)}, bf16[240,384]{1,0:T(8,128)(2,1)S(1)}, u32[]{:S(2)}, u32[]{:S(2)}) collective-permute-start(bf16[240,384]{1,0:T(8,128)(2,1)S(1)} %get-tuple-element.339), channel_id=1, source_target_pairs={{0,4},{4,8},{8,12},{12,0},{1,5},{5,9},{9,13},{13,1},{2,6},{6,10},{... | collective-permute-start | bytes 552968 | tf_op jit(solution)/shard_map/ppermute | solution.py:574
  369.7 19.6 %collective-permute-start.89 = (bf16[240,384]{1,0:T(8,128)(2,1)}, bf16[240,384]{1,0:T(8,128)(2,1)}, u32[]{:S(2)}, u32[]{:S(2)}) collective-permute-start(bf16[240,384]{1,0:T(8,128)(2,1)} %get-tuple-element.340), channel_id=1, source_target_pairs={{0,8},{4,12},{8,0},{12,4},{1,9},{5,13},{9,1},{13,5},{2,10},{6,14},... | collective-permute-start | bytes 552968 | tf_op jit(solution)/shard_map/ppermute | solution.py:574
  372.6 16.7 %collective-permute-start.90 = (bf16[240,384]{1,0:T(8,128)(2,1)}, bf16[240,384]{1,0:T(8,128)(2,1)}, u32[]{:S(2)}, u32[]{:S(2)}) collective-permute-start(bf16[240,384]{1,0:T(8,128)(2,1)} %get-tuple-element.341), channel_id=1, source_target_pairs={{0,12},{4,0},{8,4},{12,8},{1,13},{5,1},{9,5},{13,9},{2,14},{6,2},{... | collective-permute-start | bytes 552968 | tf_op jit(solution)/shard_map/ppermute | solution.py:574
  (132 other events, 1051.8 us)

commit v3 on v2

--- a/solution.py
+++ b/solution.py
@@ -226,7 +226,8 @@
 def mlp_back_kernel(
     core_ref, d_result_ref, middle_ref, mixed_ref, gate_ref, up_ref, down_ref, gain_ref, *refs
 ):
-    packed_refs, (gain_grad_ref, d_middle_ref, d_out_ref, normed_scr, total_scr) = refs[:2], refs[2:]
+    packed_refs, refs = (refs[:2], refs[2:4]), refs[4:]
+    gain_grad_ref, d_middle_ref, d_out_ref, normed_scr, total_scr = refs
     core = core_ref[0]
     gain = gain_ref[...]
     inverse, scaled, normed = norm(middle_ref[...], gain)
@@ -234,9 +235,8 @@
     total_scr[...] = jnp.zeros_like(total_scr)
     width = 384
 
-    @pl.loop(0, gate_ref.shape[1] // width)
-    def _(step):
-        at = pl.ds(pl.multiple_of(step * width, width), width)
+    for step in range(gate_ref.shape[1] // width):
+        at = slice(step * width, (step + 1) * width)
         low = d_result_ref[...]
         normed = normed_scr[...]
         gate = mm(normed, gate_ref[:, at])
@@ -251,19 +251,21 @@
         gate_grad = mm_tn(normed, d_gate)
         up_grad = mm_tn(normed, d_up)
         down_grad = mm_tn(hidden, low)
-        slot = (step // 2) ^ core
-        columns = pl.ds(pl.multiple_of((step % 2) * width, width), width)
-        wide = [
-            jnp.concatenate([grad[72 * k : 72 * k + 72] for grad in (gate_grad, up_grad)], axis=0)
-            for k in range(8)
-        ]
-        wide = jnp.stack(wide).astype(BF)
-        store(slot, packed_refs, (slice(None), slice(0, 144), columns), wide)
+        columns = slice((step % 2) * width, (step % 2 + 1) * width)
+        for z in range(4):
+            wide = [
+                jnp.concatenate([grad[72 * k : 72 * k + 72] for grad in (gate_grad, up_grad)], axis=0)
+                for k in (2 * z, 2 * z + 1)
+            ]
+            refs = [group[z // 2] for group in packed_refs]
+            place = (slice(2 * (z % 2), 2 * (z % 2) + 2), slice(0, 144), columns)
+            store(core ^ (step // 2), refs, place, jnp.stack(wide).astype(BF))
         down_grad = down_grad.reshape(2, 2, 96, D).astype(BF)
         down_grad = jnp.concatenate([down_grad, jnp.zeros((2, 2, 96, HALF - D), BF)], axis=3)
         for side in (0, 1):
-            at = (pl.ds(2 * step, 2), slice(144, 240), slice(None))
-            store(core ^ side, packed_refs, at, down_grad[:, side])
+            refs = [group[step // 2] for group in packed_refs]
+            place = (slice(2 * (step % 2), 2 * (step % 2) + 2), slice(144, 240), slice(None))
+            store(core ^ side, refs, place, down_grad[:, side])
 
     d_mlp, gain_grad = norm_back(total_scr[...], scaled, inverse, gain)
     gain_grad_ref[...] = gain_grad
@@ -365,9 +367,16 @@
         store(half ^ core, packed_refs, Ellipsis, jnp.stack(blocks).astype(BF))
 
 
-def assemble_kernel(mixed, index_ref, *refs):
-    pieces, outs = refs[:8], refs[8:]
+def assemble_kernel(mixed, doubled, index_ref, *refs):
+    pieces, outs = refs[:-3], refs[-3:]
     x, z, y, core = (index_ref[i] for i in range(4))
+
+    def piece(cross, dx, dy, place):
+        if len(pieces) == 2:
+            return pieces[cross][2 * dx + dy, place].astype(F32)
+        first, second = (dx, dy) if place < 2 else (dy, dx)
+        ref = pieces[4 * cross + 2 * (place // 2) + first]
+        return ref[2 * second + place % 2].astype(F32)
 
     def ordered(parts):
         rows = [
@@ -382,15 +391,12 @@
     gains = jnp.zeros((8, D), F32)
     owner = lax.broadcasted_iota(I32, (8, D), 1) // 144
     for place, steps in enumerate((0, 1, 3, 2)):
-        row = (z + 4 - steps) % 4
+        row = z ^ place if doubled else (z + 4 - steps) % 4
         at = pl.ds(pl.multiple_of(row * 144, 144), 144)
         for dx in (0, 1):
             columns = pl.ds(pl.multiple_of((x ^ dx) * HALF, HALF), HALF)
             parts = ordered(
-                [
-                    [pieces[4 * cross + 2 * dx + dy][place].astype(F32) for dy in (0, 1)]
-                    for cross in (0, 1)
-                ]
+                [[piece(cross, dx, dy, place) for dy in (0, 1)] for cross in (0, 1)]
             )
             outs[0][at, columns] = jnp.concatenate([part[:36] for part in parts]).astype(BF)
             if mixed:
@@ -408,23 +414,73 @@
         outs[2][...] = gains[5:6]
 
 
-def split_square_kernel(index_ref, keep_ref, received_ref, *out_refs):
+def paired(groups, z, y, lanes):
+    sums = []
+    for keep_refs, received_refs in groups:
+        each = 4 // len(keep_refs)
+        at = (2 * (z % each) + y, slice(None), lanes)
+        sums.append(keep_refs[z // each][at].astype(F32) + received_refs[z // each][at].astype(F32))
+    return jnp.concatenate(sums) if len(sums) > 1 else sums[0]
+
+
+def read_groups(counts, refs):
+    groups = []
+    for count in counts:
+        groups.append((refs[:count], refs[count : 2 * count]))
+        refs = refs[2 * count :]
+    return groups, refs
+
+
+def split_square_kernel(counts, index_ref, *refs):
     x, y = index_ref[0], index_ref[1]
-    half = keep_ref.shape[2] // 2
+    groups, out_refs = read_groups(counts, refs)
+    half = HALF // 2
     for index, ref in enumerate(out_refs):
         dx, dy = divmod(index, 2)
         lanes = pl.ds(pl.multiple_of((x ^ dx) * half, half), half)
         for z in range(4):
-            block = 2 * z + (y ^ dy)
-            held = keep_ref[block, :, lanes].astype(F32) + received_ref[block, :, lanes].astype(F32)
-            ref[z] = held.astype(ref.dtype)
+            ref[z] = paired(groups, z, y ^ dy, lanes).astype(ref.dtype)
+
+
+def split_first_kernel(counts, index_ref, *refs):
+    x, y = index_ref[0], index_ref[1]
+    groups, (own_ref, sent_ref, own_row_ref, sent_row_ref) = read_groups(counts, refs)
+    half = HALF // 2
+    for dx, ref in enumerate((own_ref, sent_ref)):
+        lanes = pl.ds(pl.multiple_of((x ^ dx) * half, half), half)
+        for z in (0, 1):
+            for row in (0, 1):
+                ref[z, row] = paired(groups, z, row, lanes).astype(ref.dtype)
+    for dy, ref in enumerate((own_row_ref, sent_row_ref)):
+        for z in (0, 1):
+            ref[z] = paired(groups, z + 2, y ^ dy, slice(None)).astype(ref.dtype)
+
+
+def split_second_kernel(index_ref, own_ref, moved_ref, own_row_ref, moved_row_ref, *out_refs):
+    x, y = index_ref[0], index_ref[1]
+    total_ref, sent_ref, sent_row_ref = out_refs
+    half = HALF // 2
+    for z in (0, 1):
+        for step, ref, at in ((0, total_ref, z), (1, sent_ref, z)):
+            part = own_ref[z, y ^ step] + moved_ref[z, y ^ step].astype(F32)
+            ref[at] = part.astype(ref.dtype)
+        for step, ref, at in ((0, total_ref, z + 2), (1, sent_row_ref, z)):
+            lanes = pl.ds(pl.multiple_of((x ^ step) * half, half), half)
+            part = own_row_ref[z, :, lanes] + moved_row_ref[z, :, lanes].astype(F32)
+            ref[at] = part.astype(ref.dtype)
 
 
 def split_column_kernel(index_ref, *refs):
-    parts, out_refs = refs[:4], refs[4:]
+    parts, out_refs = refs[:-4], refs[-4:]
     for steps, ref in enumerate(out_refs):
         row = (index_ref[2] + steps) % 4
-        ref[...] = sum(part[row].astype(F32) for part in parts).astype(ref.dtype)
+        total = parts[0][row]
+        if len(parts) == 3:
+            added = [part[row % 2].astype(F32) for part in parts[1:]]
+            total = total + jnp.where(row < 2, *added)
+        else:
+            total = total + sum(part[row].astype(F32) for part in parts[1:])
+        ref[...] = total.astype(ref.dtype)
 
 
 class Fast:
@@ -472,8 +528,11 @@
         )
 
     def key_positions(self, rows):
-        full = jnp.stack([self.positions_of(dz, dc, rows) for dc in (0, 1) for dz in (0, 1)])
-        return full.reshape(4, 2, rows // 2).swapaxes(0, 1).reshape(1, -1)
+        at = lax.broadcasted_iota(I32, (1, 4 * rows), 1)
+        half = rows // 2
+        piece = at // half % 4
+        member = 2 * ((self.z % 2) ^ (piece % 2)) + (self.core ^ (piece // 2))
+        return jnp.where(at < 4 * half, member, 7 - member) * half + at % half
 
     def jobs(self, rows, keys):
         return ((0, rows // 2, keys // 2), (rows // 2, rows // 2, keys))
@@ -501,30 +560,66 @@
             for part in (mixed, deep)
         ]
 
-    def column(self, pack, layer, *after):
-        start = tie(jnp.where(self.section == layer, *pack), *after)
-        above = lax.ppermute(start, "ctx", ring(4, 1))
-        below = lax.ppermute(start, "ctx", ring(4, 3))
-        return start, above, below, lax.ppermute(start, "ctx", ring(4, 2))
-
-    def square(self, column, *after):
-        column = jnp.stack(tie(column, *after))
+    def start(self, packs, layer, *after):
+        start = [jnp.where(self.section == layer, *pack) for pack in packs]
+        return tie(jnp.concatenate(start) if len(start) > 1 else start[0], *after)
+
+    def column(self, packs, layer, *after):
+        start = self.start(packs, layer, *after)
+        return [start] + [lax.ppermute(start, "ctx", ring(4, steps)) for steps in (1, 3, 2)]
+
+    def pair_column(self, packs, layer, *after):
+        start = self.start(packs, layer, *after)
+        return jnp.stack([start, swap_zpair(start)])
+
+    def double_column(self, pair, *after):
+        pair = tie(pair, *after)
+        return pair, lax.ppermute(pair, "ctx", flip(4, 2))
+
+    def slices(self, column, rows):
+        return [part[rows] for part in column] if len(column) == 4 else [
+            part[k, rows] for part in column for k in (0, 1)
+        ]
+
+    def square(self, column, *after, rows=slice(None)):
+        column = jnp.stack(self.slices(tie(column, *after), rows))
         return column, swap_y(column), swap_x(column), swap_corner(column)
 
-    def assemble(self, square, rows, *after):
-        square = tie(square, *after)
-        pieces = square + tuple(swap_core(part) for part in square)
-        mixed = square[0].shape[1] < 2 * rows
+    def gather_square(self, square, *after):
+        pieces = jnp.stack(tie(square, *after))
+        return [pieces, swap_core(pieces)]
+
+    def first_phase(self, column, *after, rows=slice(None)):
+        column = self.slices(tie(column, *after), rows)
+        first, second = jnp.stack(column[:2]), jnp.stack(column[2:])
+        return first, swap_y(first), second, swap_x(second)
+
+    def second_phase(self, phase, *after):
+        phase = tie(phase, *after)
+        first, second = jnp.concatenate(phase[:2]), jnp.concatenate(phase[2:])
+        return first, swap_x(first), second, swap_y(second)
+
+    def early_core(self, phase):
+        return [swap_core(phase[0]), swap_core(phase[2])]
+
+    def gather_phase(self, phase, early, *after):
+        phase = tie(phase, *after)
+        late = [swap_core(phase[1]), swap_core(phase[3])]
+        return [*phase, early[0], late[0], early[1], late[1]]
+
+    def assemble(self, pieces, rows, doubled, *after):
+        pieces = tie(pieces, *after)
+        mixed = pieces[0].shape[-2] < 2 * rows
         if mixed:
             outs = (struct((D, MIXED), BF), struct((1, D), F32), struct((1, D), F32))
         else:
-            depth = 32 * (square[0].shape[1] - 2 * rows)
+            depth = 32 * (pieces[0].shape[-2] - 2 * rows)
             outs = (struct((D, MIXED), BF), struct((D, MIXED), BF), struct((depth, D), BF))
         weights = pl.pallas_call(
-            functools.partial(assemble_kernel, mixed),
+            functools.partial(assemble_kernel, mixed, doubled),
             out_shape=outs,
             in_specs=[pl.BlockSpec(memory_space=pltpu.SMEM)]
-            + [pl.BlockSpec(memory_space=pltpu.VMEM)] * 8,
+            + [pl.BlockSpec(memory_space=pltpu.VMEM)] * len(pieces),
             compiler_params=pltpu.CompilerParams(vmem_limit_bytes=24 * MIB),
             name="assemble",
         )(jnp.stack([self.section, self.z, self.y, self.core]), *pieces)
@@ -538,25 +633,51 @@
         return lax.dynamic_index_in_dim(value, y, 1, keepdims=False)
 
     def reduce_core(self, keep, send):
-        return keep, swap_core(send)
+        return keep, [swap_core(part) for part in send]
 
     def index(self):
         return jnp.stack([self.section, self.y, self.z])
 
-    def split_square(self, keep, received):
-        shape = (4,) + keep.shape[1:2] + (keep.shape[2] // 2,)
+    def split(self, kernel, shapes, groups, name):
+        rows = sum(keep[0].shape[1] for keep, _ in groups)
+        args = [part for pair in groups for parts in pair for part in parts]
         return vmem_call(
-            split_square_kernel,
-            [struct(shape, F32)] + [struct(shape, BF)] * 3,
-            (self.index(), keep, received),
+            functools.partial(kernel, [len(keep) for keep, _ in groups]),
+            [struct(shape[:-1] + (rows, shape[-1]), dtype) for shape, dtype in shapes],
+            (self.index(), *args),
             scalars=1,
-            limit=20,
-            name="split_square",
+            limit=24,
+            name=name,
         )
+
+    def split_square(self, *groups):
+        shapes = [((4, HALF // 2), F32)] + [((4, HALF // 2), BF)] * 3
+        return self.split(split_square_kernel, shapes, groups, "split_square")
 
     def move_square(self, parts):
         swaps = (swap_y, swap_x, swap_corner)
         return [parts[0]] + [swap(part) for swap, part in zip(swaps, parts[1:])]
+
+    def split_first(self, *groups):
+        shapes = [((2, 2, HALF // 2), F32), ((2, 2, HALF // 2), BF), ((2, HALF), F32), ((2, HALF), BF)]
+        return self.split(split_first_kernel, shapes, groups, "split_first")
+
+    def move_first(self, parts):
+        return [parts[0], swap_x(parts[1]), parts[2], swap_y(parts[3])]
+
+    def split_second(self, parts):
+        rows = parts[0].shape[2]
+        return vmem_call(
+            split_second_kernel,
+            [struct((4, rows, HALF // 2), F32)] + [struct((2, rows, HALF // 2), BF)] * 2,
+            (self.index(), *parts),
+            scalars=1,
+            limit=20,
+            name="split_second",
+        )
+
+    def move_second(self, parts):
+        return [parts[0], swap_y(parts[1]), swap_x(parts[2])]
 
     def split_column(self, parts):
         shape = parts[0].shape[1:]
@@ -565,7 +686,7 @@
             [struct(shape, F32)] + [struct(shape, BF)] * 3,
             (self.index(), *parts),
             scalars=1,
-            limit=16,
+            limit=20,
             name="split_column",
         )
 
@@ -574,8 +695,8 @@
             lax.ppermute(part, "ctx", ring(4, steps)) for steps, part in zip((1, 2, 3), parts[1:])
         ]
 
-    def total(self, parts):
-        return sum(part.astype(F32) for part in parts)
+    def total(self, parts, rows=slice(None)):
+        return sum(part[rows].astype(F32) for part in parts)
 
     def finish(self, first, second, rows):
         joined = []
@@ -643,13 +764,34 @@
             packs.append((own, tuple(swap_x(part) for part in own)))
         return packs
 
-    def column(self, pack, layer, *after):
-        return [jnp.where(self.section == layer, a, b) for a, b in zip(*pack)]
-
-    def square(self, column, *after):
+    def column(self, packs, layer, *after):
+        return [jnp.where(self.section == layer, a, b) for pack in packs for a, b in zip(*pack)]
+
+    def pair_column(self, packs, layer, *after):
+        return self.column(packs, layer)
+
+    def double_column(self, pair, *after):
+        return pair
+
+    def square(self, column, *after, rows=slice(None)):
+        if len(column) == 5:
+            return column[:2] if rows.start is None else column[2:]
         return column
 
-    def assemble(self, square, rows, *after):
+    first_phase = square
+
+    def gather_square(self, square, *after):
+        return square
+
+    second_phase = gather_square
+
+    def early_core(self, phase):
+        return ()
+
+    def gather_phase(self, phase, early, *after):
+        return phase
+
+    def assemble(self, square, rows, doubled, *after):
         axes = ("ctx", "fsdp")
         weights = [
             lax.all_gather(part, axes, axis=int(part.shape[0] == 2), tiled=True) for part in square
@@ -662,22 +804,22 @@
     def reduce_core(self, keep, send):
         return keep, send
 
-    def split_square(self, keep, send):
-        return [keep, send]
-
-    def move_square(self, parts):
-        return parts
-
-    def split_column(self, parts):
-        return parts
-
-    def move_column(self, parts):
-        return parts
-
-    def total(self, parts):
-        return parts
+    def split_square(self, *groups):
+        return groups
+
+    split_first = split_square
+
+    def move_square(self, groups):
+        return groups
+
+    move_first = split_second = move_second = split_column = move_column = move_square
+
+    def total(self, groups, rows=slice(None)):
+        return groups[rows.start is not None]
 
     def reduce(self, mixed, deep):
+        mixed, deep = ([jnp.concatenate(part) for part in pair] for pair in (mixed, deep))
+
         def columns(pair, first):
             return jnp.concatenate([part[:, first : first + 72] for part in pair], axis=2)
 
@@ -725,7 +867,7 @@
         limit=12,
         name="project",
     )
-    return queries, net.share_pairs(pairs)
+    return queries, pairs
 
 
 def attend_forward(net, source, queries, pieces, mixed, place):
@@ -761,22 +903,18 @@
 
 def mlp_backward(net, d_result, middle, mixed, gate, up, down, g_mlp):
     rows = middle.shape[0]
-    deep_shape = struct((8, 144 + down.shape[0] // 16, HALF), BF)
-    return vmem_call(
+    deep_rows = 144 + down.shape[0] // 16
+    shapes = [struct((4, deep_rows, HALF), BF)] * 4
+    outs = vmem_call(
         mlp_back_kernel,
-        (
-            deep_shape,
-            deep_shape,
-            struct((1, D), F32),
-            struct((rows, D), F32),
-            struct((rows, QW), BF),
-        ),
+        shapes + [struct((1, D), F32), struct((rows, D), F32), struct((rows, QW), BF)],
         (net.core.reshape(1), d_result, middle, mixed, gate, up, down, g_mlp),
         [pltpu.VMEM((rows, D), BF), pltpu.VMEM((rows, D), F32)],
         scalars=1,
         limit=28,
         name="mlp_back",
     )
+    return outs[:2], outs[2:4], *outs[4:]
 
 
 def attend_backward(net, d_attended, attended, log_total, queries, pieces, place):
@@ -810,7 +948,7 @@
 ):
     rows = source.shape[0]
     mixed_shape = struct((8, 80, HALF), BF)
-    return vmem_call(
+    d_source, keep, send = vmem_call(
         functools.partial(input_kernel, len(adds)),
         (struct((rows, D), BF), mixed_shape, mixed_shape),
         (
@@ -821,6 +959,7 @@
         limit=20,
         name="input",
     )
+    return d_source, [keep], [send]
 
 
 def shards(
@@ -841,81 +980,102 @@
     shard = w_query.shape[1]
 
     mixed_pack, deep_pack = net.pack(wide, w_down[0], jnp.stack([g_attn[0], g_mlp[0]]))
-    mixed_column = net.column(mixed_pack, 0)
-    deep_column = net.column(deep_pack, 0, mixed_column)
     source = lax.dynamic_index_in_dim(inputs[0], net.section, 0, keepdims=False)
-    source = net.spread(tie(source, mixed_column))
     d_result = lax.dynamic_index_in_dim(cotangent[0], net.section, 0, keepdims=False)
+    mixed_column = net.column([mixed_pack], 0)
     mixed_square = net.square(mixed_column)
-    deep_square = net.square(deep_column, mixed_square)
-    mixed_0, g_attn_0, g_mlp_0 = net.assemble(mixed_square, shard)
-
-    queries_0, pieces_0 = project(net, source, mixed_0, g_attn_0, place)
-    mixed_column = net.column(mixed_pack, 1, deep_column, queries_0)
-    deep_column = net.column(deep_pack, 1, deep_column, queries_0)
+    deep_column = net.column([deep_pack], 0, mixed_column)
+    source, d_result, place = tie((source, d_result, place), mixed_column)
+    mixed_rows = mixed_square[0].shape[-2]
+    mixed_pieces = net.gather_square(mixed_square)
+    deep_phase = net.first_phase(deep_column, mixed_square)
+    source = net.spread(tie(source, deep_column))
+    mixed_0, g_attn_0, g_mlp_0 = net.assemble(mixed_pieces, shard, False)
+
+    queries_0, pairs = project(net, source, mixed_0, g_attn_0, place)
+    deep_phase = net.second_phase(deep_phase, source)
+    pieces_0 = net.share_pairs(pairs)
+    column = net.pair_column([mixed_pack, deep_pack], 1, queries_0)
+    early = net.early_core(deep_phase)
+    column = net.double_column(column, pieces_0)
     attended_0, log_0, middle_0 = attend_forward(net, source, queries_0, pieces_0, mixed_0, place)
-    mixed_column, deep_column, deep_square = tie((mixed_column, deep_column, deep_square), middle_0)
-    mixed_square = net.square(mixed_column, deep_square)
-    deep_0 = net.assemble(deep_square, shard, mixed_column, deep_column)
+    middle_0, column, deep_phase, early = tie((middle_0, column, deep_phase, early))
+    mixed_square = net.square(column, rows=slice(None, mixed_rows))
+    deep_0 = net.assemble(net.gather_phase(deep_phase, early), shard, False)
+    d_result = net.spread(tie(d_result, deep_0))
     first = mlp_forward(middle_0, *deep_0, g_mlp_0)
-    deep_square = net.square(deep_column, mixed_square, first)
-    mixed_1, g_attn_1, g_mlp_1 = net.assemble(mixed_square, shard, first)
-
-    queries_1, pieces_1 = project(net, first, mixed_1, g_attn_1, place)
-    d_result = net.spread(tie(d_result, pieces_1))
+    first, mixed_square = tie((first, mixed_square))
+    mixed_pieces = net.gather_square(mixed_square)
+    deep_phase = net.first_phase(column, mixed_square, rows=slice(mixed_rows, None))
+    mixed_1, g_attn_1, g_mlp_1 = net.assemble(mixed_pieces, shard, True)
+
+    queries_1, pairs = project(net, first, mixed_1, g_attn_1, place)
+    pairs, d_result = tie((pairs, d_result))
+    pieces_1 = net.share_pairs(pairs)
+    deep_phase = net.second_phase(deep_phase, queries_1)
+    early = net.early_core(deep_phase)
     attended_1, log_1, middle_1 = attend_forward(net, first, queries_1, pieces_1, mixed_1, place)
-    deep_1 = net.assemble(deep_square, shard, middle_1)
+    middle_1, deep_phase, early = tie((middle_1, deep_phase, early))
+    deep_1 = net.assemble(net.gather_phase(deep_phase, early), shard, True)
 
     deep_keep, deep_send, gain_grad, d_middle, d_attended = mlp_backward(
         net, d_result, middle_1, mixed_1, *deep_1, g_mlp_1
     )
-    deep_sum_1 = net.reduce_core(deep_keep, deep_send)
+    deep_sum = net.reduce_core(deep_keep, deep_send)
     d_queries, *d_pairs = attend_backward(
         net, d_attended, attended_1, log_1, queries_1, pieces_1, place
     )
-    deep_sum_1 = net.split_square(*tie(deep_sum_1, d_pairs))
-    second = mlp_forward(tie(middle_1, deep_sum_1), *deep_1, g_mlp_1)
-    adds = tie(net.reduce_pairs(d_pairs), deep_sum_1, second)
+    d_queries, d_pairs, deep_sum = tie((d_queries, d_pairs, deep_sum))
+    deep_sum = net.split_first(deep_sum)
+    d_pairs = tie(d_pairs, deep_sum)
+    deep_sum = net.move_first(deep_sum)
+    second = mlp_forward(tie(middle_1, d_pairs), *deep_1, g_mlp_1)
+    adds, deep_sum = tie((net.reduce_pairs(d_pairs), deep_sum), second)
+    deep_sum = net.split_second(deep_sum)
+    adds = tie(adds, deep_sum)
+    deep_sum = net.move_second(deep_sum)
     d_first, mixed_keep, mixed_send = input_backward(
         net, first, attended_1, d_middle, d_queries, adds, gain_grad, mixed_1, g_attn_1, place
     )
-    deep_sum_1 = net.move_square(deep_sum_1)
-    mixed_sum_1 = net.reduce_core(mixed_keep, mixed_send)
-
-    deep_keep, deep_send, gain_grad, d_middle, d_attended = mlp_backward(
-        net, d_first, middle_0, mixed_0, *deep_0, g_mlp_0
-    )
-    deep_sum_0 = net.reduce_core(deep_keep, deep_send)
-    mixed_sum_1 = net.split_square(*tie(mixed_sum_1, d_attended))
-    deep_sum_1 = net.split_column(tie(deep_sum_1, d_attended))
-    d_attended = tie(d_attended, mixed_sum_1, deep_sum_1)
-    mixed_sum_1 = net.move_square(mixed_sum_1)
-    deep_sum_1 = net.move_column(deep_sum_1)
+    mixed_sum = net.reduce_core(mixed_keep, mixed_send)
+    second = net.unspread(tie(second, d_first))
+
+    outs = mlp_backward(net, d_first, middle_0, mixed_0, *deep_0, g_mlp_0)
+    outs, mixed_sum, deep_sum, second = tie((outs, mixed_sum, deep_sum, second))
+    deep_keep, deep_send, gain_grad, d_middle, d_attended = outs
+    deep_sum = net.split_column(deep_sum)
+    d_attended = tie(d_attended, deep_sum)
+    deep_sum_1 = net.move_column(deep_sum)
+    deep_sum = net.reduce_core(deep_keep, deep_send)
     d_queries, *d_pairs = attend_backward(
         net, d_attended, attended_0, log_0, queries_0, pieces_0, place
     )
-    deep_sum_0 = net.split_square(*tie(deep_sum_0, d_pairs))
-    mixed_sum_1 = net.split_column(tie(mixed_sum_1, d_pairs))
-    deep_sum_1 = net.total(tie(deep_sum_1, d_pairs))
-    second = net.unspread(tie(second, d_pairs))
-    adds = tie(net.reduce_pairs(d_pairs), deep_sum_0, mixed_sum_1, deep_sum_1)
+    d_queries, d_pairs, deep_sum, deep_sum_1 = tie((d_queries, d_pairs, deep_sum, deep_sum_1))
+    sums = net.split_first(mixed_sum, deep_sum)
+    d_pairs = tie(d_pairs, sums)
+    sums = net.move_first(sums)
+    deep_sum_1 = net.total(deep_sum_1)
+    adds, sums = tie((net.reduce_pairs(d_pairs), sums), deep_sum_1)
+    sums = net.split_second(sums)
+    adds = tie(adds, sums)
+    sums = net.move_second(sums)
     d_input, mixed_keep, mixed_send = input_backward(
         net, source, attended_0, d_middle, d_queries, adds, gain_grad, mixed_0, g_attn_0, place
     )
-    deep_sum_0 = net.move_square(deep_sum_0)
-    mixed_sum_1 = net.move_column(mixed_sum_1)
-
-    mixed_sum_0 = net.reduce_core(mixed_keep, mixed_send)
-    mixed_sum_1 = net.total(tie(mixed_sum_1, d_input))
-    deep_sum_0 = tie(deep_sum_0, d_input)
-    mixed_sum_0 = net.move_square(tie(net.split_square(*mixed_sum_0), deep_sum_0))
-    deep_sum_0 = net.move_column(net.split_column(deep_sum_0))
-    deep_sum_0 = net.total(tie(deep_sum_0, mixed_sum_0))
-    mixed_sum_0 = net.total(net.move_column(net.split_column(mixed_sum_0)))
+
+    mixed_sum = net.split_square(net.reduce_core(mixed_keep, mixed_send))
+    d_input = net.unspread(tie(d_input, mixed_sum))
+    mixed_sum, sums = tie((mixed_sum, sums))
+    mixed_sum = net.move_square(mixed_sum)
+    sums = net.move_column(net.split_column(sums))
+    mixed_sum = net.move_column(net.split_column(mixed_sum))
+    sums = tie(sums, mixed_sum)
+    mixed_sum_1 = net.total(sums, slice(None, 80))
+    deep_sum_0 = net.total(sums, slice(80, None))
+    mixed_sum_0 = net.total(mixed_sum)
     wide_grad, down_grad, gain_grads = net.finish(
         (mixed_sum_0, deep_sum_0), (mixed_sum_1, deep_sum_1), shard
     )
-    d_input = net.unspread(d_input)
     kept = jnp.where(net.section == 0, d_input, second)
     crossed = swap_x(jnp.where(net.section == 0, second, d_input))
     edges = jnp.stack(

time: 416 us -> 372 us (0.89)
  the two profiles are of different devices: /device:TPU:0 before, /device:TPU:9 now
where the time goes in v3:
time: 372 us; the launch traced here: 367 us
  Pallas kernels  113 us (30%)
  waiting for transfers between devices  112 us (30%)
  starting transfers between devices  93.8 us (25%)
  local copies, waits for them, and re-layouts  32.6 us (9%)
  other arithmetic  12.9 us (3%)
    pallas_call x20, Pallas kernels, vmem_call(): pl.pallas_call(kernel, out_shape=out_shape, in_specs=specs, scratch_shape...  103 us
    ppermute x16, waiting for transfers between devices, swap_x(): return lax.ppermute(value, 'section', flip(2, 1))  33.8 us
    ppermute x24, starting transfers between devices, swap_core(): return lax.ppermute(value, 'fsdp', flip(4, 1))  23.5 us
    unnamed x92, local copies, waits for them, and re-layouts  18.4 us
    ppermute x9, waiting for transfers between devices, move_column(): lax.ppermute(part, 'ctx', ring(4, steps))  18 us
    ppermute x16, starting transfers between devices, swap_x(): return lax.ppermute(value, 'section', flip(2, 1))  13.9 us
    ppermute x4, waiting for transfers between devices, spread(): lax.ppermute(block[k * half:(k + 1) * half], ('ctx', 'fsdp'), spread_pair...  13.7 us
    ppermute x9, starting transfers between devices, move_column(): lax.ppermute(part, 'ctx', ring(4, steps))  12.3 us
  transfers between devices with their start and end apart: 83, of which 35 were waited for; matrix products, arithmetic and copies ran while one was open for 9% of the time, Pallas kernels for 23%

profile of v3, /device:TPU:9, one launch (start us, length us, event | category | flops | bytes accessed | tf_op | source)
XLA Modules:
  0.0 366.8 jit_solution(8390247737421450281)
XLA Ops:
  26.6 3.3 collective-permute-start.8
  29.9 2.8 collective-permute-done.13
  36.1 5.5 %collective-permute-done.8 = bf16[120,768]{1,0:T(8,128)(2,1)S(1)} collective-permute-done((bf16[120,768]{1,0:T(8,128)(2,1)S(1)}, bf16[120,768]{1,0:T(8,128)(2,1)S(1)}, u32[]{:S(2)}, u32[]{:S(2)}) %collective-permute-start.8) | collective-permute-done | bytes 184352 | tf_op jit(solution)/shard_map/ppermute | solution.py:569
  41.6 5.4 %collective-permute-start.9 = (bf16[192,576]{1,0:T(8,128)(2,1)S(1)}, bf16[192,576]{1,0:T(8,128)(2,1)S(1)}, u32[]{:S(2)}, u32[]{:S(2)}) collective-permute-start(bf16[192,576]{1,0:T(8,128)(2,1)S(1)} %get-tuple-element.556), channel_id=1, source_target_pairs={{0,0},{1,8},{2,2},{3,10},{4,4},{5,12},{6,6},{7,14},{8,5},{9,13},{1... | collective-permute-start | bytes 663560 | tf_op jit(solution)/shard_map/ppermute | solution.py:512
  50.0 5.0 %collective-permute-done.9 = bf16[192,576]{1,0:T(8,128)(2,1)S(1)} collective-permute-done((bf16[192,576]{1,0:T(8,128)(2,1)S(1)}, bf16[192,576]{1,0:T(8,128)(2,1)S(1)}, u32[]{:S(2)}, u32[]{:S(2)}) %collective-permute-start.9) | collective-permute-done | bytes 221216 | tf_op jit(solution)/shard_map/ppermute | solution.py:512
  69.5 3.1 collective-permute-start.17
  84.1 11.1 %attend.2 = (f32[384,576]{1,0:T(8,128)S(1)}, f32[384,9]{1,0:T(8,128)S(1)}, f32[384,576]{1,0:T(8,128)S(1)}) custom-call(bf16[384,576]{1,0:T(8,128)(2,1)S(1)} %pad_maximum_fusion.2.source_ref, bf16[384,576]{1,0:T(8,128)(2,1)S(1)} %get-tuple-element.266.query_ref, s32[384,1]{1,0:T(8,128)S(1)} %copy.69.position_ref, s32[384,1]{1,0:T(8,128)S(1)} %copy.70.start_ref, ...), custom_call_target="tpu_custom_call" | custom-call | tf_op jit(solution)/shard_map/attend/pallas_call | solution.py:851
  96.0 4.6 %collective-permute-done.19 = bf16[2,160,768]{2,1,0:T(8,128)(2,1)} collective-permute-done((bf16[2,160,768]{2,1,0:T(8,128)(2,1)}, bf16[2,160,768]{2,1,0:T(8,128)(2,1)}, u32[]{:S(2)}, u32[]{:S(2)}) %collective-permute-start.19) | collective-permute-done | bytes 491552 | tf_op jit(solution)/shard_map/ppermute | solution.py:577
  106.2 4.1 %assemble.5 = (bf16[576,1536]{1,0:T(8,128)(2,1)S(1)}, bf16[576,1536]{1,0:T(8,128)(2,1)S(1)}, bf16[1536,576]{1,0:T(8,128)(2,1)S(1)}) custom-call(s32[4]{0:T(128)S(1)} %pad_add_fusion.1.index_ref, bf16[4,120,768]{2,1,0:T(8,128)(2,1)} %constant_dynamic-update-slice_fusion.refs_0_, bf16[4,120,768]{2,1,0:T(8,128)(2,1)} %collective-permute-done.22.refs_1_, ...), custom_call_target="tpu_custom_call" | custom-call | tf_op jit(solution)/shard_map/assemble/pallas_call | solution.py:618
  110.3 4.6 %mlp.2.source_ref = bf16[384,576]{1,0:T(8,128)(2,1)S(1)} custom-call(f32[384,576]{1,0:T(8,128)S(1)} %get-tuple-element.283.middle_ref, bf16[576,1536]{1,0:T(8,128)(2,1)S(1)} %get-tuple-element.302.gate_ref, bf16[576,1536]{1,0:T(8,128)(2,1)S(1)} %get-tuple-element.303.up_ref, bf16[1536,576]{1,0:T(8,128)(2,1)S(1)} %get-tuple-element.304.down_ref, ...), custom_call_target="tpu_custom_call" | custom-call | tf_op jit(solution)/shard_map/mlp/pallas_call | solution.py:851
  118.6 5.1 %collective-permute-start.32 = (bf16[192,576]{1,0:T(8,128)(2,1)S(1)}, bf16[192,576]{1,0:T(8,128)(2,1)S(1)}, u32[]{:S(2)}, u32[]{:S(2)}) collective-permute-start(bf16[192,576]{1,0:T(8,128)(2,1)S(1)} %get-tuple-element.552), channel_id=1, source_target_pairs={{0,0},{1,8},{2,2},{3,10},{4,4},{5,12},{6,6},{7,14},{8,5},{9,13},{1... | collective-permute-start | bytes 663560 | tf_op jit(solution)/shard_map/ppermute | solution.py:512
  128.5 3.4 collective-permute-done.32
  140.3 3.2 collective-permute-start.41
  149.8 11.2 %attend.3 = (f32[384,576]{1,0:T(8,128)S(1)}, f32[384,9]{1,0:T(8,128)S(1)}, f32[384,576]{1,0:T(8,128)S(1)}) custom-call(bf16[384,576]{1,0:T(8,128)(2,1)S(1)} %mlp.2.source_ref, bf16[384,576]{1,0:T(8,128)(2,1)S(1)} %get-tuple-element.323.query_ref, s32[384,1]{1,0:T(8,128)S(1)} %copy.69.position_ref, s32[384,1]{1,0:T(8,128)S(1)} %copy.70.start_ref, ...), custom_call_target="tpu_custom_call" | custom-call | tf_op jit(solution)/shard_map/attend/pallas_call | solution.py:851
  166.8 13.8 %mlp_back.2 = (bf16[4,240,768]{2,1,0:T(8,128)(2,1)S(1)}, bf16[4,240,768]{2,1,0:T(8,128)(2,1)S(1)}, bf16[4,240,768]{2,1,0:T(8,128)(2,1)}, bf16[4,240,768]{2,1,0:T...) custom-call(s32[1]{0:T(128)} %bitcast.core_ref, ...), custom_call_target="tpu_custom_call" | custom-call | tf_op jit(solution)/shard_map/mlp_back/pallas_call | solution.py:851
  184.4 15.1 %attend_back.2 = (f32[384,576]{1,0:T(8,128)S(1)}, bf16[2,384,384]{2,1,0:T(8,128)(2,1)S(1)}, bf16[2,384,384]{2,1,0:T(8,128)(2,1)S(1)}) custom-call(bf16[384,576]{1,0:T(8,128)(2,1)S(1)} %get-tuple-element.361.d_out_ref, f32[384,576]{1,0:T(8,128)S(1)} %get-tuple-element.328.attended_ref, f32[384,9]{1,0:T(8,128)S(1)} %get-tuple-element.362.log_ref, ...), custom_call_target="tpu_custom_call" | custom-call | tf_op jit(solution)/shard_map/attend_back/pallas_call | solution.py:851
  203.8 4.6 %mlp.3 = bf16[384,576]{1,0:T(8,128)(2,1)S(1)} custom-call(f32[384,576]{1,0:T(8,128)S(1)} %get-tuple-element.384.middle_ref, bf16[576,1536]{1,0:T(8,128)(2,1)S(1)} %get-tuple-element.356.gate_ref, bf16[576,1536]{1,0:T(8,128)(2,1)S(1)} %get-tuple-element.357.up_ref, bf16[1536,576]{1,0:T(8,128)(2,1)S(1)} %get-tuple-element.358.down_ref, ...), custom_call_target="tpu_custom_call" | custom-call | tf_op jit(solution)/shard_map/mlp/pallas_call | solution.py:851
  208.5 10.6 %collective-permute-done.49.moved_ref = bf16[2,2,240,384]{3,2,1,0:T(8,128)(2,1)S(1)} collective-permute-done((bf16[2,2,240,384]{3,2,1,0:T(8,128)(2,1)S(1)}, bf16[2,2,240,384]{3,2,1,0:T(8,128)(2,1)S(1)}, u32[]{:S(2)}, u32[]{:S(2)}) %collective-permute-start.49) | collective-permute-done | bytes 737312 | tf_op jit(solution)/shard_map/ppermute | solution.py:66
  220.9 3.0 input.2
  227.5 3.1 collective-permute-start.54
  230.6 12.1 %mlp_back.3 = (bf16[4,240,768]{2,1,0:T(8,128)(2,1)S(1)}, bf16[4,240,768]{2,1,0:T(8,128)(2,1)S(1)}, bf16[4,240,768]{2,1,0:T(8,128)(2,1)S(1)}, bf16[4,240,768]{2,1...) custom-call(s32[1]{0:T(128)} %bitcast.core_ref, ...), custom_call_target="tpu_custom_call" | custom-call | tf_op jit(solution)/shard_map/mlp_back/pallas_call | solution.py:851
  248.7 14.9 %attend_back.3 = (f32[384,576]{1,0:T(8,128)S(1)}, bf16[2,384,384]{2,1,0:T(8,128)(2,1)S(1)}, bf16[2,384,384]{2,1,0:T(8,128)(2,1)S(1)}) custom-call(bf16[384,576]{1,0:T(8,128)(2,1)S(1)} %get-tuple-element.418.d_out_ref, f32[384,576]{1,0:T(8,128)S(1)} %get-tuple-element.271.attended_ref, f32[384,9]{1,0:T(8,128)S(1)} %copy-done.19, ...), custom_call_target="tpu_custom_call" | custom-call | tf_op jit(solution)/shard_map/attend_back/pallas_call | solution.py:851
  270.0 7.1 %collective-permute-done.62.refs_2_ = bf16[384,384]{1,0:T(8,128)(2,1)S(1)} collective-permute-done((bf16[384,384]{1,0:T(8,128)(2,1)S(1)}, bf16[384,384]{1,0:T(8,128)(2,1)S(1)}, u32[]{:S(2)}, u32[]{:S(2)}) %collective-permute-start.62) | collective-permute-done | bytes 294944 | tf_op jit(solution)/shard_map/ppermute | solution.py:62
  277.1 13.0 %collective-permute-done.63.moved_ref = bf16[2,2,320,384]{3,2,1,0:T(8,128)(2,1)S(1)} collective-permute-done((bf16[2,2,320,384]{3,2,1,0:T(8,128)(2,1)S(1)}, bf16[2,2,320,384]{3,2,1,0:T(8,128)(2,1)S(1)}, u32[]{:S(2)}, u32[]{:S(2)}) %collective-permute-start.63) | collective-permute-done | bytes 983072 | tf_op jit(solution)/shard_map/ppermute | solution.py:66
  291.8 3.0 input.3
  299.8 3.0 collective-permute-start.66
  303.1 5.8 %collective-permute-done.69.refs_1_ = bf16[2,320,384]{2,1,0:T(8,128)(2,1)S(1)} collective-permute-done((bf16[2,320,384]{2,1,0:T(8,128)(2,1)S(1)}, bf16[2,320,384]{2,1,0:T(8,128)(2,1)S(1)}, u32[]{:S(2)}, u32[]{:S(2)}) %collective-permute-start.69) | collective-permute-done | bytes 491552 | tf_op jit(solution)/shard_map/ppermute | solution.py:58
  314.5 4.7 %collective-permute-start.78 = (bf16[320,384]{1,0:T(8,128)(2,1)S(1)}, bf16[320,384]{1,0:T(8,128)(2,1)S(1)}, u32[]{:S(2)}, u32[]{:S(2)}) collective-permute-start(bf16[320,384]{1,0:T(8,128)(2,1)S(1)} %get-tuple-element.482), channel_id=1, source_target_pairs={{0,8},{4,12},{8,0},{12,4},{1,9},{5,13},{9,1},{13,5},{2,10},{6,14},... | collective-permute-start | bytes 737288 | tf_op jit(solution)/shard_map/ppermute | solution.py:695
  326.2 12.0 %collective-permute-done.78 = bf16[320,384]{1,0:T(8,128)(2,1)S(1)} collective-permute-done((bf16[320,384]{1,0:T(8,128)(2,1)S(1)}, bf16[320,384]{1,0:T(8,128)(2,1)S(1)}, u32[]{:S(2)}, u32[]{:S(2)}) %collective-permute-start.78) | collective-permute-done | bytes 245792 | tf_op jit(solution)/shard_map/ppermute | solution.py:695
  338.5 4.2 %collective-permute-done.79 = bf16[320,384]{1,0:T(8,128)(2,1)S(1)} collective-permute-done((bf16[320,384]{1,0:T(8,128)(2,1)S(1)}, bf16[320,384]{1,0:T(8,128)(2,1)S(1)}, u32[]{:S(2)}, u32[]{:S(2)}) %collective-permute-start.79) | collective-permute-done | bytes 245792 | tf_op jit(solution)/shard_map/ppermute | solution.py:695
  346.4 5.9 %collective-permute-done.80 = bf16[80,384]{1,0:T(8,128)(2,1)S(1)} collective-permute-done((bf16[80,384]{1,0:T(8,128)(2,1)S(1)}, bf16[80,384]{1,0:T(8,128)(2,1)S(1)}, u32[]{:S(2)}, u32[]{:S(2)}) %collective-permute-start.80) | collective-permute-done | bytes 61472 | tf_op jit(solution)/shard_map/ppermute | solution.py:66
  352.4 3.9 %collective-permute-done.81 = bf16[240,384]{1,0:T(8,128)(2,1)} collective-permute-done((bf16[240,384]{1,0:T(8,128)(2,1)}, bf16[240,384]{1,0:T(8,128)(2,1)}, u32[]{:S(2)}, u32[]{:S(2)}) %collective-permute-start.81) | collective-permute-done | bytes 184352 | tf_op jit(solution)/shard_map/ppermute | solution.py:66
  (334 shorter events, 152.3 us)
Async XLA Ops:
  32.9 25.2 %collective-permute-start.14 = (bf16[4,4,40,768]{3,2,1,0:T(8,128)(2,1)S(1)}, bf16[4,4,40,768]{3,2,1,0:T(8,128)(2,1)S(1)}, u32[]{:S(2)}, u32[]{:S(2)}) collective-permute-start(bf16[4,4,40,768]{3,2,1,0:T(8,128)(2,1)S(1)} %pad_maximum_fusion.refs_0_), channel_id=1, source_target_pairs={{0,1},{1,0},{2,3},{3,2},{4,5},{5,4},{6,7},{7,6},{8,9},{9,8},{10,11... | collective-permute-start | bytes 2949128 | tf_op jit(solution)/shard_map/ppermute | solution.py:54
  66.0 30.0 %collective-permute-start.22 = (bf16[4,120,768]{2,1,0:T(8,128)(2,1)}, bf16[4,120,768]{2,1,0:T(8,128)(2,1)}, u32[]{:S(2)}, u32[]{:S(2)}) collective-permute-start(bf16[4,120,768]{2,1,0:T(8,128)(2,1)} %constant_dynamic-update-slice_fusion.refs_0_), channel_id=1, source_target_pairs={{0,16},{16,0},{1,17},{17,1},{2,18},{18,2},{3,19},{19,3},{4,20},{20... | collective-permute-start | bytes 2211848 | tf_op jit(solution)/shard_map/ppermute | solution.py:66
  67.2 28.8 %collective-permute-start.24 = (bf16[4,120,768]{2,1,0:T(8,128)(2,1)}, bf16[4,120,768]{2,1,0:T(8,128)(2,1)}, u32[]{:S(2)}, u32[]{:S(2)}) collective-permute-start(bf16[4,120,768]{2,1,0:T(8,128)(2,1)} %constant_dynamic-update-slice_fusion.refs_0_), channel_id=1, source_target_pairs={{0,1},{1,0},{2,3},{3,2},{4,5},{5,4},{6,7},{7,6},{8,9},{9,8},{10,11... | collective-permute-start | bytes 2211848 | tf_op jit(solution)/shard_map/ppermute | solution.py:54
  74.9 21.0 %collective-permute-start.23 = (bf16[4,120,768]{2,1,0:T(8,128)(2,1)}, bf16[4,120,768]{2,1,0:T(8,128)(2,1)}, u32[]{:S(2)}, u32[]{:S(2)}) collective-permute-start(bf16[4,120,768]{2,1,0:T(8,128)(2,1)} %constant_dynamic-update-slice_fusion.2.refs_2_), channel_id=1, source_target_pairs={{0,2},{1,3},{2,0},{3,1},{4,6},{5,7},{6,4},{7,5},{8,10},{9,11},{10,... | collective-permute-start | bytes 2211848 | tf_op jit(solution)/shard_map/ppermute | solution.py:58
  75.2 20.8 %collective-permute-start.25 = (bf16[4,120,768]{2,1,0:T(8,128)(2,1)}, bf16[4,120,768]{2,1,0:T(8,128)(2,1)}, u32[]{:S(2)}, u32[]{:S(2)}) collective-permute-start(bf16[4,120,768]{2,1,0:T(8,128)(2,1)} %constant_dynamic-update-slice_fusion.2.refs_2_), channel_id=1, source_target_pairs={{0,1},{1,0},{2,3},{3,2},{4,5},{5,4},{6,7},{7,6},{8,9},{9,8},{10,11... | collective-permute-start | bytes 2211848 | tf_op jit(solution)/shard_map/ppermute | solution.py:54
  78.7 21.9 %collective-permute-start.19 = (bf16[2,160,768]{2,1,0:T(8,128)(2,1)}, bf16[2,160,768]{2,1,0:T(8,128)(2,1)}, u32[]{:S(2)}, u32[]{:S(2)}) collective-permute-start(bf16[2,160,768]{2,1,0:T(8,128)(2,1)} %pad_maximum_fusion.3), channel_id=1, source_target_pairs={{0,8},{4,12},{8,0},{12,4},{1,9},{5,13},{9,1},{13,5},{2,10},{6,14},... | collective-permute-start | bytes 1474568 | tf_op jit(solution)/shard_map/ppermute | solution.py:577
  116.8 17.9 %collective-permute-start.31 = (bf16[4,4,40,768]{3,2,1,0:T(8,128)(2,1)S(1)}, bf16[4,4,40,768]{3,2,1,0:T(8,128)(2,1)S(1)}, u32[]{:S(2)}, u32[]{:S(2)}) collective-permute-start(bf16[4,4,40,768]{3,2,1,0:T(8,128)(2,1)S(1)} %pad_maximum_fusion.1.refs_0_), channel_id=1, source_target_pairs={{0,1},{1,0},{2,3},{3,2},{4,5},{5,4},{6,7},{7,6},{8,9},{9,8},{10,11... | collective-permute-start | bytes 2949128 | tf_op jit(solution)/shard_map/ppermute | solution.py:54
  137.7 23.3 %collective-permute-start.39 = (bf16[4,120,768]{2,1,0:T(8,128)(2,1)S(1)}, bf16[4,120,768]{2,1,0:T(8,128)(2,1)S(1)}, u32[]{:S(2)}, u32[]{:S(2)}) collective-permute-start(bf16[4,120,768]{2,1,0:T(8,128)(2,1)S(1)} %constant_dynamic-update-slice_fusion.4.refs_0_), channel_id=1, source_target_pairs={{0,16},{16,0},{1,17},{17,1},{2,18},{18,2},{3,19},{19,3},{4,20},{20... | collective-permute-start | bytes 2211848 | tf_op jit(solution)/shard_map/ppermute | solution.py:66
  139.0 22.0 %collective-permute-start.40 = (bf16[4,120,768]{2,1,0:T(8,128)(2,1)S(1)}, bf16[4,120,768]{2,1,0:T(8,128)(2,1)S(1)}, u32[]{:S(2)}, u32[]{:S(2)}) collective-permute-start(bf16[4,120,768]{2,1,0:T(8,128)(2,1)S(1)} %constant_dynamic-update-slice_fusion.6.refs_2_), channel_id=1, source_target_pairs={{0,2},{1,3},{2,0},{3,1},{4,6},{5,7},{6,4},{7,5},{8,10},{9,11},{10,... | collective-permute-start | bytes 2211848 | tf_op jit(solution)/shard_map/ppermute | solution.py:58
  140.3 20.7 %collective-permute-start.41 = (bf16[4,120,768]{2,1,0:T(8,128)(2,1)S(1)}, bf16[4,120,768]{2,1,0:T(8,128)(2,1)S(1)}, u32[]{:S(2)}, u32[]{:S(2)}) collective-permute-start(bf16[4,120,768]{2,1,0:T(8,128)(2,1)S(1)} %constant_dynamic-update-slice_fusion.4.refs_0_), channel_id=1, source_target_pairs={{0,1},{1,0},{2,3},{3,2},{4,5},{5,4},{6,7},{7,6},{8,9},{9,8},{10,11... | collective-permute-start | bytes 2211848 | tf_op jit(solution)/shard_map/ppermute | solution.py:54
  143.5 17.5 %collective-permute-start.42 = (bf16[4,120,768]{2,1,0:T(8,128)(2,1)S(1)}, bf16[4,120,768]{2,1,0:T(8,128)(2,1)S(1)}, u32[]{:S(2)}, u32[]{:S(2)}) collective-permute-start(bf16[4,120,768]{2,1,0:T(8,128)(2,1)S(1)} %constant_dynamic-update-slice_fusion.6.refs_2_), channel_id=1, source_target_pairs={{0,1},{1,0},{2,3},{3,2},{4,5},{5,4},{6,7},{7,6},{8,9},{9,8},{10,11... | collective-permute-start | bytes 2211848 | tf_op jit(solution)/shard_map/ppermute | solution.py:54
  183.8 15.7 %collective-permute-start.45 = (bf16[4,240,768]{2,1,0:T(8,128)(2,1)}, bf16[4,240,768]{2,1,0:T(8,128)(2,1)S(1)}, u32[]{:S(2)}, u32[]{:S(2)}) collective-permute-start(bf16[4,240,768]{2,1,0:T(8,128)(2,1)} %get-tuple-element.368), channel_id=1, source_target_pairs={{0,1},{1,0},{2,3},{3,2},{4,5},{5,4},{6,7},{7,6},{8,9},{9,8},{10,11... | collective-permute-start | bytes 4423688 | tf_op jit(solution)/shard_map/ppermute | solution.py:54
  201.2 17.9 %collective-permute-start.49 = (bf16[2,2,240,384]{3,2,1,0:T(8,128)(2,1)S(1)}, bf16[2,2,240,384]{3,2,1,0:T(8,128)(2,1)S(1)}, u32[]{:S(2)}, u32[]{:S(2)}) collective-permute-start(bf16[2,2,240,384]{3,2,1,0:T(8,128)(2,1)S(1)} %get-tuple-element.379), channel_id=1, source_target_pairs={{0,16},{16,0},{1,17},{17,1},{2,18},{18,2},{3,19},{19,3},{4,20},{20... | collective-permute-start | bytes 2211848 | tf_op jit(solution)/shard_map/ppermute | solution.py:66
  202.4 17.6 %collective-permute-start.50 = (bf16[2,240,768]{2,1,0:T(8,128)(2,1)S(1)}, bf16[2,240,768]{2,1,0:T(8,128)(2,1)S(1)}, u32[]{:S(2)}, u32[]{:S(2)}) collective-permute-start(bf16[2,240,768]{2,1,0:T(8,128)(2,1)S(1)} %get-tuple-element.381), channel_id=1, source_target_pairs={{0,2},{1,3},{2,0},{3,1},{4,6},{5,7},{6,4},{7,5},{8,10},{9,11},{10,... | collective-permute-start | bytes 2211848 | tf_op jit(solution)/shard_map/ppermute | solution.py:58
  203.7 16.3 %collective-permute-start.48 = (bf16[384,384]{1,0:T(8,128)(2,1)S(1)}, bf16[384,384]{1,0:T(8,128)(2,1)S(1)}, u32[]{:S(2)}, u32[]{:S(2)}) collective-permute-start(bf16[384,384]{1,0:T(8,128)(2,1)S(1)} %fusion), channel_id=1, source_target_pairs={{0,4},{4,0},{8,12},{12,8},{1,5},{5,1},{9,13},{13,9},{2,6},{6,2},{1... | collective-permute-start | bytes 884744 | tf_op jit(solution)/shard_map/ppermute | solution.py:62
  223.9 19.7 %collective-permute-start.51 = (bf16[8,80,768]{2,1,0:T(8,128)(2,1)S(1)}, bf16[8,80,768]{2,1,0:T(8,128)(2,1)S(1)}, u32[]{:S(2)}, u32[]{:S(2)}) collective-permute-start(bf16[8,80,768]{2,1,0:T(8,128)(2,1)S(1)} %get-tuple-element.407), channel_id=1, source_target_pairs={{0,1},{1,0},{2,3},{3,2},{4,5},{5,4},{6,7},{7,6},{8,9},{9,8},{10,11... | collective-permute-start | bytes 2949128 | tf_op jit(solution)/shard_map/ppermute | solution.py:54
  225.2 18.4 %collective-permute-start.52 = (bf16[2,240,384]{2,1,0:T(8,128)(2,1)S(1)}, bf16[2,240,384]{2,1,0:T(8,128)(2,1)S(1)}, u32[]{:S(2)}, u32[]{:S(2)}) collective-permute-start(bf16[2,240,384]{2,1,0:T(8,128)(2,1)S(1)} %get-tuple-element.393), channel_id=1, source_target_pairs={{0,2},{1,3},{2,0},{3,1},{4,6},{5,7},{6,4},{7,5},{8,10},{9,11},{10,... | collective-permute-start | bytes 1105928 | tf_op jit(solution)/shard_map/ppermute | solution.py:58
  226.5 17.1 %collective-permute-start.53 = (bf16[2,240,384]{2,1,0:T(8,128)(2,1)S(1)}, bf16[2,240,384]{2,1,0:T(8,128)(2,1)S(1)}, u32[]{:S(2)}, u32[]{:S(2)}) collective-permute-start(bf16[2,240,384]{2,1,0:T(8,128)(2,1)S(1)} %get-tuple-element.394), channel_id=1, source_target_pairs={{0,16},{16,0},{1,17},{17,1},{2,18},{18,2},{3,19},{19,3},{4,20},{20... | collective-permute-start | bytes 1105928 | tf_op jit(solution)/shard_map/ppermute | solution.py:66
  226.8 15.9 %collective-permute-start.55 = (bf16[192,576]{1,0:T(8,128)(2,1)S(1)}, bf16[192,576]{1,0:T(8,128)(2,1)S(1)}, u32[]{:S(2)}, u32[]{:S(2)}) collective-permute-start(bf16[192,576]{1,0:T(8,128)(2,1)S(1)} %get-tuple-element.549), channel_id=1, source_target_pairs={{1,0},{9,1},{3,2},{11,3},{5,4},{13,5},{7,6},{15,7},{4,8},{12,9},{6... | collective-permute-start | bytes 663560 | tf_op jit(solution)/shard_map/ppermute | solution.py:524
  243.6 20.5 %collective-permute-start.56 = (bf16[4,240,768]{2,1,0:T(8,128)(2,1)S(1)}, bf16[4,240,768]{2,1,0:T(8,128)(2,1)S(1)}, u32[]{:S(2)}, u32[]{:S(2)}) collective-permute-start(bf16[4,240,768]{2,1,0:T(8,128)(2,1)S(1)} %get-tuple-element.425), channel_id=1, source_target_pairs={{0,1},{1,0},{2,3},{3,2},{4,5},{5,4},{6,7},{7,6},{8,9},{9,8},{10,11... | collective-permute-start | bytes 4423688 | tf_op jit(solution)/shard_map/ppermute | solution.py:54
  243.7 20.5 %collective-permute-start.57 = (bf16[4,240,768]{2,1,0:T(8,128)(2,1)S(1)}, bf16[4,240,768]{2,1,0:T(8,128)(2,1)S(1)}, u32[]{:S(2)}, u32[]{:S(2)}) collective-permute-start(bf16[4,240,768]{2,1,0:T(8,128)(2,1)S(1)} %get-tuple-element.426), channel_id=1, source_target_pairs={{0,1},{1,0},{2,3},{3,2},{4,5},{5,4},{6,7},{7,6},{8,9},{9,8},{10,11... | collective-permute-start | bytes 4423688 | tf_op jit(solution)/shard_map/ppermute | solution.py:54
  245.0 18.7 %collective-permute-start.58 = (bf16[240,384]{1,0:T(8,128)(2,1)S(1)}, bf16[240,384]{1,0:T(8,128)(2,1)S(1)}, u32[]{:S(2)}, u32[]{:S(2)}) collective-permute-start(bf16[240,384]{1,0:T(8,128)(2,1)S(1)} %get-tuple-element.415), channel_id=1, source_target_pairs={{0,4},{4,8},{8,12},{12,0},{1,5},{5,9},{9,13},{13,1},{2,6},{6,10},{... | collective-permute-start | bytes 552968 | tf_op jit(solution)/shard_map/ppermute | solution.py:695
  246.0 17.6 %collective-permute-start.59 = (bf16[240,384]{1,0:T(8,128)(2,1)S(1)}, bf16[240,384]{1,0:T(8,128)(2,1)S(1)}, u32[]{:S(2)}, u32[]{:S(2)}) collective-permute-start(bf16[240,384]{1,0:T(8,128)(2,1)S(1)} %get-tuple-element.416), channel_id=1, source_target_pairs={{0,8},{4,12},{8,0},{12,4},{1,9},{5,13},{9,1},{13,5},{2,10},{6,14},... | collective-permute-start | bytes 552968 | tf_op jit(solution)/shard_map/ppermute | solution.py:695
  248.3 15.8 %collective-permute-start.60 = (bf16[240,384]{1,0:T(8,128)(2,1)S(1)}, bf16[240,384]{1,0:T(8,128)(2,1)S(1)}, u32[]{:S(2)}, u32[]{:S(2)}) collective-permute-start(bf16[240,384]{1,0:T(8,128)(2,1)S(1)} %get-tuple-element.417), channel_id=1, source_target_pairs={{0,12},{4,0},{8,4},{12,8},{1,13},{5,1},{9,5},{13,9},{2,14},{6,2},{... | collective-permute-start | bytes 552968 | tf_op jit(solution)/shard_map/ppermute | solution.py:695
  266.7 23.3 %collective-permute-start.63 = (bf16[2,2,320,384]{3,2,1,0:T(8,128)(2,1)S(1)}, bf16[2,2,320,384]{3,2,1,0:T(8,128)(2,1)S(1)}, u32[]{:S(2)}, u32[]{:S(2)}) collective-permute-start(bf16[2,2,320,384]{3,2,1,0:T(8,128)(2,1)S(1)} %get-tuple-element.438), channel_id=1, source_target_pairs={{0,16},{16,0},{1,17},{17,1},{2,18},{18,2},{3,19},{19,3},{4,20},{20... | collective-permute-start | bytes 2949128 | tf_op jit(solution)/shard_map/ppermute | solution.py:66
  267.9 23.0 %collective-permute-start.64 = (bf16[2,320,768]{2,1,0:T(8,128)(2,1)S(1)}, bf16[2,320,768]{2,1,0:T(8,128)(2,1)S(1)}, u32[]{:S(2)}, u32[]{:S(2)}) collective-permute-start(bf16[2,320,768]{2,1,0:T(8,128)(2,1)S(1)} %get-tuple-element.440), channel_id=1, source_target_pairs={{0,2},{1,3},{2,0},{3,1},{4,6},{5,7},{6,4},{7,5},{8,10},{9,11},{10,... | collective-permute-start | bytes 2949128 | tf_op jit(solution)/shard_map/ppermute | solution.py:58
  314.5 23.7 %collective-permute-start.78 = (bf16[320,384]{1,0:T(8,128)(2,1)S(1)}, bf16[320,384]{1,0:T(8,128)(2,1)S(1)}, u32[]{:S(2)}, u32[]{:S(2)}) collective-permute-start(bf16[320,384]{1,0:T(8,128)(2,1)S(1)} %get-tuple-element.482), channel_id=1, source_target_pairs={{0,8},{4,12},{8,0},{12,4},{1,9},{5,13},{9,1},{13,5},{2,10},{6,14},... | collective-permute-start | bytes 737288 | tf_op jit(solution)/shard_map/ppermute | solution.py:695
  320.2 22.4 %collective-permute-start.79 = (bf16[320,384]{1,0:T(8,128)(2,1)S(1)}, bf16[320,384]{1,0:T(8,128)(2,1)S(1)}, u32[]{:S(2)}, u32[]{:S(2)}) collective-permute-start(bf16[320,384]{1,0:T(8,128)(2,1)S(1)} %get-tuple-element.483), channel_id=1, source_target_pairs={{0,12},{4,0},{8,4},{12,8},{1,13},{5,1},{9,5},{13,9},{2,14},{6,2},{... | collective-permute-start | bytes 737288 | tf_op jit(solution)/shard_map/ppermute | solution.py:695
  322.1 21.9 %collective-permute-start.76 = (bf16[80,384]{1,0:T(8,128)(2,1)S(1)}, bf16[80,384]{1,0:T(8,128)(2,1)S(1)}, u32[]{:S(2)}, u32[]{:S(2)}) collective-permute-start(bf16[80,384]{1,0:T(8,128)(2,1)S(1)} %get-tuple-element.476), channel_id=1, source_target_pairs={{0,12},{4,0},{8,4},{12,8},{1,13},{5,1},{9,5},{13,9},{2,14},{6,2},{... | collective-permute-start | bytes 184328 | tf_op jit(solution)/shard_map/ppermute | solution.py:695
  322.9 21.1 %collective-permute-start.75 = (bf16[80,384]{1,0:T(8,128)(2,1)S(1)}, bf16[80,384]{1,0:T(8,128)(2,1)S(1)}, u32[]{:S(2)}, u32[]{:S(2)}) collective-permute-start(bf16[80,384]{1,0:T(8,128)(2,1)S(1)} %get-tuple-element.475), channel_id=1, source_target_pairs={{0,8},{4,12},{8,0},{12,4},{1,9},{5,13},{9,1},{13,5},{2,10},{6,14},... | collective-permute-start | bytes 184328 | tf_op jit(solution)/shard_map/ppermute | solution.py:695
  325.1 18.9 %collective-permute-start.74 = (bf16[80,384]{1,0:T(8,128)(2,1)S(1)}, bf16[80,384]{1,0:T(8,128)(2,1)S(1)}, u32[]{:S(2)}, u32[]{:S(2)}) collective-permute-start(bf16[80,384]{1,0:T(8,128)(2,1)S(1)} %get-tuple-element.474), channel_id=1, source_target_pairs={{0,4},{4,8},{8,12},{12,0},{1,5},{5,9},{9,13},{13,1},{2,6},{6,10},{... | collective-permute-start | bytes 184328 | tf_op jit(solution)/shard_map/ppermute | solution.py:695
  338.2 26.4 %collective-permute-start.68 = (bf16[384,576]{1,0:T(8,128)(2,1)S(1)}, bf16[384,576]{1,0:T(8,128)(2,1)S(1)}, u32[]{:S(2)}, u32[]{:S(2)}) collective-permute-start(bf16[384,576]{1,0:T(8,128)(2,1)S(1)} %broadcast_select_fusion), channel_id=1, source_target_pairs={{0,16},{16,0},{1,17},{17,1},{2,18},{18,2},{3,19},{19,3},{4,20},{20... | collective-permute-start | bytes 1327112 | tf_op jit(solution)/shard_map/ppermute | solution.py:66
  (89 other events, 712.0 us)

commit v4 on v3

--- a/solution.py
+++ b/solution.py
@@ -548,17 +548,17 @@
         return [near[0], received[0], swap_zpair(along.astype(BF))]
 
 
-    def pack(self, wide, down, gains):
-        rows = wide.shape[1]
-        gains = jnp.pad(gains, ((0, 2), (0, MIXED - rows)))
-        mixed = jnp.concatenate([wide[0], gains], axis=0)
+    def halves(self, part):
+        return self.lanes(part, self.section), swap_x(self.lanes(part, 1 - self.section))
+
+    def pack_mixed(self, mixed, gains):
+        gains = jnp.pad(gains, ((0, 2), (0, MIXED - mixed.shape[0])))
+        return self.halves(jnp.concatenate([mixed, gains], axis=0))
+
+    def pack_deep(self, gate, up, down):
         half = down.shape[0] // 2
         down = jnp.pad(jnp.stack([down[:half], down[half:]], axis=1), ((0, 0), (0, 0), (0, HALF - D)))
-        deep = jnp.concatenate([wide[1], wide[2], down.reshape(half, MIXED)], axis=0)
-        return [
-            (self.lanes(part, self.section), swap_x(self.lanes(part, 1 - self.section)))
-            for part in (mixed, deep)
-        ]
+        return self.halves(jnp.concatenate([gate, up, down.reshape(half, MIXED)], axis=0))
 
     def start(self, packs, layer, *after):
         start = [jnp.where(self.section == layer, *pack) for pack in packs]
@@ -620,7 +620,7 @@
             out_shape=outs,
             in_specs=[pl.BlockSpec(memory_space=pltpu.SMEM)]
             + [pl.BlockSpec(memory_space=pltpu.VMEM)] * len(pieces),
-            compiler_params=pltpu.CompilerParams(vmem_limit_bytes=24 * MIB),
+            compiler_params=pltpu.CompilerParams(vmem_limit_bytes=20 * MIB),
             name="assemble",
         )(jnp.stack([self.section, self.z, self.y, self.core]), *pieces)
         return weights
@@ -646,7 +646,7 @@
             [struct(shape[:-1] + (rows, shape[-1]), dtype) for shape, dtype in shapes],
             (self.index(), *args),
             scalars=1,
-            limit=24,
+            limit=20,
             name=name,
         )
 
@@ -698,21 +698,13 @@
     def total(self, parts, rows=slice(None)):
         return sum(part[rows].astype(F32) for part in parts)
 
-    def finish(self, first, second, rows):
-        joined = []
-        for a, b in zip(first, second):
-            own = jnp.where(self.section == 0, a, b)
-            other = swap_x(jnp.where(self.section == 0, b, a).astype(BF)).astype(F32)
-            joined.append(
-                jnp.concatenate(
-                    [
-                        jnp.where(self.section == 0, own, other),
-                        jnp.where(self.section == 0, other, own),
-                    ],
-                    axis=1,
-                )
-            )
-        mixed, deep = joined
+    def cross(self, first, second):
+        own = jnp.where(self.section == 0, first, second)
+        other = swap_x(jnp.where(self.section == 0, second, first).astype(BF)).astype(F32)
+        left = jnp.where(self.section == 0, own, other)
+        return jnp.concatenate([left, jnp.where(self.section == 0, other, own)], axis=1)
+
+    def finish(self, mixed, deep, rows):
         wide = jnp.stack([mixed[: 2 * rows], deep[: 2 * rows], deep[2 * rows : 4 * rows]])
         wide = wide.reshape(3, 2, rows, HALF)
         keep = lax.dynamic_index_in_dim(wide, self.core, 1, keepdims=False)
@@ -758,11 +750,10 @@
     def reduce_pairs(self, grads):
         return [lax.psum_scatter(grads[0], "ctx", scatter_dimension=0)]
 
-    def pack(self, wide, down, gains):
-        packs = []
-        for own in ((wide[0], gains), (wide[1], wide[2], down)):
-            packs.append((own, tuple(swap_x(part) for part in own)))
-        return packs
+    def pack_mixed(self, *own):
+        return own, tuple(swap_x(part) for part in own)
+
+    pack_deep = pack_mixed
 
     def column(self, packs, layer, *after):
         return [jnp.where(self.section == layer, a, b) for pack in packs for a, b in zip(*pack)]
@@ -837,8 +828,11 @@
             )
         )
 
-    def finish(self, first, second, rows):
-        first, second = self.reduce(*first), self.reduce(*second)
+    def cross(self, first, second):
+        return first, second
+
+    def finish(self, mixed, deep, rows):
+        first, second = (self.reduce(*pair) for pair in zip(mixed, deep))
         return tuple(
             jnp.where(self.section == 0, a, b) + swap_x(jnp.where(self.section == 0, b, a))
             for a, b in zip(first, second)
@@ -864,7 +858,7 @@
         project_kernel,
         (struct((rows, QW), BF), struct((rows, 2 * KW), BF)),
         (source, mixed, g_attn, place[2], place[3]),
-        limit=12,
+        limit=8,
         name="project",
     )
     return queries, pairs
@@ -884,7 +878,7 @@
             pltpu.VMEM((HQ, rows, HD), F32),
             pltpu.VMEM((HQ, rows, 1), F32),
         ],
-        limit=net.limit(28),
+        limit=net.limit(16),
         name="attend",
     )
 
@@ -896,7 +890,7 @@
         struct((rows, D), BF),
         (middle, gate, up, down, g_mlp),
         [pltpu.VMEM((rows, D), BF), pltpu.VMEM((rows, D), F32)],
-        limit=16,
+        limit=12,
         name="mlp",
     )
 
@@ -911,7 +905,7 @@
         (net.core.reshape(1), d_result, middle, mixed, gate, up, down, g_mlp),
         [pltpu.VMEM((rows, D), BF), pltpu.VMEM((rows, D), F32)],
         scalars=1,
-        limit=28,
+        limit=22,
         name="mlp_back",
     )
     return outs[:2], outs[2:4], *outs[4:]
@@ -938,7 +932,7 @@
             pltpu.VMEM((KV, HD, keys), F32),
             pltpu.VMEM((KV, HD, keys), F32),
         ],
-        limit=net.limit(32),
+        limit=net.limit(22),
         name="attend_back",
     )
 
@@ -956,7 +950,7 @@
             place[2], place[3], *adds,
         ),
         scalars=1,
-        limit=20,
+        limit=12,
         name="input",
     )
     return d_source, [keep], [send]
@@ -968,21 +962,22 @@
     sizes = tuple(lax.axis_size(axis) for axis in ("section", "ctx", "fsdp"))
     net = Fast() if sizes == (2, 4, 4) else Plain()
     rows = inputs.shape[2]
-    wide = jnp.stack(
-        [jnp.concatenate([w_query[0], w_key[0], w_out[0], w_value[0]], axis=1), w_gate[0], w_up[0]]
-    )
+    mixed = jnp.concatenate([w_query[0], w_key[0], w_out[0], w_value[0]], axis=1)
+    mixed_pack = net.pack_mixed(mixed, jnp.stack([g_attn[0], g_mlp[0]]))
+    shard = w_query.shape[1]
+    lengths, gate, up, down, inputs, cotangent = tie(
+        (lengths, w_gate[0], w_up[0], w_down[0], inputs, cotangent), mixed_pack[0]
+    )
+    deep_pack = net.pack_deep(gate, up, down)
+    mixed_column = net.column([mixed_pack], 0)
     own = net.lengths(lengths)
     positions = net.positions_of(0, 0, rows)
     passed = (positions[:, None] >= jnp.cumsum(own)[None, :]).astype(I32)
     starts = jnp.sum(passed * own[None, :], axis=1)
     cosine, sine = turn_tables(positions - starts)
     place = (positions[:, None], starts[:, None], cosine, sine, net.key_positions(rows))
-    shard = w_query.shape[1]
-
-    mixed_pack, deep_pack = net.pack(wide, w_down[0], jnp.stack([g_attn[0], g_mlp[0]]))
     source = lax.dynamic_index_in_dim(inputs[0], net.section, 0, keepdims=False)
     d_result = lax.dynamic_index_in_dim(cotangent[0], net.section, 0, keepdims=False)
-    mixed_column = net.column([mixed_pack], 0)
     mixed_square = net.square(mixed_column)
     deep_column = net.column([deep_pack], 0, mixed_column)
     source, d_result, place = tie((source, d_result, place), mixed_column)
@@ -1002,7 +997,6 @@
     middle_0, column, deep_phase, early = tie((middle_0, column, deep_phase, early))
     mixed_square = net.square(column, rows=slice(None, mixed_rows))
     deep_0 = net.assemble(net.gather_phase(deep_phase, early), shard, False)
-    d_result = net.spread(tie(d_result, deep_0))
     first = mlp_forward(middle_0, *deep_0, g_mlp_0)
     first, mixed_square = tie((first, mixed_square))
     mixed_pieces = net.gather_square(mixed_square)
@@ -1010,13 +1004,14 @@
     mixed_1, g_attn_1, g_mlp_1 = net.assemble(mixed_pieces, shard, True)
 
     queries_1, pairs = project(net, first, mixed_1, g_attn_1, place)
-    pairs, d_result = tie((pairs, d_result))
     pieces_1 = net.share_pairs(pairs)
     deep_phase = net.second_phase(deep_phase, queries_1)
-    early = net.early_core(deep_phase)
+    d_result = net.spread(tie(d_result, pieces_1))
     attended_1, log_1, middle_1 = attend_forward(net, first, queries_1, pieces_1, mixed_1, place)
-    middle_1, deep_phase, early = tie((middle_1, deep_phase, early))
-    deep_1 = net.assemble(net.gather_phase(deep_phase, early), shard, True)
+    middle_1, deep_phase, d_result = tie((middle_1, deep_phase, d_result))
+    deep_1 = net.assemble(
+        net.gather_phase(deep_phase, net.early_core(deep_phase)), shard, True
+    )
 
     deep_keep, deep_send, gain_grad, d_middle, d_attended = mlp_backward(
         net, d_result, middle_1, mixed_1, *deep_1, g_mlp_1
@@ -1030,13 +1025,14 @@
     d_pairs = tie(d_pairs, deep_sum)
     deep_sum = net.move_first(deep_sum)
     second = mlp_forward(tie(middle_1, d_pairs), *deep_1, g_mlp_1)
-    adds, deep_sum = tie((net.reduce_pairs(d_pairs), deep_sum), second)
+    adds = tie(net.reduce_pairs(d_pairs), second)
+    outs = input_backward(
+        net, first, attended_1, d_middle, d_queries, adds, gain_grad, mixed_1, g_attn_1, place
+    )
+    (d_first, mixed_keep, mixed_send), deep_sum = tie((outs, deep_sum))
     deep_sum = net.split_second(deep_sum)
-    adds = tie(adds, deep_sum)
+    d_first = tie(d_first, deep_sum)
     deep_sum = net.move_second(deep_sum)
-    d_first, mixed_keep, mixed_send = input_backward(
-        net, first, attended_1, d_middle, d_queries, adds, gain_grad, mixed_1, g_attn_1, place
-    )
     mixed_sum = net.reduce_core(mixed_keep, mixed_send)
     second = net.unspread(tie(second, d_first))
 
@@ -1046,41 +1042,44 @@
     deep_sum = net.split_column(deep_sum)
     d_attended = tie(d_attended, deep_sum)
     deep_sum_1 = net.move_column(deep_sum)
-    deep_sum = net.reduce_core(deep_keep, deep_send)
+    sums = net.split_first(mixed_sum, net.reduce_core(deep_keep, deep_send))
+    d_attended = tie(d_attended, sums)
+    sums = net.move_first(sums)
     d_queries, *d_pairs = attend_backward(
         net, d_attended, attended_0, log_0, queries_0, pieces_0, place
     )
-    d_queries, d_pairs, deep_sum, deep_sum_1 = tie((d_queries, d_pairs, deep_sum, deep_sum_1))
-    sums = net.split_first(mixed_sum, deep_sum)
+    d_queries, d_pairs, sums, deep_sum_1 = tie((d_queries, d_pairs, sums, deep_sum_1))
+    sums = net.split_second(sums)
     d_pairs = tie(d_pairs, sums)
-    sums = net.move_first(sums)
+    sums = net.move_second(sums)
     deep_sum_1 = net.total(deep_sum_1)
     adds, sums = tie((net.reduce_pairs(d_pairs), sums), deep_sum_1)
-    sums = net.split_second(sums)
+    sums = net.split_column(sums)
     adds = tie(adds, sums)
-    sums = net.move_second(sums)
+    sums = net.move_column(sums)
     d_input, mixed_keep, mixed_send = input_backward(
         net, source, attended_0, d_middle, d_queries, adds, gain_grad, mixed_0, g_attn_0, place
     )
+    d_input, mixed_keep, mixed_send = tie((d_input, mixed_keep, mixed_send), sums[1])
 
     mixed_sum = net.split_square(net.reduce_core(mixed_keep, mixed_send))
     d_input = net.unspread(tie(d_input, mixed_sum))
-    mixed_sum, sums = tie((mixed_sum, sums))
     mixed_sum = net.move_square(mixed_sum)
-    sums = net.move_column(net.split_column(sums))
-    mixed_sum = net.move_column(net.split_column(mixed_sum))
-    sums = tie(sums, mixed_sum)
+    mixed_sum, d_input = tie((mixed_sum, d_input))
+    mixed_sum = net.split_column(mixed_sum)
+    sums, d_input = tie((sums, d_input), mixed_sum)
+    mixed_sum = net.move_column(mixed_sum)
     mixed_sum_1 = net.total(sums, slice(None, 80))
-    deep_sum_0 = net.total(sums, slice(80, None))
-    mixed_sum_0 = net.total(mixed_sum)
-    wide_grad, down_grad, gain_grads = net.finish(
-        (mixed_sum_0, deep_sum_0), (mixed_sum_1, deep_sum_1), shard
-    )
+    deep_sum = net.cross(net.total(sums, slice(80, None)), deep_sum_1)
     kept = jnp.where(net.section == 0, d_input, second)
     crossed = swap_x(jnp.where(net.section == 0, second, d_input))
+    mixed_sum, crossed, deep_sum = tie((mixed_sum, crossed, deep_sum))
     edges = jnp.stack(
         [jnp.where(net.section == 0, kept, crossed), jnp.where(net.section == 0, crossed, kept)]
     ).astype(F32)
+    mixed_sum = net.cross(net.total(mixed_sum), mixed_sum_1)
+    mixed_sum, edges = tie((mixed_sum, edges))
+    wide_grad, down_grad, gain_grads = net.finish(mixed_sum, deep_sum, shard)
     mixed = wide_grad[0]
     return (
         edges[None, None],

time: 372 us -> 358 us (0.962)
  waiting for transfers between devices: 112 us -> 95.9 us
  starting transfers between devices: 93.8 us -> 106 us
  local copies, waits for them, and re-layouts: 32.6 us -> 25 us
  other arithmetic: 12.9 us -> 8.91 us
    ppermute x16, waiting for transfers between devices: 33.8 us -> 22.4 us  [swap_x(): return lax.ppermute(value, 'section', flip(2, 1))]
    ppermute x6, waiting for transfers between devices: 9.05 us -> 2.64 us  [column(): lax.ppermute(start, 'ctx', ring(4, steps))]
    ppermute x5, waiting for transfers between devices: 11.6 us -> 5.26 us  [swap_zpair(): return lax.ppermute(value, 'ctx', flip(4, 1))]
    ppermute x11, waiting for transfers between devices: 8.44 us -> 14.5 us  [swap_y(): return lax.ppermute(value, 'fsdp', flip(4, 2))]
    ppermute x9, starting transfers between devices: 12.3 us -> 18.4 us  [move_column(): lax.ppermute(part, 'ctx', ring(4, steps))]
    ppermute x4, waiting for transfers between devices: 13.7 us -> 7.66 us  [spread(): lax.ppermute(block[k * half:(k + 1) * half], ('ctx', 'fsdp'), spread_pair...]
    ppermute x24, waiting for transfers between devices: 6.92 us -> 12.7 us  [swap_core(): return lax.ppermute(value, 'fsdp', flip(4, 1))]
    unnamed x92 -> x67, local copies, waits for them, and re-layouts: 18.4 us -> 12.7 us
  transfers between devices with their start and end apart: 83 -> 83, of which waited for: 35 -> 43; matrix products, arithmetic and copies ran while one was open for 9% -> 5% of each run, Pallas kernels for 23% -> 26%
where the time goes in v4:
time: 358 us; the launch traced here: 351 us
  Pallas kernels  113 us (32%)
  starting transfers between devices  106 us (30%)
  waiting for transfers between devices  95.9 us (27%)
  local copies, waits for them, and re-layouts  25 us (7%)
  other arithmetic  8.91 us (2%)
    pallas_call x20, Pallas kernels, vmem_call(): pl.pallas_call(kernel, out_shape=out_shape, in_specs=specs, scratch_shape...  103 us
    ppermute x24, starting transfers between devices, swap_core(): return lax.ppermute(value, 'fsdp', flip(4, 1))  27 us
    ppermute x16, waiting for transfers between devices, swap_x(): return lax.ppermute(value, 'section', flip(2, 1))  22.4 us
    ppermute x9, starting transfers between devices, move_column(): lax.ppermute(part, 'ctx', ring(4, steps))  18.4 us
    ppermute x11, waiting for transfers between devices, swap_y(): return lax.ppermute(value, 'fsdp', flip(4, 2))  14.5 us
    ppermute x9, waiting for transfers between devices, move_column(): lax.ppermute(part, 'ctx', ring(4, steps))  13.9 us
    ppermute x16, starting transfers between devices, swap_x(): return lax.ppermute(value, 'section', flip(2, 1))  13.2 us
    unnamed x67, local copies, waits for them, and re-layouts  12.7 us
  transfers between devices with their start and end apart: 83, of which 43 were waited for; matrix products, arithmetic and copies ran while one was open for 5% of the time, Pallas kernels for 26%

profile of v4, /device:TPU:9, one launch (start us, length us, event | category | flops | bytes accessed | tf_op | source)
XLA Modules:
  0.0 351.0 jit_solution(17724752353559384460)
XLA Ops:
  12.0 2.7 collective-permute-start
  26.3 6.6 %collective-permute-done.13 = bf16[4,40,768]{2,1,0:T(8,128)(2,1)S(1)} collective-permute-done((bf16[4,40,768]{2,1,0:T(8,128)(2,1)S(1)}, bf16[4,40,768]{2,1,0:T(8,128)(2,1)S(1)}, u32[]{:S(2)}, u32[]{:S(2)}) %collective-permute-start.13) | collective-permute-done | bytes 245792 | tf_op jit(solution)/shard_map/ppermute | solution.py:70
  34.7 2.6 collective-permute-done.8
  37.4 6.5 %collective-permute-start.9 = (bf16[192,576]{1,0:T(8,128)(2,1)S(1)}, bf16[192,576]{1,0:T(8,128)(2,1)S(1)}, u32[]{:S(2)}, u32[]{:S(2)}) collective-permute-start(bf16[192,576]{1,0:T(8,128)(2,1)S(1)} %get-tuple-element.586), channel_id=1, source_target_pairs={{0,0},{1,8},{2,2},{3,10},{4,4},{5,12},{6,6},{7,14},{8,5},{9,13},{1... | collective-permute-start | bytes 663560 | tf_op jit(solution)/shard_map/ppermute | solution.py:512
  46.8 5.0 %collective-permute-done.9 = bf16[192,576]{1,0:T(8,128)(2,1)S(1)} collective-permute-done((bf16[192,576]{1,0:T(8,128)(2,1)S(1)}, bf16[192,576]{1,0:T(8,128)(2,1)S(1)}, u32[]{:S(2)}, u32[]{:S(2)}) %collective-permute-start.9) | collective-permute-done | bytes 221216 | tf_op jit(solution)/shard_map/ppermute | solution.py:512
  51.8 2.6 collective-permute-done.10
  65.3 4.1 %collective-permute-start.17 = (bf16[384,384]{1,0:T(8,128)(2,1)S(1)}, bf16[384,384]{1,0:T(8,128)(2,1)S(1)}, u32[]{:S(2)}, u32[]{:S(2)}) collective-permute-start(bf16[384,384]{1,0:T(8,128)(2,1)S(1)} %collective-permute-done.15), channel_id=1, source_target_pairs={{0,1},{1,0},{2,3},{3,2},{4,5},{5,4},{6,7},{7,6},{8,9},{9,8},{10,11... | collective-permute-start | bytes 884744 | tf_op jit(solution)/shard_map/ppermute | solution.py:54
  81.2 11.6 %attend.2 = (f32[384,576]{1,0:T(8,128)S(1)}, f32[384,9]{1,0:T(8,128)S(1)}, f32[384,576]{1,0:T(8,128)S(1)}) custom-call(bf16[384,576]{1,0:T(8,128)(2,1)S(1)} %pad_maximum_fusion.3.source_ref, bf16[384,576]{1,0:T(8,128)(2,1)S(1)} %get-tuple-element.286.query_ref, s32[384,1]{1,0:T(8,128)S(1)} %copy.69.position_ref, s32[384,1]{1,0:T(8,128)S(1)} %copy.70.start_ref, ...), custom_call_target="tpu_custom_call" | custom-call | tf_op jit(solution)/shard_map/attend/pallas_call | solution.py:845
  92.8 4.8 %collective-permute-done.19 = bf16[2,160,768]{2,1,0:T(8,128)(2,1)} collective-permute-done((bf16[2,160,768]{2,1,0:T(8,128)(2,1)}, bf16[2,160,768]{2,1,0:T(8,128)(2,1)}, u32[]{:S(2)}, u32[]{:S(2)}) %collective-permute-start.19) | collective-permute-done | bytes 491552 | tf_op jit(solution)/shard_map/ppermute | solution.py:577
  102.7 4.1 %assemble.5 = (bf16[576,1536]{1,0:T(8,128)(2,1)S(1)}, bf16[576,1536]{1,0:T(8,128)(2,1)S(1)}, bf16[1536,576]{1,0:T(8,128)(2,1)S(1)}) custom-call(s32[4]{0:T(128)S(1)} %pad_add_fusion.2.index_ref, bf16[4,120,768]{2,1,0:T(8,128)(2,1)} %constant_dynamic-update-slice_fusion.refs_0_, bf16[4,120,768]{2,1,0:T(8,128)(2,1)} %collective-permute-done.22.refs_1_, ...), custom_call_target="tpu_custom_call" | custom-call | tf_op jit(solution)/shard_map/assemble/pallas_call | solution.py:618
  106.8 4.6 %mlp.2.source_ref = bf16[384,576]{1,0:T(8,128)(2,1)S(1)} custom-call(f32[384,576]{1,0:T(8,128)S(1)} %get-tuple-element.303.middle_ref, bf16[576,1536]{1,0:T(8,128)(2,1)S(1)} %get-tuple-element.322.gate_ref, bf16[576,1536]{1,0:T(8,128)(2,1)S(1)} %get-tuple-element.323.up_ref, bf16[1536,576]{1,0:T(8,128)(2,1)S(1)} %get-tuple-element.324.down_ref, ...), custom_call_target="tpu_custom_call" | custom-call | tf_op jit(solution)/shard_map/mlp/pallas_call | solution.py:845
  127.7 3.6 %collective-permute-done.32 = bf16[384,384]{1,0:T(8,128)(2,1)S(1)} collective-permute-done((bf16[384,384]{1,0:T(8,128)(2,1)S(1)}, bf16[384,384]{1,0:T(8,128)(2,1)S(1)}, u32[]{:S(2)}, u32[]{:S(2)}) %collective-permute-start.32) | collective-permute-done | bytes 294944 | tf_op jit(solution)/shard_map/ppermute | solution.py:62
  134.1 4.1 %collective-permute-start.39 = (bf16[192,576]{1,0:T(8,128)(2,1)S(1)}, bf16[192,576]{1,0:T(8,128)(2,1)S(1)}, u32[]{:S(2)}, u32[]{:S(2)}) collective-permute-start(bf16[192,576]{1,0:T(8,128)(2,1)S(1)} %get-tuple-element.582), channel_id=1, source_target_pairs={{0,0},{1,8},{2,2},{3,10},{4,4},{5,12},{6,6},{7,14},{8,5},{9,13},{1... | collective-permute-start | bytes 663560 | tf_op jit(solution)/shard_map/ppermute | solution.py:512
  138.3 11.4 %attend.3 = (f32[384,576]{1,0:T(8,128)S(1)}, f32[384,9]{1,0:T(8,128)S(1)}, f32[384,576]{1,0:T(8,128)S(1)}) custom-call(bf16[384,576]{1,0:T(8,128)(2,1)S(1)} %mlp.2.source_ref, bf16[384,576]{1,0:T(8,128)(2,1)S(1)} %get-tuple-element.343.query_ref, s32[384,1]{1,0:T(8,128)S(1)} %copy.69.position_ref, s32[384,1]{1,0:T(8,128)S(1)} %copy.70.start_ref, ...), custom_call_target="tpu_custom_call" | custom-call | tf_op jit(solution)/shard_map/attend/pallas_call | solution.py:845
  159.3 12.3 %mlp_back.2 = (bf16[4,240,768]{2,1,0:T(8,128)(2,1)S(1)}, bf16[4,240,768]{2,1,0:T(8,128)(2,1)S(1)}, bf16[4,240,768]{2,1,0:T(8,128)(2,1)S(1)}, bf16[4,240,768]{2,1...) custom-call(s32[1]{0:T(128)} %bitcast.3.core_ref, ...), custom_call_target="tpu_custom_call" | custom-call | tf_op jit(solution)/shard_map/mlp_back/pallas_call | solution.py:845
  172.3 15.4 %attend_back.2 = (f32[384,576]{1,0:T(8,128)S(1)}, bf16[2,384,384]{2,1,0:T(8,128)(2,1)S(1)}, bf16[2,384,384]{2,1,0:T(8,128)(2,1)S(1)}) custom-call(bf16[384,576]{1,0:T(8,128)(2,1)S(1)} %get-tuple-element.378.d_out_ref, f32[384,576]{1,0:T(8,128)S(1)} %get-tuple-element.345.attended_ref, f32[384,9]{1,0:T(8,128)S(1)} %get-tuple-element.379.log_ref, ...), custom_call_target="tpu_custom_call" | custom-call | tf_op jit(solution)/shard_map/attend_back/pallas_call | solution.py:845
  193.3 4.6 %mlp.3 = bf16[384,576]{1,0:T(8,128)(2,1)S(1)} custom-call(f32[384,576]{1,0:T(8,128)S(1)} %get-tuple-element.401.middle_ref, bf16[576,1536]{1,0:T(8,128)(2,1)S(1)} %get-tuple-element.373.gate_ref, bf16[576,1536]{1,0:T(8,128)(2,1)S(1)} %get-tuple-element.374.up_ref, bf16[1536,576]{1,0:T(8,128)(2,1)S(1)} %get-tuple-element.375.down_ref, ...), custom_call_target="tpu_custom_call" | custom-call | tf_op jit(solution)/shard_map/mlp/pallas_call | solution.py:845
  199.6 3.0 input.2
  202.6 4.6 %collective-permute-done.49.moved_ref = bf16[2,2,240,384]{3,2,1,0:T(8,128)(2,1)S(1)} collective-permute-done((bf16[2,2,240,384]{3,2,1,0:T(8,128)(2,1)S(1)}, bf16[2,2,240,384]{3,2,1,0:T(8,128)(2,1)S(1)}, u32[]{:S(2)}, u32[]{:S(2)}) %collective-permute-start.49) | collective-permute-done | bytes 737312 | tf_op jit(solution)/shard_map/ppermute | solution.py:66
  212.4 3.8 %collective-permute-start.54 = (bf16[192,576]{1,0:T(8,128)(2,1)S(1)}, bf16[192,576]{1,0:T(8,128)(2,1)S(1)}, u32[]{:S(2)}, u32[]{:S(2)}) collective-permute-start(bf16[192,576]{1,0:T(8,128)(2,1)S(1)} %get-tuple-element.578), channel_id=1, source_target_pairs={{0,0},{8,1},{2,2},{10,3},{4,4},{12,5},{6,6},{14,7},{5,8},{13,9},{7... | collective-permute-start | bytes 663560 | tf_op jit(solution)/shard_map/ppermute | solution.py:524
  216.2 12.3 %mlp_back.3 = (bf16[4,240,768]{2,1,0:T(8,128)(2,1)S(1)}, bf16[4,240,768]{2,1,0:T(8,128)(2,1)S(1)}, bf16[4,240,768]{2,1,0:T(8,128)(2,1)S(1)}, bf16[4,240,768]{2,1...) custom-call(s32[1]{0:T(128)} %bitcast.3.core_ref, ...), custom_call_target="tpu_custom_call" | custom-call | tf_op jit(solution)/shard_map/mlp_back/pallas_call | solution.py:845
  229.2 2.8 collective-permute-done.56.refs_4_
  241.6 15.0 %attend_back.3 = (f32[384,576]{1,0:T(8,128)S(1)}, bf16[2,384,384]{2,1,0:T(8,128)(2,1)S(1)}, bf16[2,384,384]{2,1,0:T(8,128)(2,1)S(1)}) custom-call(bf16[384,576]{1,0:T(8,128)(2,1)S(1)} %get-tuple-element.447.d_out_ref, f32[384,576]{1,0:T(8,128)S(1)} %get-tuple-element.291.attended_ref, f32[384,9]{1,0:T(8,128)S(1)} %get-tuple-element.448.log_ref, ...), custom_call_target="tpu_custom_call" | custom-call | tf_op jit(solution)/shard_map/attend_back/pallas_call | solution.py:845
  265.0 9.8 %collective-permute-done.65.refs_1_ = bf16[2,320,384]{2,1,0:T(8,128)(2,1)S(1)} collective-permute-done((bf16[2,320,384]{2,1,0:T(8,128)(2,1)S(1)}, bf16[2,320,384]{2,1,0:T(8,128)(2,1)S(1)}, u32[]{:S(2)}, u32[]{:S(2)}) %collective-permute-start.65) | collective-permute-done | bytes 491552 | tf_op jit(solution)/shard_map/ppermute | solution.py:58
  277.0 3.0 input.3
  280.0 2.7 collective-permute-done.67
  288.2 3.3 collective-permute-start.72
  296.4 4.0 %collective-permute-start.77 = (bf16[320,384]{1,0:T(8,128)(2,1)S(1)}, bf16[320,384]{1,0:T(8,128)(2,1)S(1)}, u32[]{:S(2)}, u32[]{:S(2)}) collective-permute-start(bf16[320,384]{1,0:T(8,128)(2,1)S(1)} %get-tuple-element.477), channel_id=1, source_target_pairs={{0,8},{4,12},{8,0},{12,4},{1,9},{5,13},{9,1},{13,5},{2,10},{6,14},... | collective-permute-start | bytes 737288 | tf_op jit(solution)/shard_map/ppermute | solution.py:695
  302.0 7.6 %collective-permute-start.78 = (bf16[320,384]{1,0:T(8,128)(2,1)S(1)}, bf16[320,384]{1,0:T(8,128)(2,1)S(1)}, u32[]{:S(2)}, u32[]{:S(2)}) collective-permute-start(bf16[320,384]{1,0:T(8,128)(2,1)S(1)} %get-tuple-element.478), channel_id=1, source_target_pairs={{0,12},{4,0},{8,4},{12,8},{1,13},{5,1},{9,5},{13,9},{2,14},{6,2},{... | collective-permute-start | bytes 737288 | tf_op jit(solution)/shard_map/ppermute | solution.py:695
  310.4 5.8 %collective-permute-done.77 = bf16[320,384]{1,0:T(8,128)(2,1)S(1)} collective-permute-done((bf16[320,384]{1,0:T(8,128)(2,1)S(1)}, bf16[320,384]{1,0:T(8,128)(2,1)S(1)}, u32[]{:S(2)}, u32[]{:S(2)}) %collective-permute-start.77) | collective-permute-done | bytes 245792 | tf_op jit(solution)/shard_map/ppermute | solution.py:695
  326.2 7.7 %collective-permute-done.79 = bf16[384,576]{1,0:T(8,128)(2,1)} collective-permute-done((bf16[384,576]{1,0:T(8,128)(2,1)}, bf16[384,576]{1,0:T(8,128)(2,1)}, u32[]{:S(2)}, u32[]{:S(2)}) %collective-permute-start.79) | collective-permute-done | bytes 442400 | tf_op jit(solution)/shard_map/ppermute | solution.py:66
  341.4 3.2 collective-permute-start.82
  (312 shorter events, 153.4 us)
Async XLA Ops:
  19.2 13.7 %collective-permute-start.13 = (bf16[4,40,768]{2,1,0:T(8,128)(2,1)S(1)}, bf16[4,40,768]{2,1,0:T(8,128)(2,1)S(1)}, u32[]{:S(2)}, u32[]{:S(2)}) collective-permute-start(bf16[4,40,768]{2,1,0:T(8,128)(2,1)S(1)} %pad_maximum_fusion.12), channel_id=1, source_target_pairs={{0,18},{1,19},{2,16},{3,17},{16,2},{17,3},{18,0},{19,1},{4,22},{5,... | collective-permute-start | bytes 737288 | tf_op jit(solution)/shard_map/ppermute | solution.py:70
  33.0 21.9 %collective-permute-start.14 = (bf16[4,4,40,768]{3,2,1,0:T(8,128)(2,1)S(1)}, bf16[4,4,40,768]{3,2,1,0:T(8,128)(2,1)S(1)}, u32[]{:S(2)}, u32[]{:S(2)}) collective-permute-start(bf16[4,4,40,768]{3,2,1,0:T(8,128)(2,1)S(1)} %pad_maximum_fusion.refs_0_), channel_id=1, source_target_pairs={{0,1},{1,0},{2,3},{3,2},{4,5},{5,4},{6,7},{7,6},{8,9},{9,8},{10,11... | collective-permute-start | bytes 2949128 | tf_op jit(solution)/shard_map/ppermute | solution.py:54
  37.4 14.4 %collective-permute-start.9 = (bf16[192,576]{1,0:T(8,128)(2,1)S(1)}, bf16[192,576]{1,0:T(8,128)(2,1)S(1)}, u32[]{:S(2)}, u32[]{:S(2)}) collective-permute-start(bf16[192,576]{1,0:T(8,128)(2,1)S(1)} %get-tuple-element.586), channel_id=1, source_target_pairs={{0,0},{1,8},{2,2},{3,10},{4,4},{5,12},{6,6},{7,14},{8,5},{9,13},{1... | collective-permute-start | bytes 663560 | tf_op jit(solution)/shard_map/ppermute | solution.py:512
  62.8 30.0 %collective-permute-start.22 = (bf16[4,120,768]{2,1,0:T(8,128)(2,1)}, bf16[4,120,768]{2,1,0:T(8,128)(2,1)}, u32[]{:S(2)}, u32[]{:S(2)}) collective-permute-start(bf16[4,120,768]{2,1,0:T(8,128)(2,1)} %constant_dynamic-update-slice_fusion.refs_0_), channel_id=1, source_target_pairs={{0,16},{16,0},{1,17},{17,1},{2,18},{18,2},{3,19},{19,3},{4,20},{20... | collective-permute-start | bytes 2211848 | tf_op jit(solution)/shard_map/ppermute | solution.py:66
  64.0 28.8 %collective-permute-start.24 = (bf16[4,120,768]{2,1,0:T(8,128)(2,1)}, bf16[4,120,768]{2,1,0:T(8,128)(2,1)}, u32[]{:S(2)}, u32[]{:S(2)}) collective-permute-start(bf16[4,120,768]{2,1,0:T(8,128)(2,1)} %constant_dynamic-update-slice_fusion.refs_0_), channel_id=1, source_target_pairs={{0,1},{1,0},{2,3},{3,2},{4,5},{5,4},{6,7},{7,6},{8,9},{9,8},{10,11... | collective-permute-start | bytes 2211848 | tf_op jit(solution)/shard_map/ppermute | solution.py:54
  70.2 22.6 %collective-permute-start.23 = (bf16[4,120,768]{2,1,0:T(8,128)(2,1)}, bf16[4,120,768]{2,1,0:T(8,128)(2,1)}, u32[]{:S(2)}, u32[]{:S(2)}) collective-permute-start(bf16[4,120,768]{2,1,0:T(8,128)(2,1)} %constant_dynamic-update-slice_fusion.2.refs_2_), channel_id=1, source_target_pairs={{0,2},{1,3},{2,0},{3,1},{4,6},{5,7},{6,4},{7,5},{8,10},{9,11},{10,... | collective-permute-start | bytes 2211848 | tf_op jit(solution)/shard_map/ppermute | solution.py:58
  72.2 20.6 %collective-permute-start.25 = (bf16[4,120,768]{2,1,0:T(8,128)(2,1)}, bf16[4,120,768]{2,1,0:T(8,128)(2,1)}, u32[]{:S(2)}, u32[]{:S(2)}) collective-permute-start(bf16[4,120,768]{2,1,0:T(8,128)(2,1)} %constant_dynamic-update-slice_fusion.2.refs_2_), channel_id=1, source_target_pairs={{0,1},{1,0},{2,3},{3,2},{4,5},{5,4},{6,7},{7,6},{8,9},{9,8},{10,11... | collective-permute-start | bytes 2211848 | tf_op jit(solution)/shard_map/ppermute | solution.py:54
  75.5 22.1 %collective-permute-start.19 = (bf16[2,160,768]{2,1,0:T(8,128)(2,1)}, bf16[2,160,768]{2,1,0:T(8,128)(2,1)}, u32[]{:S(2)}, u32[]{:S(2)}) collective-permute-start(bf16[2,160,768]{2,1,0:T(8,128)(2,1)} %pad_maximum_fusion.4), channel_id=1, source_target_pairs={{0,8},{4,12},{8,0},{12,4},{1,9},{5,13},{9,1},{13,5},{2,10},{6,14},... | collective-permute-start | bytes 1474568 | tf_op jit(solution)/shard_map/ppermute | solution.py:577
  132.5 18.2 %collective-permute-start.37 = (bf16[4,120,768]{2,1,0:T(8,128)(2,1)S(1)}, bf16[4,120,768]{2,1,0:T(8,128)(2,1)S(1)}, u32[]{:S(2)}, u32[]{:S(2)}) collective-permute-start(bf16[4,120,768]{2,1,0:T(8,128)(2,1)S(1)} %constant_dynamic-update-slice_fusion.4.refs_0_), channel_id=1, source_target_pairs={{0,16},{16,0},{1,17},{17,1},{2,18},{18,2},{3,19},{19,3},{4,20},{20... | collective-permute-start | bytes 2211848 | tf_op jit(solution)/shard_map/ppermute | solution.py:66
  132.9 17.9 %collective-permute-start.38 = (bf16[4,120,768]{2,1,0:T(8,128)(2,1)S(1)}, bf16[4,120,768]{2,1,0:T(8,128)(2,1)S(1)}, u32[]{:S(2)}, u32[]{:S(2)}) collective-permute-start(bf16[4,120,768]{2,1,0:T(8,128)(2,1)S(1)} %constant_dynamic-update-slice_fusion.6.refs_2_), channel_id=1, source_target_pairs={{0,2},{1,3},{2,0},{3,1},{4,6},{5,7},{6,4},{7,5},{8,10},{9,11},{10,... | collective-permute-start | bytes 2211848 | tf_op jit(solution)/shard_map/ppermute | solution.py:58
  134.1 15.6 %collective-permute-start.39 = (bf16[192,576]{1,0:T(8,128)(2,1)S(1)}, bf16[192,576]{1,0:T(8,128)(2,1)S(1)}, u32[]{:S(2)}, u32[]{:S(2)}) collective-permute-start(bf16[192,576]{1,0:T(8,128)(2,1)S(1)} %get-tuple-element.582), channel_id=1, source_target_pairs={{0,0},{1,8},{2,2},{3,10},{4,4},{5,12},{6,6},{7,14},{8,5},{9,13},{1... | collective-permute-start | bytes 663560 | tf_op jit(solution)/shard_map/ppermute | solution.py:512
  171.6 16.0 %collective-permute-start.45 = (bf16[4,240,768]{2,1,0:T(8,128)(2,1)S(1)}, bf16[4,240,768]{2,1,0:T(8,128)(2,1)S(1)}, u32[]{:S(2)}, u32[]{:S(2)}) collective-permute-start(bf16[4,240,768]{2,1,0:T(8,128)(2,1)S(1)} %get-tuple-element.385), channel_id=1, source_target_pairs={{0,1},{1,0},{2,3},{3,2},{4,5},{5,4},{6,7},{7,6},{8,9},{9,8},{10,11... | collective-permute-start | bytes 4423688 | tf_op jit(solution)/shard_map/ppermute | solution.py:54
  172.1 15.6 %collective-permute-start.46 = (bf16[4,240,768]{2,1,0:T(8,128)(2,1)S(1)}, bf16[4,240,768]{2,1,0:T(8,128)(2,1)S(1)}, u32[]{:S(2)}, u32[]{:S(2)}) collective-permute-start(bf16[4,240,768]{2,1,0:T(8,128)(2,1)S(1)} %get-tuple-element.386), channel_id=1, source_target_pairs={{0,1},{1,0},{2,3},{3,2},{4,5},{5,4},{6,7},{7,6},{8,9},{9,8},{10,11... | collective-permute-start | bytes 4423688 | tf_op jit(solution)/shard_map/ppermute | solution.py:54
  189.3 18.0 %collective-permute-start.49 = (bf16[2,2,240,384]{3,2,1,0:T(8,128)(2,1)S(1)}, bf16[2,2,240,384]{3,2,1,0:T(8,128)(2,1)S(1)}, u32[]{:S(2)}, u32[]{:S(2)}) collective-permute-start(bf16[2,2,240,384]{3,2,1,0:T(8,128)(2,1)S(1)} %get-tuple-element.396), channel_id=1, source_target_pairs={{0,16},{16,0},{1,17},{17,1},{2,18},{18,2},{3,19},{19,3},{4,20},{20... | collective-permute-start | bytes 2211848 | tf_op jit(solution)/shard_map/ppermute | solution.py:66
  190.5 17.6 %collective-permute-start.50 = (bf16[2,240,768]{2,1,0:T(8,128)(2,1)S(1)}, bf16[2,240,768]{2,1,0:T(8,128)(2,1)S(1)}, u32[]{:S(2)}, u32[]{:S(2)}) collective-permute-start(bf16[2,240,768]{2,1,0:T(8,128)(2,1)S(1)} %get-tuple-element.398), channel_id=1, source_target_pairs={{0,2},{1,3},{2,0},{3,1},{4,6},{5,7},{6,4},{7,5},{8,10},{9,11},{10,... | collective-permute-start | bytes 2211848 | tf_op jit(solution)/shard_map/ppermute | solution.py:58
  208.2 20.5 %collective-permute-start.51 = (bf16[8,80,768]{2,1,0:T(8,128)(2,1)S(1)}, bf16[8,80,768]{2,1,0:T(8,128)(2,1)S(1)}, u32[]{:S(2)}, u32[]{:S(2)}) collective-permute-start(bf16[8,80,768]{2,1,0:T(8,128)(2,1)S(1)} %get-tuple-element.425), channel_id=1, source_target_pairs={{0,1},{1,0},{2,3},{3,2},{4,5},{5,4},{6,7},{7,6},{8,9},{9,8},{10,11... | collective-permute-start | bytes 2949128 | tf_op jit(solution)/shard_map/ppermute | solution.py:54
  210.3 18.4 %collective-permute-start.52 = (bf16[2,240,384]{2,1,0:T(8,128)(2,1)S(1)}, bf16[2,240,384]{2,1,0:T(8,128)(2,1)S(1)}, u32[]{:S(2)}, u32[]{:S(2)}) collective-permute-start(bf16[2,240,384]{2,1,0:T(8,128)(2,1)S(1)} %get-tuple-element.414), channel_id=1, source_target_pairs={{0,2},{1,3},{2,0},{3,1},{4,6},{5,7},{6,4},{7,5},{8,10},{9,11},{10,... | collective-permute-start | bytes 1105928 | tf_op jit(solution)/shard_map/ppermute | solution.py:58
  211.5 17.2 %collective-permute-start.53 = (bf16[2,240,384]{2,1,0:T(8,128)(2,1)S(1)}, bf16[2,240,384]{2,1,0:T(8,128)(2,1)S(1)}, u32[]{:S(2)}, u32[]{:S(2)}) collective-permute-start(bf16[2,240,384]{2,1,0:T(8,128)(2,1)S(1)} %get-tuple-element.415), channel_id=1, source_target_pairs={{0,16},{16,0},{1,17},{17,1},{2,18},{18,2},{3,19},{19,3},{4,20},{20... | collective-permute-start | bytes 1105928 | tf_op jit(solution)/shard_map/ppermute | solution.py:66
  211.8 16.8 %collective-permute-start.55 = (bf16[192,576]{1,0:T(8,128)(2,1)S(1)}, bf16[192,576]{1,0:T(8,128)(2,1)S(1)}, u32[]{:S(2)}, u32[]{:S(2)}) collective-permute-start(bf16[192,576]{1,0:T(8,128)(2,1)S(1)} %get-tuple-element.579), channel_id=1, source_target_pairs={{1,0},{9,1},{3,2},{11,3},{5,4},{13,5},{7,6},{15,7},{4,8},{12,9},{6... | collective-permute-start | bytes 663560 | tf_op jit(solution)/shard_map/ppermute | solution.py:524
  212.4 16.2 %collective-permute-start.54 = (bf16[192,576]{1,0:T(8,128)(2,1)S(1)}, bf16[192,576]{1,0:T(8,128)(2,1)S(1)}, u32[]{:S(2)}, u32[]{:S(2)}) collective-permute-start(bf16[192,576]{1,0:T(8,128)(2,1)S(1)} %get-tuple-element.578), channel_id=1, source_target_pairs={{0,0},{8,1},{2,2},{10,3},{4,4},{12,5},{6,6},{14,7},{5,8},{13,9},{7... | collective-permute-start | bytes 663560 | tf_op jit(solution)/shard_map/ppermute | solution.py:524
  235.6 23.3 %collective-permute-start.58 = (bf16[2,2,320,384]{3,2,1,0:T(8,128)(2,1)S(1)}, bf16[2,2,320,384]{3,2,1,0:T(8,128)(2,1)S(1)}, u32[]{:S(2)}, u32[]{:S(2)}) collective-permute-start(bf16[2,2,320,384]{3,2,1,0:T(8,128)(2,1)S(1)} %get-tuple-element.444), channel_id=1, source_target_pairs={{0,16},{16,0},{1,17},{17,1},{2,18},{18,2},{3,19},{19,3},{4,20},{20... | collective-permute-start | bytes 2949128 | tf_op jit(solution)/shard_map/ppermute | solution.py:66
  236.9 22.9 %collective-permute-start.59 = (bf16[2,320,768]{2,1,0:T(8,128)(2,1)S(1)}, bf16[2,320,768]{2,1,0:T(8,128)(2,1)S(1)}, u32[]{:S(2)}, u32[]{:S(2)}) collective-permute-start(bf16[2,320,768]{2,1,0:T(8,128)(2,1)S(1)} %get-tuple-element.446), channel_id=1, source_target_pairs={{0,2},{1,3},{2,0},{3,1},{4,6},{5,7},{6,4},{7,5},{8,10},{9,11},{10,... | collective-permute-start | bytes 2949128 | tf_op jit(solution)/shard_map/ppermute | solution.py:58
  238.3 18.2 %collective-permute-start.60 = (bf16[240,384]{1,0:T(8,128)(2,1)S(1)}, bf16[240,384]{1,0:T(8,128)(2,1)S(1)}, u32[]{:S(2)}, u32[]{:S(2)}) collective-permute-start(bf16[240,384]{1,0:T(8,128)(2,1)S(1)} %get-tuple-element.433), channel_id=1, source_target_pairs={{0,4},{4,8},{8,12},{12,0},{1,5},{5,9},{9,13},{13,1},{2,6},{6,10},{... | collective-permute-start | bytes 552968 | tf_op jit(solution)/shard_map/ppermute | solution.py:695
  239.1 17.5 %collective-permute-start.61 = (bf16[240,384]{1,0:T(8,128)(2,1)S(1)}, bf16[240,384]{1,0:T(8,128)(2,1)S(1)}, u32[]{:S(2)}, u32[]{:S(2)}) collective-permute-start(bf16[240,384]{1,0:T(8,128)(2,1)S(1)} %get-tuple-element.434), channel_id=1, source_target_pairs={{0,8},{4,12},{8,0},{12,4},{1,9},{5,13},{9,1},{13,5},{2,10},{6,14},... | collective-permute-start | bytes 552968 | tf_op jit(solution)/shard_map/ppermute | solution.py:695
  241.6 15.9 %collective-permute-start.62 = (bf16[240,384]{1,0:T(8,128)(2,1)S(1)}, bf16[240,384]{1,0:T(8,128)(2,1)S(1)}, u32[]{:S(2)}, u32[]{:S(2)}) collective-permute-start(bf16[240,384]{1,0:T(8,128)(2,1)S(1)} %get-tuple-element.435), channel_id=1, source_target_pairs={{0,12},{4,0},{8,4},{12,8},{1,13},{5,1},{9,5},{13,9},{2,14},{6,2},{... | collective-permute-start | bytes 552968 | tf_op jit(solution)/shard_map/ppermute | solution.py:695
  288.2 13.8 %collective-permute-start.72 = (bf16[192,576]{1,0:T(8,128)(2,1)S(1)}, bf16[192,576]{1,0:T(8,128)(2,1)S(1)}, u32[]{:S(2)}, u32[]{:S(2)}) collective-permute-start(bf16[192,576]{1,0:T(8,128)(2,1)S(1)} %get-tuple-element.576), channel_id=1, source_target_pairs={{0,0},{8,1},{2,2},{10,3},{4,4},{12,5},{6,6},{14,7},{5,8},{13,9},{7... | collective-permute-start | bytes 663560 | tf_op jit(solution)/shard_map/ppermute | solution.py:524
  291.6 18.1 %collective-permute-start.69 = (bf16[4,80,384]{2,1,0:T(8,128)(2,1)S(1)}, bf16[4,80,384]{2,1,0:T(8,128)(2,1)S(1)}, u32[]{:S(2)}, u32[]{:S(2)}) collective-permute-start(bf16[4,80,384]{2,1,0:T(8,128)(2,1)S(1)} %get-tuple-element.488), channel_id=1, source_target_pairs={{0,2},{1,3},{2,0},{3,1},{4,6},{5,7},{6,4},{7,5},{8,10},{9,11},{10,... | collective-permute-start | bytes 737288 | tf_op jit(solution)/shard_map/ppermute | solution.py:58
  292.7 17.0 %collective-permute-start.70 = (bf16[4,80,384]{2,1,0:T(8,128)(2,1)S(1)}, bf16[4,80,384]{2,1,0:T(8,128)(2,1)S(1)}, u32[]{:S(2)}, u32[]{:S(2)}) collective-permute-start(bf16[4,80,384]{2,1,0:T(8,128)(2,1)S(1)} %get-tuple-element.489), channel_id=1, source_target_pairs={{0,16},{16,0},{1,17},{17,1},{2,18},{18,2},{3,19},{19,3},{4,20},{20... | collective-permute-start | bytes 737288 | tf_op jit(solution)/shard_map/ppermute | solution.py:66
  293.0 16.7 %collective-permute-start.71 = (bf16[4,80,384]{2,1,0:T(8,128)(2,1)S(1)}, bf16[4,80,384]{2,1,0:T(8,128)(2,1)S(1)}, u32[]{:S(2)}, u32[]{:S(2)}) collective-permute-start(bf16[4,80,384]{2,1,0:T(8,128)(2,1)S(1)} %get-tuple-element.490), channel_id=1, source_target_pairs={{0,18},{1,19},{2,16},{3,17},{16,2},{17,3},{18,0},{19,1},{4,22},{5,... | collective-permute-start | bytes 737288 | tf_op jit(solution)/shard_map/ppermute | solution.py:70
  296.4 19.8 %collective-permute-start.77 = (bf16[320,384]{1,0:T(8,128)(2,1)S(1)}, bf16[320,384]{1,0:T(8,128)(2,1)S(1)}, u32[]{:S(2)}, u32[]{:S(2)}) collective-permute-start(bf16[320,384]{1,0:T(8,128)(2,1)S(1)} %get-tuple-element.477), channel_id=1, source_target_pairs={{0,8},{4,12},{8,0},{12,4},{1,9},{5,13},{9,1},{13,5},{2,10},{6,14},... | collective-permute-start | bytes 737288 | tf_op jit(solution)/shard_map/ppermute | solution.py:695
  302.0 15.9 %collective-permute-start.78 = (bf16[320,384]{1,0:T(8,128)(2,1)S(1)}, bf16[320,384]{1,0:T(8,128)(2,1)S(1)}, u32[]{:S(2)}, u32[]{:S(2)}) collective-permute-start(bf16[320,384]{1,0:T(8,128)(2,1)S(1)} %get-tuple-element.478), channel_id=1, source_target_pairs={{0,12},{4,0},{8,4},{12,8},{1,13},{5,1},{9,5},{13,9},{2,14},{6,2},{... | collective-permute-start | bytes 737288 | tf_op jit(solution)/shard_map/ppermute | solution.py:695
  319.3 14.6 %collective-permute-start.79 = (bf16[384,576]{1,0:T(8,128)(2,1)}, bf16[384,576]{1,0:T(8,128)(2,1)}, u32[]{:S(2)}, u32[]{:S(2)}) collective-permute-start(bf16[384,576]{1,0:T(8,128)(2,1)} %broadcast_select_fusion.1), channel_id=1, source_target_pairs={{0,16},{16,0},{1,17},{17,1},{2,18},{18,2},{3,19},{19,3},{4,20},{20... | collective-permute-start | bytes 1327112 | tf_op jit(solution)/shard_map/ppermute | solution.py:66
  (77 other events, 680.8 us)

commit v5 on v4

--- a/solution.py
+++ b/solution.py
@@ -135,18 +135,6 @@
             index += 1
 
 
-def each_job(jobs, tile, visit):
-    if tile is None:
-        for first, rows, keys in jobs:
-            visit(first, rows, keys)
-        return
-    _, rows, keys = jobs[0]
-
-    @pl.loop(0, rows // tile)
-    def _(step):
-        visit(pl.multiple_of(step * tile, tile), tile, keys)
-
-
 def store(slot, refs, at, value):
     for index, ref in enumerate(refs):
 
@@ -155,8 +143,20 @@
             ref[at] = value
 
 
-def job_bias(first, rows, keys, position_ref, start_ref, key_position_ref):
-    at = key_position_ref[:, :keys]
+def each_job(jobs, tile, visit):
+    if tile is None:
+        visit(jobs)
+        return
+    _, rows, first_key, keys = jobs[0]
+
+    @pl.loop(0, rows // tile)
+    def _(step):
+        visit([(pl.multiple_of(step * tile, tile), tile, first_key, keys)])
+
+
+def job_bias(job, position_ref, start_ref, key_position_ref):
+    first, rows, first_key, keys = job
+    at = key_position_ref[:, first_key : first_key + keys]
     allowed = (at <= position_ref[pl.ds(first, rows), :]) & (at >= start_ref[pl.ds(first, rows), :])
     return jnp.where(allowed, 0.0, -1e30)
 
@@ -181,14 +181,19 @@
     for head in range(HQ):
         query_scr[head] = query_ref[:, head * HD : (head + 1) * HD] * jnp.asarray(HD**-0.5, BF)
 
-    def visit(first, rows, keys):
-        bias = job_bias(first, rows, keys, position_ref, start_ref, key_position_ref)
-        at = pl.ds(first, rows)
+    def visit(jobs):
+        for job in jobs:
+            visit_one(job)
+
+    def visit_one(job):
+        bias = job_bias(job, position_ref, start_ref, key_position_ref)
+        at = pl.ds(job[0], job[1])
+        among = slice(job[2], job[2] + job[3])
 
         @pl.loop(0, KV)
         def _(group):
-            key = key_scr[group, :keys, :]
-            value = value_scr[group, :keys, :]
+            key = key_scr[group, among, :]
+            value = value_scr[group, among, :]
             for member in range(GROUP):
                 head = group * GROUP + member
                 scores = mm_nt(query_scr[head, at, :], key) + bias
@@ -295,24 +300,29 @@
     d_key_scr[...] = jnp.zeros_like(d_key_scr)
     d_value_scr[...] = jnp.zeros_like(d_value_scr)
 
-    def visit(first, rows, keys):
-        bias = job_bias(first, rows, keys, position_ref, start_ref, key_position_ref)
-        at = pl.ds(first, rows)
+    def visit(jobs):
+        biases = [job_bias(job, position_ref, start_ref, key_position_ref) for job in jobs]
 
         @pl.loop(0, KV)
         def _(group):
-            key = key_scr[group, :keys, :]
-            value = value_scr[group, :keys, :]
-            for member in range(GROUP):
-                head = group * GROUP + member
-                query = query_scr[head, at, :]
-                d_out = d_out_scr[head, at, :]
-                chances = jnp.exp(mm_nt(query, key) + bias - log_scr[head, at, :])
-                d_chances = mm_nt(d_out, value)
-                d_scores = (chances * (d_chances - delta_scr[head, at, :])).astype(BF)
-                d_query_scr[head, at, :] = mm(d_scores, key) * HD**-0.5
-                d_value_scr[group, :, :keys] += mm_tn(d_out, chances.astype(BF))
-                d_key_scr[group, :, :keys] += mm_tn(query, d_scores)
+            for index, (job, bias) in enumerate(zip(jobs, biases)):
+                at = pl.ds(job[0], job[1])
+                among = slice(job[2], job[2] + job[3])
+                key = key_scr[group, among, :]
+                value = value_scr[group, among, :]
+                for member in range(GROUP):
+                    head = group * GROUP + member
+                    query = query_scr[head, at, :]
+                    d_out = d_out_scr[head, at, :]
+                    chances = jnp.exp(mm_nt(query, key) + bias - log_scr[head, at, :])
+                    d_chances = mm_nt(d_out, value)
+                    d_scores = (chances * (d_chances - delta_scr[head, at, :])).astype(BF)
+                    d_query = mm(d_scores, key) * HD**-0.5
+                    if index:
+                        d_query = d_query + d_query_scr[head, at, :]
+                    d_query_scr[head, at, :] = d_query
+                    d_value_scr[group, :, among] += mm_tn(d_out, chances.astype(BF))
+                    d_key_scr[group, :, among] += mm_tn(query, d_scores)
 
     each_job(jobs, tile, visit)
     d_query_ref[...] = jnp.concatenate([d_query_scr[head] for head in range(HQ)], axis=1)
@@ -535,7 +545,11 @@
         return jnp.where(at < 4 * half, member, 7 - member) * half + at % half
 
     def jobs(self, rows, keys):
-        return ((0, rows // 2, keys // 2), (rows // 2, rows // 2, keys))
+        half = rows // 2
+        return ((0, half, 0, keys // 2), (half, half, 0, keys))
+
+    def back_jobs(self, rows, keys):
+        return ((0, rows, 0, keys // 2), (rows // 2, rows // 2, keys // 2, keys // 2))
 
     def share_pairs(self, pairs):
         along = swap_zpair(pairs)
@@ -742,7 +756,9 @@
         return jnp.arange(lax.axis_size("ctx") * rows, dtype=I32)[None]
 
     def jobs(self, rows, keys):
-        return ((0, rows, keys),)
+        return ((0, rows, 0, keys),)
+
+    back_jobs = jobs
 
     def share_pairs(self, pairs):
         return [lax.all_gather(pairs, "ctx", axis=0)]
@@ -916,7 +932,7 @@
     rows, keys = positions.shape[0], key_positions.shape[1]
     return vmem_call(
         functools.partial(
-            attend_back_kernel, net.jobs(rows, keys), net.tile, net.parts, len(pieces)
+            attend_back_kernel, net.back_jobs(rows, keys), net.tile, net.parts, len(pieces)
         ),
         [struct((rows, QW), F32)]
         + [struct((keys // rows // net.parts, rows, 2 * KW), BF)] * net.parts,
@@ -1053,14 +1069,12 @@
     d_pairs = tie(d_pairs, sums)
     sums = net.move_second(sums)
     deep_sum_1 = net.total(deep_sum_1)
-    adds, sums = tie((net.reduce_pairs(d_pairs), sums), deep_sum_1)
-    sums = net.split_column(sums)
-    adds = tie(adds, sums)
-    sums = net.move_column(sums)
+    adds = tie(net.reduce_pairs(d_pairs), deep_sum_1)
     d_input, mixed_keep, mixed_send = input_backward(
         net, source, attended_0, d_middle, d_queries, adds, gain_grad, mixed_0, g_attn_0, place
     )
-    d_input, mixed_keep, mixed_send = tie((d_input, mixed_keep, mixed_send), sums[1])
+    d_input, mixed_keep, mixed_send, sums = tie((d_input, mixed_keep, mixed_send, sums))
+    sums = net.move_column(net.split_column(sums))
 
     mixed_sum = net.split_square(net.reduce_core(mixed_keep, mixed_send))
     d_input = net.unspread(tie(d_input, mixed_sum))

time: 358 us -> 354 us (0.989)
  starting transfers between devices: 106 us -> 94.2 us
  waiting for transfers between devices: 95.9 us -> 107 us
    ppermute x9, starting transfers between devices: 18.4 us -> 7.51 us  [move_column(): lax.ppermute(part, 'ctx', ring(4, steps))]
    ppermute x9, waiting for transfers between devices: 13.9 us -> 23.7 us  [move_column(): lax.ppermute(part, 'ctx', ring(4, steps))]
    ppermute x11, waiting for transfers between devices: 14.5 us -> 4.7 us  [swap_y(): return lax.ppermute(value, 'fsdp', flip(4, 2))]
    ppermute x5, waiting for transfers between devices: 5.26 us -> 12.3 us  [swap_zpair(): return lax.ppermute(value, 'ctx', flip(4, 1))]
    unnamed x67 -> x63, local copies, waits for them, and re-layouts: 12.7 us -> 12.7 us
  transfers between devices with their start and end apart: 83 -> 83, of which waited for: 43 -> 42; matrix products, arithmetic and copies ran while one was open for 5% -> 5% of each run, Pallas kernels for 26% -> 26%
where the time goes in v5:
time: 354 us; the launch traced here: 347 us
  Pallas kernels  111 us (31%)
  waiting for transfers between devices  107 us (30%)
  starting transfers between devices  94.2 us (27%)
  local copies, waits for them, and re-layouts  25 us (7%)
  other arithmetic  8 us (2%)
    pallas_call x20, Pallas kernels, vmem_call(): pl.pallas_call(kernel, out_shape=out_shape, in_specs=specs, scratch_shape...  101 us
    ppermute x24, starting transfers between devices, swap_core(): return lax.ppermute(value, 'fsdp', flip(4, 1))  25.3 us
    ppermute x9, waiting for transfers between devices, move_column(): lax.ppermute(part, 'ctx', ring(4, steps))  23.7 us
    ppermute x16, waiting for transfers between devices, swap_x(): return lax.ppermute(value, 'section', flip(2, 1))  23.2 us
    ppermute x16, starting transfers between devices, swap_x(): return lax.ppermute(value, 'section', flip(2, 1))  13.9 us
    ppermute x24, waiting for transfers between devices, swap_core(): return lax.ppermute(value, 'fsdp', flip(4, 1))  12.7 us
    unnamed x63, local copies, waits for them, and re-layouts  12.7 us
    ppermute x5, waiting for transfers between devices, swap_zpair(): return lax.ppermute(value, 'ctx', flip(4, 1))  12.3 us
  transfers between devices with their start and end apart: 83, of which 42 were waited for; matrix products, arithmetic and copies ran while one was open for 5% of the time, Pallas kernels for 26%

profile of v5, /device:TPU:9, one launch (start us, length us, event | category | flops | bytes accessed | tf_op | source)
XLA Modules:
  0.0 347.2 jit_solution(1707694233931134660)
XLA Ops:
  12.0 2.7 collective-permute-start
  26.3 6.6 %collective-permute-done.13 = bf16[4,40,768]{2,1,0:T(8,128)(2,1)S(1)} collective-permute-done((bf16[4,40,768]{2,1,0:T(8,128)(2,1)S(1)}, bf16[4,40,768]{2,1,0:T(8,128)(2,1)S(1)}, u32[]{:S(2)}, u32[]{:S(2)}) %collective-permute-start.13) | collective-permute-done | bytes 245792 | tf_op jit(solution)/shard_map/ppermute | solution.py:70
  34.7 2.6 collective-permute-done.8
  37.4 6.5 %collective-permute-start.9 = (bf16[192,576]{1,0:T(8,128)(2,1)S(1)}, bf16[192,576]{1,0:T(8,128)(2,1)S(1)}, u32[]{:S(2)}, u32[]{:S(2)}) collective-permute-start(bf16[192,576]{1,0:T(8,128)(2,1)S(1)} %get-tuple-element.580), channel_id=1, source_target_pairs={{0,0},{1,8},{2,2},{3,10},{4,4},{5,12},{6,6},{7,14},{8,5},{9,13},{1... | collective-permute-start | bytes 663560 | tf_op jit(solution)/shard_map/ppermute | solution.py:522
  46.8 5.0 %collective-permute-done.9 = bf16[192,576]{1,0:T(8,128)(2,1)S(1)} collective-permute-done((bf16[192,576]{1,0:T(8,128)(2,1)S(1)}, bf16[192,576]{1,0:T(8,128)(2,1)S(1)}, u32[]{:S(2)}, u32[]{:S(2)}) %collective-permute-start.9) | collective-permute-done | bytes 221216 | tf_op jit(solution)/shard_map/ppermute | solution.py:522
  51.8 2.6 collective-permute-done.10
  65.3 4.1 %collective-permute-start.17 = (bf16[384,384]{1,0:T(8,128)(2,1)S(1)}, bf16[384,384]{1,0:T(8,128)(2,1)S(1)}, u32[]{:S(2)}, u32[]{:S(2)}) collective-permute-start(bf16[384,384]{1,0:T(8,128)(2,1)S(1)} %collective-permute-done.15), channel_id=1, source_target_pairs={{0,1},{1,0},{2,3},{3,2},{4,5},{5,4},{6,7},{7,6},{8,9},{9,8},{10,11... | collective-permute-start | bytes 884744 | tf_op jit(solution)/shard_map/ppermute | solution.py:54
  81.2 11.4 %attend.2 = (f32[384,576]{1,0:T(8,128)S(1)}, f32[384,9]{1,0:T(8,128)S(1)}, f32[384,576]{1,0:T(8,128)S(1)}) custom-call(bf16[384,576]{1,0:T(8,128)(2,1)S(1)} %pad_maximum_fusion.3.source_ref, bf16[384,576]{1,0:T(8,128)(2,1)S(1)} %get-tuple-element.283.query_ref, s32[384,1]{1,0:T(8,128)S(1)} %copy.69.position_ref, s32[384,1]{1,0:T(8,128)S(1)} %copy.70.start_ref, ...), custom_call_target="tpu_custom_call" | custom-call | tf_op jit(solution)/shard_map/attend/pallas_call | solution.py:861
  92.6 5.0 %collective-permute-done.19 = bf16[2,160,768]{2,1,0:T(8,128)(2,1)} collective-permute-done((bf16[2,160,768]{2,1,0:T(8,128)(2,1)}, bf16[2,160,768]{2,1,0:T(8,128)(2,1)}, u32[]{:S(2)}, u32[]{:S(2)}) %collective-permute-start.19) | collective-permute-done | bytes 491552 | tf_op jit(solution)/shard_map/ppermute | solution.py:591
  102.7 4.1 %assemble.5 = (bf16[576,1536]{1,0:T(8,128)(2,1)S(1)}, bf16[576,1536]{1,0:T(8,128)(2,1)S(1)}, bf16[1536,576]{1,0:T(8,128)(2,1)S(1)}) custom-call(s32[4]{0:T(128)S(1)} %pad_add_fusion.2.index_ref, bf16[4,120,768]{2,1,0:T(8,128)(2,1)} %constant_dynamic-update-slice_fusion.refs_0_, bf16[4,120,768]{2,1,0:T(8,128)(2,1)} %collective-permute-done.22.refs_1_, ...), custom_call_target="tpu_custom_call" | custom-call | tf_op jit(solution)/shard_map/assemble/pallas_call | solution.py:632
  106.9 4.6 %mlp.2.source_ref = bf16[384,576]{1,0:T(8,128)(2,1)S(1)} custom-call(f32[384,576]{1,0:T(8,128)S(1)} %get-tuple-element.300.middle_ref, bf16[576,1536]{1,0:T(8,128)(2,1)S(1)} %get-tuple-element.319.gate_ref, bf16[576,1536]{1,0:T(8,128)(2,1)S(1)} %get-tuple-element.320.up_ref, bf16[1536,576]{1,0:T(8,128)(2,1)S(1)} %get-tuple-element.321.down_ref, ...), custom_call_target="tpu_custom_call" | custom-call | tf_op jit(solution)/shard_map/mlp/pallas_call | solution.py:861
  121.9 2.6 collective-permute-start.32
  127.8 3.6 %collective-permute-done.32 = bf16[384,384]{1,0:T(8,128)(2,1)S(1)} collective-permute-done((bf16[384,384]{1,0:T(8,128)(2,1)S(1)}, bf16[384,384]{1,0:T(8,128)(2,1)S(1)}, u32[]{:S(2)}, u32[]{:S(2)}) %collective-permute-start.32) | collective-permute-done | bytes 294944 | tf_op jit(solution)/shard_map/ppermute | solution.py:62
  134.1 4.1 %collective-permute-start.39 = (bf16[192,576]{1,0:T(8,128)(2,1)S(1)}, bf16[192,576]{1,0:T(8,128)(2,1)S(1)}, u32[]{:S(2)}, u32[]{:S(2)}) collective-permute-start(bf16[192,576]{1,0:T(8,128)(2,1)S(1)} %get-tuple-element.576), channel_id=1, source_target_pairs={{0,0},{1,8},{2,2},{3,10},{4,4},{5,12},{6,6},{7,14},{8,5},{9,13},{1... | collective-permute-start | bytes 663560 | tf_op jit(solution)/shard_map/ppermute | solution.py:522
  138.3 11.6 %attend.3 = (f32[384,576]{1,0:T(8,128)S(1)}, f32[384,9]{1,0:T(8,128)S(1)}, f32[384,576]{1,0:T(8,128)S(1)}) custom-call(bf16[384,576]{1,0:T(8,128)(2,1)S(1)} %mlp.2.source_ref, bf16[384,576]{1,0:T(8,128)(2,1)S(1)} %get-tuple-element.340.query_ref, s32[384,1]{1,0:T(8,128)S(1)} %copy.69.position_ref, s32[384,1]{1,0:T(8,128)S(1)} %copy.70.start_ref, ...), custom_call_target="tpu_custom_call" | custom-call | tf_op jit(solution)/shard_map/attend/pallas_call | solution.py:861
  159.3 12.3 %mlp_back.2 = (bf16[4,240,768]{2,1,0:T(8,128)(2,1)S(1)}, bf16[4,240,768]{2,1,0:T(8,128)(2,1)S(1)}, bf16[4,240,768]{2,1,0:T(8,128)(2,1)S(1)}, bf16[4,240,768]{2,1...) custom-call(s32[1]{0:T(128)} %bitcast.3.core_ref, ...), custom_call_target="tpu_custom_call" | custom-call | tf_op jit(solution)/shard_map/mlp_back/pallas_call | solution.py:861
  172.3 14.2 %attend_back.2 = (f32[384,576]{1,0:T(8,128)S(1)}, bf16[2,384,384]{2,1,0:T(8,128)(2,1)S(1)}, bf16[2,384,384]{2,1,0:T(8,128)(2,1)S(1)}) custom-call(bf16[384,576]{1,0:T(8,128)(2,1)S(1)} %get-tuple-element.375.d_out_ref, f32[384,576]{1,0:T(8,128)S(1)} %get-tuple-element.342.attended_ref, f32[384,9]{1,0:T(8,128)S(1)} %get-tuple-element.376.log_ref, ...), custom_call_target="tpu_custom_call" | custom-call | tf_op jit(solution)/shard_map/attend_back/pallas_call | solution.py:861
  192.1 4.6 %mlp.3 = bf16[384,576]{1,0:T(8,128)(2,1)S(1)} custom-call(f32[384,576]{1,0:T(8,128)S(1)} %get-tuple-element.398.middle_ref, bf16[576,1536]{1,0:T(8,128)(2,1)S(1)} %get-tuple-element.370.gate_ref, bf16[576,1536]{1,0:T(8,128)(2,1)S(1)} %get-tuple-element.371.up_ref, bf16[1536,576]{1,0:T(8,128)(2,1)S(1)} %get-tuple-element.372.down_ref, ...), custom_call_target="tpu_custom_call" | custom-call | tf_op jit(solution)/shard_map/mlp/pallas_call | solution.py:861
  198.5 3.0 input.2
  201.5 4.6 %collective-permute-done.49.moved_ref = bf16[2,2,240,384]{3,2,1,0:T(8,128)(2,1)S(1)} collective-permute-done((bf16[2,2,240,384]{3,2,1,0:T(8,128)(2,1)S(1)}, bf16[2,2,240,384]{3,2,1,0:T(8,128)(2,1)S(1)}, u32[]{:S(2)}, u32[]{:S(2)}) %collective-permute-start.49) | collective-permute-done | bytes 737312 | tf_op jit(solution)/shard_map/ppermute | solution.py:66
  211.3 4.1 %collective-permute-start.54 = (bf16[192,576]{1,0:T(8,128)(2,1)S(1)}, bf16[192,576]{1,0:T(8,128)(2,1)S(1)}, u32[]{:S(2)}, u32[]{:S(2)}) collective-permute-start(bf16[192,576]{1,0:T(8,128)(2,1)S(1)} %get-tuple-element.572), channel_id=1, source_target_pairs={{0,0},{8,1},{2,2},{10,3},{4,4},{12,5},{6,6},{14,7},{5,8},{13,9},{7... | collective-permute-start | bytes 663560 | tf_op jit(solution)/shard_map/ppermute | solution.py:534
  215.3 12.1 %mlp_back.3 = (bf16[4,240,768]{2,1,0:T(8,128)(2,1)S(1)}, bf16[4,240,768]{2,1,0:T(8,128)(2,1)S(1)}, bf16[4,240,768]{2,1,0:T(8,128)(2,1)S(1)}, bf16[4,240,768]{2,1...) custom-call(s32[1]{0:T(128)} %bitcast.3.core_ref, ...), custom_call_target="tpu_custom_call" | custom-call | tf_op jit(solution)/shard_map/mlp_back/pallas_call | solution.py:861
  228.1 2.8 collective-permute-done.56.refs_4_
  240.7 14.0 %attend_back.3 = (f32[384,576]{1,0:T(8,128)S(1)}, bf16[2,384,384]{2,1,0:T(8,128)(2,1)S(1)}, bf16[2,384,384]{2,1,0:T(8,128)(2,1)S(1)}) custom-call(bf16[384,576]{1,0:T(8,128)(2,1)S(1)} %get-tuple-element.444.d_out_ref, f32[384,576]{1,0:T(8,128)S(1)} %get-tuple-element.288.attended_ref, f32[384,9]{1,0:T(8,128)S(1)} %get-tuple-element.445.log_ref, ...), custom_call_target="tpu_custom_call" | custom-call | tf_op jit(solution)/shard_map/attend_back/pallas_call | solution.py:861
  263.9 7.1 %collective-permute-done.64.refs_2_ = bf16[384,384]{1,0:T(8,128)(2,1)S(1)} collective-permute-done((bf16[384,384]{1,0:T(8,128)(2,1)S(1)}, bf16[384,384]{1,0:T(8,128)(2,1)S(1)}, u32[]{:S(2)}, u32[]{:S(2)}) %collective-permute-start.64) | collective-permute-done | bytes 294944 | tf_op jit(solution)/shard_map/ppermute | solution.py:62
  271.0 2.9 input.3
  279.9 3.3 collective-permute-start.71
  288.7 4.7 %collective-permute-done.71 = bf16[192,576]{1,0:T(8,128)(2,1)S(1)} collective-permute-done((bf16[192,576]{1,0:T(8,128)(2,1)S(1)}, bf16[192,576]{1,0:T(8,128)(2,1)S(1)}, u32[]{:S(2)}, u32[]{:S(2)}) %collective-permute-start.71) | collective-permute-done | bytes 221216 | tf_op jit(solution)/shard_map/ppermute | solution.py:534
  296.3 15.2 %collective-permute-done.77 = bf16[320,384]{1,0:T(8,128)(2,1)S(1)} collective-permute-done((bf16[320,384]{1,0:T(8,128)(2,1)S(1)}, bf16[320,384]{1,0:T(8,128)(2,1)S(1)}, u32[]{:S(2)}, u32[]{:S(2)}) %collective-permute-start.77) | collective-permute-done | bytes 245792 | tf_op jit(solution)/shard_map/ppermute | solution.py:709
  311.4 3.0 collective-permute-done.78
  321.7 3.7 %collective-permute-done.75 = bf16[80,384]{1,0:T(8,128)(2,1)S(1)} collective-permute-done((bf16[80,384]{1,0:T(8,128)(2,1)S(1)}, bf16[80,384]{1,0:T(8,128)(2,1)S(1)}, u32[]{:S(2)}, u32[]{:S(2)}) %collective-permute-start.75) | collective-permute-done | bytes 61472 | tf_op jit(solution)/shard_map/ppermute | solution.py:709
  325.4 6.5 %collective-permute-done.79 = bf16[384,576]{1,0:T(8,128)(2,1)S(1)} collective-permute-done((bf16[384,576]{1,0:T(8,128)(2,1)}, bf16[384,576]{1,0:T(8,128)(2,1)S(1)}, u32[]{:S(2)}, u32[]{:S(2)}) %collective-permute-start.79) | collective-permute-done | bytes 442400 | tf_op jit(solution)/shard_map/ppermute | solution.py:66
  (308 shorter events, 149.8 us)
Async XLA Ops:
  19.2 13.7 %collective-permute-start.13 = (bf16[4,40,768]{2,1,0:T(8,128)(2,1)S(1)}, bf16[4,40,768]{2,1,0:T(8,128)(2,1)S(1)}, u32[]{:S(2)}, u32[]{:S(2)}) collective-permute-start(bf16[4,40,768]{2,1,0:T(8,128)(2,1)S(1)} %pad_maximum_fusion.12), channel_id=1, source_target_pairs={{0,18},{1,19},{2,16},{3,17},{16,2},{17,3},{18,0},{19,1},{4,22},{5,... | collective-permute-start | bytes 737288 | tf_op jit(solution)/shard_map/ppermute | solution.py:70
  21.5 13.2 %collective-permute-start.6 = (bf16[120,768]{1,0:T(8,128)(2,1)S(1)}, bf16[120,768]{1,0:T(8,128)(2,1)S(1)}, u32[]{:S(2)}, u32[]{:S(2)}) collective-permute-start(bf16[120,768]{1,0:T(8,128)(2,1)S(1)} %get-tuple-element.292), channel_id=1, source_target_pairs={{0,4},{4,8},{8,12},{12,0},{1,5},{5,9},{9,13},{13,1},{2,6},{6,10},{... | collective-permute-start | bytes 552968 | tf_op jit(solution)/shard_map/ppermute | solution.py:583
  33.0 21.9 %collective-permute-start.14 = (bf16[4,4,40,768]{3,2,1,0:T(8,128)(2,1)S(1)}, bf16[4,4,40,768]{3,2,1,0:T(8,128)(2,1)S(1)}, u32[]{:S(2)}, u32[]{:S(2)}) collective-permute-start(bf16[4,4,40,768]{3,2,1,0:T(8,128)(2,1)S(1)} %pad_maximum_fusion.refs_0_), channel_id=1, source_target_pairs={{0,1},{1,0},{2,3},{3,2},{4,5},{5,4},{6,7},{7,6},{8,9},{9,8},{10,11... | collective-permute-start | bytes 2949128 | tf_op jit(solution)/shard_map/ppermute | solution.py:54
  37.4 14.4 %collective-permute-start.9 = (bf16[192,576]{1,0:T(8,128)(2,1)S(1)}, bf16[192,576]{1,0:T(8,128)(2,1)S(1)}, u32[]{:S(2)}, u32[]{:S(2)}) collective-permute-start(bf16[192,576]{1,0:T(8,128)(2,1)S(1)} %get-tuple-element.580), channel_id=1, source_target_pairs={{0,0},{1,8},{2,2},{3,10},{4,4},{5,12},{6,6},{7,14},{8,5},{9,13},{1... | collective-permute-start | bytes 663560 | tf_op jit(solution)/shard_map/ppermute | solution.py:522
  58.6 13.6 %collective-permute-start.16 = (bf16[384,384]{1,0:T(8,128)(2,1)S(1)}, bf16[384,384]{1,0:T(8,128)(2,1)S(1)}, u32[]{:S(2)}, u32[]{:S(2)}) collective-permute-start(bf16[384,384]{1,0:T(8,128)(2,1)S(1)} %get-tuple-element.287), channel_id=1, source_target_pairs={{0,1},{1,0},{2,3},{3,2},{4,5},{5,4},{6,7},{7,6},{8,9},{9,8},{10,11... | collective-permute-start | bytes 884744 | tf_op jit(solution)/shard_map/ppermute | solution.py:54
  62.8 29.8 %collective-permute-start.22 = (bf16[4,120,768]{2,1,0:T(8,128)(2,1)}, bf16[4,120,768]{2,1,0:T(8,128)(2,1)}, u32[]{:S(2)}, u32[]{:S(2)}) collective-permute-start(bf16[4,120,768]{2,1,0:T(8,128)(2,1)} %constant_dynamic-update-slice_fusion.refs_0_), channel_id=1, source_target_pairs={{0,16},{16,0},{1,17},{17,1},{2,18},{18,2},{3,19},{19,3},{4,20},{20... | collective-permute-start | bytes 2211848 | tf_op jit(solution)/shard_map/ppermute | solution.py:66
  64.0 28.6 %collective-permute-start.24 = (bf16[4,120,768]{2,1,0:T(8,128)(2,1)}, bf16[4,120,768]{2,1,0:T(8,128)(2,1)}, u32[]{:S(2)}, u32[]{:S(2)}) collective-permute-start(bf16[4,120,768]{2,1,0:T(8,128)(2,1)} %constant_dynamic-update-slice_fusion.refs_0_), channel_id=1, source_target_pairs={{0,1},{1,0},{2,3},{3,2},{4,5},{5,4},{6,7},{7,6},{8,9},{9,8},{10,11... | collective-permute-start | bytes 2211848 | tf_op jit(solution)/shard_map/ppermute | solution.py:54
  70.2 22.3 %collective-permute-start.23 = (bf16[4,120,768]{2,1,0:T(8,128)(2,1)}, bf16[4,120,768]{2,1,0:T(8,128)(2,1)}, u32[]{:S(2)}, u32[]{:S(2)}) collective-permute-start(bf16[4,120,768]{2,1,0:T(8,128)(2,1)} %constant_dynamic-update-slice_fusion.2.refs_2_), channel_id=1, source_target_pairs={{0,2},{1,3},{2,0},{3,1},{4,6},{5,7},{6,4},{7,5},{8,10},{9,11},{10,... | collective-permute-start | bytes 2211848 | tf_op jit(solution)/shard_map/ppermute | solution.py:58
  72.3 20.3 %collective-permute-start.25 = (bf16[4,120,768]{2,1,0:T(8,128)(2,1)}, bf16[4,120,768]{2,1,0:T(8,128)(2,1)}, u32[]{:S(2)}, u32[]{:S(2)}) collective-permute-start(bf16[4,120,768]{2,1,0:T(8,128)(2,1)} %constant_dynamic-update-slice_fusion.2.refs_2_), channel_id=1, source_target_pairs={{0,1},{1,0},{2,3},{3,2},{4,5},{5,4},{6,7},{7,6},{8,9},{9,8},{10,11... | collective-permute-start | bytes 2211848 | tf_op jit(solution)/shard_map/ppermute | solution.py:54
  75.5 22.1 %collective-permute-start.19 = (bf16[2,160,768]{2,1,0:T(8,128)(2,1)}, bf16[2,160,768]{2,1,0:T(8,128)(2,1)}, u32[]{:S(2)}, u32[]{:S(2)}) collective-permute-start(bf16[2,160,768]{2,1,0:T(8,128)(2,1)} %pad_maximum_fusion.4), channel_id=1, source_target_pairs={{0,8},{4,12},{8,0},{12,4},{1,9},{5,13},{9,1},{13,5},{2,10},{6,14},... | collective-permute-start | bytes 1474568 | tf_op jit(solution)/shard_map/ppermute | solution.py:591
  132.5 18.2 %collective-permute-start.37 = (bf16[4,120,768]{2,1,0:T(8,128)(2,1)S(1)}, bf16[4,120,768]{2,1,0:T(8,128)(2,1)S(1)}, u32[]{:S(2)}, u32[]{:S(2)}) collective-permute-start(bf16[4,120,768]{2,1,0:T(8,128)(2,1)S(1)} %constant_dynamic-update-slice_fusion.4.refs_0_), channel_id=1, source_target_pairs={{0,16},{16,0},{1,17},{17,1},{2,18},{18,2},{3,19},{19,3},{4,20},{20... | collective-permute-start | bytes 2211848 | tf_op jit(solution)/shard_map/ppermute | solution.py:66
  132.9 17.9 %collective-permute-start.38 = (bf16[4,120,768]{2,1,0:T(8,128)(2,1)S(1)}, bf16[4,120,768]{2,1,0:T(8,128)(2,1)S(1)}, u32[]{:S(2)}, u32[]{:S(2)}) collective-permute-start(bf16[4,120,768]{2,1,0:T(8,128)(2,1)S(1)} %constant_dynamic-update-slice_fusion.6.refs_2_), channel_id=1, source_target_pairs={{0,2},{1,3},{2,0},{3,1},{4,6},{5,7},{6,4},{7,5},{8,10},{9,11},{10,... | collective-permute-start | bytes 2211848 | tf_op jit(solution)/shard_map/ppermute | solution.py:58
  134.1 15.8 %collective-permute-start.39 = (bf16[192,576]{1,0:T(8,128)(2,1)S(1)}, bf16[192,576]{1,0:T(8,128)(2,1)S(1)}, u32[]{:S(2)}, u32[]{:S(2)}) collective-permute-start(bf16[192,576]{1,0:T(8,128)(2,1)S(1)} %get-tuple-element.576), channel_id=1, source_target_pairs={{0,0},{1,8},{2,2},{3,10},{4,4},{5,12},{6,6},{7,14},{8,5},{9,13},{1... | collective-permute-start | bytes 663560 | tf_op jit(solution)/shard_map/ppermute | solution.py:522
  171.6 14.9 %collective-permute-start.45 = (bf16[4,240,768]{2,1,0:T(8,128)(2,1)S(1)}, bf16[4,240,768]{2,1,0:T(8,128)(2,1)S(1)}, u32[]{:S(2)}, u32[]{:S(2)}) collective-permute-start(bf16[4,240,768]{2,1,0:T(8,128)(2,1)S(1)} %get-tuple-element.382), channel_id=1, source_target_pairs={{0,1},{1,0},{2,3},{3,2},{4,5},{5,4},{6,7},{7,6},{8,9},{9,8},{10,11... | collective-permute-start | bytes 4423688 | tf_op jit(solution)/shard_map/ppermute | solution.py:54
  172.1 14.5 %collective-permute-start.46 = (bf16[4,240,768]{2,1,0:T(8,128)(2,1)S(1)}, bf16[4,240,768]{2,1,0:T(8,128)(2,1)S(1)}, u32[]{:S(2)}, u32[]{:S(2)}) collective-permute-start(bf16[4,240,768]{2,1,0:T(8,128)(2,1)S(1)} %get-tuple-element.383), channel_id=1, source_target_pairs={{0,1},{1,0},{2,3},{3,2},{4,5},{5,4},{6,7},{7,6},{8,9},{9,8},{10,11... | collective-permute-start | bytes 4423688 | tf_op jit(solution)/shard_map/ppermute | solution.py:54
  188.2 18.0 %collective-permute-start.49 = (bf16[2,2,240,384]{3,2,1,0:T(8,128)(2,1)S(1)}, bf16[2,2,240,384]{3,2,1,0:T(8,128)(2,1)S(1)}, u32[]{:S(2)}, u32[]{:S(2)}) collective-permute-start(bf16[2,2,240,384]{3,2,1,0:T(8,128)(2,1)S(1)} %get-tuple-element.393), channel_id=1, source_target_pairs={{0,16},{16,0},{1,17},{17,1},{2,18},{18,2},{3,19},{19,3},{4,20},{20... | collective-permute-start | bytes 2211848 | tf_op jit(solution)/shard_map/ppermute | solution.py:66
  189.4 17.6 %collective-permute-start.50 = (bf16[2,240,768]{2,1,0:T(8,128)(2,1)S(1)}, bf16[2,240,768]{2,1,0:T(8,128)(2,1)S(1)}, u32[]{:S(2)}, u32[]{:S(2)}) collective-permute-start(bf16[2,240,768]{2,1,0:T(8,128)(2,1)S(1)} %get-tuple-element.395), channel_id=1, source_target_pairs={{0,2},{1,3},{2,0},{3,1},{4,6},{5,7},{6,4},{7,5},{8,10},{9,11},{10,... | collective-permute-start | bytes 2211848 | tf_op jit(solution)/shard_map/ppermute | solution.py:58
  207.0 20.5 %collective-permute-start.51 = (bf16[8,80,768]{2,1,0:T(8,128)(2,1)S(1)}, bf16[8,80,768]{2,1,0:T(8,128)(2,1)S(1)}, u32[]{:S(2)}, u32[]{:S(2)}) collective-permute-start(bf16[8,80,768]{2,1,0:T(8,128)(2,1)S(1)} %get-tuple-element.422), channel_id=1, source_target_pairs={{0,1},{1,0},{2,3},{3,2},{4,5},{5,4},{6,7},{7,6},{8,9},{9,8},{10,11... | collective-permute-start | bytes 2949128 | tf_op jit(solution)/shard_map/ppermute | solution.py:54
  209.2 18.4 %collective-permute-start.52 = (bf16[2,240,384]{2,1,0:T(8,128)(2,1)S(1)}, bf16[2,240,384]{2,1,0:T(8,128)(2,1)S(1)}, u32[]{:S(2)}, u32[]{:S(2)}) collective-permute-start(bf16[2,240,384]{2,1,0:T(8,128)(2,1)S(1)} %get-tuple-element.411), channel_id=1, source_target_pairs={{0,2},{1,3},{2,0},{3,1},{4,6},{5,7},{6,4},{7,5},{8,10},{9,11},{10,... | collective-permute-start | bytes 1105928 | tf_op jit(solution)/shard_map/ppermute | solution.py:58
  210.3 17.2 %collective-permute-start.53 = (bf16[2,240,384]{2,1,0:T(8,128)(2,1)S(1)}, bf16[2,240,384]{2,1,0:T(8,128)(2,1)S(1)}, u32[]{:S(2)}, u32[]{:S(2)}) collective-permute-start(bf16[2,240,384]{2,1,0:T(8,128)(2,1)S(1)} %get-tuple-element.412), channel_id=1, source_target_pairs={{0,16},{16,0},{1,17},{17,1},{2,18},{18,2},{3,19},{19,3},{4,20},{20... | collective-permute-start | bytes 1105928 | tf_op jit(solution)/shard_map/ppermute | solution.py:66
  210.6 16.8 %collective-permute-start.55 = (bf16[192,576]{1,0:T(8,128)(2,1)S(1)}, bf16[192,576]{1,0:T(8,128)(2,1)S(1)}, u32[]{:S(2)}, u32[]{:S(2)}) collective-permute-start(bf16[192,576]{1,0:T(8,128)(2,1)S(1)} %get-tuple-element.573), channel_id=1, source_target_pairs={{1,0},{9,1},{3,2},{11,3},{5,4},{13,5},{7,6},{15,7},{4,8},{12,9},{6... | collective-permute-start | bytes 663560 | tf_op jit(solution)/shard_map/ppermute | solution.py:534
  211.3 16.2 %collective-permute-start.54 = (bf16[192,576]{1,0:T(8,128)(2,1)S(1)}, bf16[192,576]{1,0:T(8,128)(2,1)S(1)}, u32[]{:S(2)}, u32[]{:S(2)}) collective-permute-start(bf16[192,576]{1,0:T(8,128)(2,1)S(1)} %get-tuple-element.572), channel_id=1, source_target_pairs={{0,0},{8,1},{2,2},{10,3},{4,4},{12,5},{6,6},{14,7},{5,8},{13,9},{7... | collective-permute-start | bytes 663560 | tf_op jit(solution)/shard_map/ppermute | solution.py:534
  234.5 23.3 %collective-permute-start.58 = (bf16[2,2,320,384]{3,2,1,0:T(8,128)(2,1)S(1)}, bf16[2,2,320,384]{3,2,1,0:T(8,128)(2,1)S(1)}, u32[]{:S(2)}, u32[]{:S(2)}) collective-permute-start(bf16[2,2,320,384]{3,2,1,0:T(8,128)(2,1)S(1)} %get-tuple-element.441), channel_id=1, source_target_pairs={{0,16},{16,0},{1,17},{17,1},{2,18},{18,2},{3,19},{19,3},{4,20},{20... | collective-permute-start | bytes 2949128 | tf_op jit(solution)/shard_map/ppermute | solution.py:66
  235.8 22.9 %collective-permute-start.59 = (bf16[2,320,768]{2,1,0:T(8,128)(2,1)S(1)}, bf16[2,320,768]{2,1,0:T(8,128)(2,1)S(1)}, u32[]{:S(2)}, u32[]{:S(2)}) collective-permute-start(bf16[2,320,768]{2,1,0:T(8,128)(2,1)S(1)} %get-tuple-element.443), channel_id=1, source_target_pairs={{0,2},{1,3},{2,0},{3,1},{4,6},{5,7},{6,4},{7,5},{8,10},{9,11},{10,... | collective-permute-start | bytes 2949128 | tf_op jit(solution)/shard_map/ppermute | solution.py:58
  237.2 17.5 %collective-permute-start.60 = (bf16[240,384]{1,0:T(8,128)(2,1)S(1)}, bf16[240,384]{1,0:T(8,128)(2,1)S(1)}, u32[]{:S(2)}, u32[]{:S(2)}) collective-permute-start(bf16[240,384]{1,0:T(8,128)(2,1)S(1)} %get-tuple-element.430), channel_id=1, source_target_pairs={{0,4},{4,8},{8,12},{12,0},{1,5},{5,9},{9,13},{13,1},{2,6},{6,10},{... | collective-permute-start | bytes 552968 | tf_op jit(solution)/shard_map/ppermute | solution.py:709
  237.9 16.8 %collective-permute-start.61 = (bf16[240,384]{1,0:T(8,128)(2,1)S(1)}, bf16[240,384]{1,0:T(8,128)(2,1)S(1)}, u32[]{:S(2)}, u32[]{:S(2)}) collective-permute-start(bf16[240,384]{1,0:T(8,128)(2,1)S(1)} %get-tuple-element.431), channel_id=1, source_target_pairs={{0,8},{4,12},{8,0},{12,4},{1,9},{5,13},{9,1},{13,5},{2,10},{6,14},... | collective-permute-start | bytes 552968 | tf_op jit(solution)/shard_map/ppermute | solution.py:709
  240.5 15.9 %collective-permute-start.62 = (bf16[240,384]{1,0:T(8,128)(2,1)S(1)}, bf16[240,384]{1,0:T(8,128)(2,1)S(1)}, u32[]{:S(2)}, u32[]{:S(2)}) collective-permute-start(bf16[240,384]{1,0:T(8,128)(2,1)S(1)} %get-tuple-element.432), channel_id=1, source_target_pairs={{0,12},{4,0},{8,4},{12,8},{1,13},{5,1},{9,5},{13,9},{2,14},{6,2},{... | collective-permute-start | bytes 552968 | tf_op jit(solution)/shard_map/ppermute | solution.py:709
  278.3 16.3 %collective-permute-start.68 = (bf16[4,80,384]{2,1,0:T(8,128)(2,1)S(1)}, bf16[4,80,384]{2,1,0:T(8,128)(2,1)S(1)}, u32[]{:S(2)}, u32[]{:S(2)}) collective-permute-start(bf16[4,80,384]{2,1,0:T(8,128)(2,1)S(1)} %get-tuple-element.475), channel_id=1, source_target_pairs={{0,2},{1,3},{2,0},{3,1},{4,6},{5,7},{6,4},{7,5},{8,10},{9,11},{10,... | collective-permute-start | bytes 737288 | tf_op jit(solution)/shard_map/ppermute | solution.py:58
  279.9 13.5 %collective-permute-start.71 = (bf16[192,576]{1,0:T(8,128)(2,1)S(1)}, bf16[192,576]{1,0:T(8,128)(2,1)S(1)}, u32[]{:S(2)}, u32[]{:S(2)}) collective-permute-start(bf16[192,576]{1,0:T(8,128)(2,1)S(1)} %get-tuple-element.570), channel_id=1, source_target_pairs={{0,0},{8,1},{2,2},{10,3},{4,4},{12,5},{6,6},{14,7},{5,8},{13,9},{7... | collective-permute-start | bytes 663560 | tf_op jit(solution)/shard_map/ppermute | solution.py:534
  293.4 18.0 %collective-permute-start.77 = (bf16[320,384]{1,0:T(8,128)(2,1)S(1)}, bf16[320,384]{1,0:T(8,128)(2,1)S(1)}, u32[]{:S(2)}, u32[]{:S(2)}) collective-permute-start(bf16[320,384]{1,0:T(8,128)(2,1)S(1)} %get-tuple-element.494), channel_id=1, source_target_pairs={{0,8},{4,12},{8,0},{12,4},{1,9},{5,13},{9,1},{13,5},{2,10},{6,14},... | collective-permute-start | bytes 737288 | tf_op jit(solution)/shard_map/ppermute | solution.py:709
  294.6 19.9 %collective-permute-start.78 = (bf16[320,384]{1,0:T(8,128)(2,1)S(1)}, bf16[320,384]{1,0:T(8,128)(2,1)S(1)}, u32[]{:S(2)}, u32[]{:S(2)}) collective-permute-start(bf16[320,384]{1,0:T(8,128)(2,1)S(1)} %get-tuple-element.495), channel_id=1, source_target_pairs={{0,12},{4,0},{8,4},{12,8},{1,13},{5,1},{9,5},{13,9},{2,14},{6,2},{... | collective-permute-start | bytes 737288 | tf_op jit(solution)/shard_map/ppermute | solution.py:709
  316.7 15.2 %collective-permute-start.79 = (bf16[384,576]{1,0:T(8,128)(2,1)}, bf16[384,576]{1,0:T(8,128)(2,1)S(1)}, u32[]{:S(2)}, u32[]{:S(2)}) collective-permute-start(bf16[384,576]{1,0:T(8,128)(2,1)} %broadcast_select_fusion.1), channel_id=1, source_target_pairs={{0,16},{16,0},{1,17},{17,1},{2,18},{18,2},{3,19},{19,3},{4,20},{20... | collective-permute-start | bytes 1327112 | tf_op jit(solution)/shard_map/ppermute | solution.py:66
  (75 other events, 605.6 us)
